TPU v7x, 32 devices: a whole 2x2x4 slice. The times are simulated.
32 devices in a mesh: section: 2 (over x), dp: 16 (over z, y, core).
Axes of the slice: x: 2, y: 2, z: 4, core: 2. Of those that a mesh axis runs over, the one named last changes fastest.
Arguments:
- token_ids: int32 [32, 512], P('dp'), may hold values from 0 to 15359
- segment_ids: int32 [32, 512], P('dp'), may hold values from 0 to 3, never falling along the last dimension, each value on 1 to 256 neighbouring positions
- masked_pos: int32 [32, 80], P('dp'), may hold values from 0 to 511, as said below
- word_table: bfloat16 [15360, 768], P('dp'), may hold values from -0.3125 to 0.3125
- position_table: bfloat16 [512, 768], replicated, may hold values from -0.3125 to 0.3125
- embed_gain: float32 [768], replicated, may hold values from 0.5 to 1.5
- embed_bias: float32 [768], replicated, may hold values from -1.25 to 1.25
- query_weight: bfloat16 [2, 4, 192, 192], P('section'), may hold values from -0.4375 to 0.4375
- key_weight: bfloat16 [2, 4, 192, 192], P('section'), may hold values from -0.4375 to 0.4375
- value_weight: bfloat16 [2, 4, 192, 192], P('section'), may hold values from -0.4375 to 0.4375
- output_weight: bfloat16 [2, 768, 768], P('section'), may hold values from -1.75 to 1.75
- attention_gain: float32 [2, 768], P('section'), may hold values from 0.5 to 1.5
- attention_bias: float32 [2, 768], P('section'), may hold values from -1.25 to 1.25
- expand_weight: bfloat16 [2, 4, 192, 768], P('section'), may hold values from -0.4375 to 0.4375
- shrink_weight: bfloat16 [2, 4, 768, 192], P('section'), may hold values from -0.3125 to 0.3125
- feed_gain: float32 [2, 768], P('section'), may hold values from 0.5 to 1.5
- feed_bias: float32 [2, 768], P('section'), may hold values from -1.25 to 1.25
- logit_grad: bfloat16 [32, 80, 15360], P('dp', 'section'), may hold values from -1.25 to 1.25
Outputs:
- logits: bfloat16 [32, 80, 15360], P('dp', 'section')
- word_table_grad: float32 [15360, 768], P('dp')
- position_table_grad: float32 [512, 768], P(None, 'section')
- embed_gain_grad: float32 [768], P('section')
- embed_bias_grad: float32 [768], P('section')
- query_weight_grad: float32 [2, 4, 192, 192], P('section')
- key_weight_grad: float32 [2, 4, 192, 192], P('section')
- value_weight_grad: float32 [2, 4, 192, 192], P('section')
- output_weight_grad: float32 [2, 768, 768], P('section')
- attention_gain_grad: float32 [2, 768], P('section')
- attention_bias_grad: float32 [2, 768], P('section')
- expand_weight_grad: float32 [2, 4, 192, 768], P('section')
- shrink_weight_grad: float32 [2, 4, 768, 192], P('section')
- feed_gain_grad: float32 [2, 768], P('section')
- feed_bias_grad: float32 [2, 768], P('section')
Inputs may be any that keep to these rules, and one draw needn't show every extreme that they name: `masked_pos`: within a row the 80 positions are distinct.
All inputs are finite; a program needn't handle non-finite values.
Results may differ from a plain program's by a relative error of at most 0.02.
Values may be sent and summed in bfloat16 or wider, within the bound.
No kernel may reach another device: no remote copies, remote signals or barrier semaphores. Data moves between devices by JAX's collectives and lax.ppermute only.
A program may use at most 384 MiB of HBM per device.

v0:
```python
import jax
import jax.numpy as jnp
from jax import lax
from jax.sharding import PartitionSpec as P

HEAD = 64
MICRO = 2


norm_eps = 1e-06


def shifted_2(shard, axis, by):
    devices = lax.axis_size(axis)
    pairs = [(i, i + by) for i in range(devices) if 0 <= i + by < devices]
    return lax.ppermute(shard, axis, pairs)


def layer_norm(values, gain_vec, bias_vec):
    centre = jnp.mean(values, axis=-1, keepdims=True)
    shifted = values - centre
    spread = jnp.mean(shifted * shifted, axis=-1, keepdims=True)
    return shifted * lax.rsqrt(spread + norm_eps) * gain_vec + bias_vec


def gelu_exact(values):
    return jax.nn.gelu(values, approximate=False)


def restart(segments):
    counter = lax.broadcasted_iota(jnp.int32, segments.shape, 1)
    begins = jnp.concatenate(
        [jnp.ones(segments[:, :1].shape, dtype=bool), segments[:, 1:] != segments[:, :-1]], axis=1
    )
    return counter - lax.cummax(jnp.where(begins, counter, 0), axis=1)


def grouped(values, weight):
    groups, width_in, width_out = weight.shape
    pieces = values.reshape(values.shape[0], groups, width_in)
    result = jnp.einsum("ngi,gio->ngo", pieces, weight, preferred_element_type=jnp.float32)
    return result.reshape(values.shape[0], groups * width_out)


def grouped_back(gradient, weight):
    groups, width_in, width_out = weight.shape
    pieces = gradient.reshape(gradient.shape[0], groups, width_out)
    result = jnp.einsum("ngo,gio->ngi", pieces, weight, preferred_element_type=jnp.float32)
    return result.reshape(gradient.shape[0], groups * width_in)


def grouped_weight(values, gradient, weight):
    groups, width_in, width_out = weight.shape
    value_parts = values.reshape(values.shape[0], groups, width_in)
    grad_parts = gradient.reshape(gradient.shape[0], groups, width_out)
    return jnp.einsum("ngi,ngo->gio", value_parts, grad_parts, preferred_element_type=jnp.float32)


def attention_scores(query_split, keys_split, same_doc, factor):
    scores = (
        jnp.einsum("bqhd,bkhd->bhqk", query_split, keys_split, preferred_element_type=jnp.float32)
        * factor
    )
    return jnp.where(same_doc[:, None], scores, -1000000000.0)


def layer_forward(layer_input, same_doc, weights, factor):
    (
        query_weight,
        key_weight,
        value_weight,
        output_weight,
        attention_gain,
        attention_bias,
        expand_weight,
        shrink_weight,
        feed_gain,
        feed_bias,
    ) = weights
    count_rows, model_width = layer_input.shape
    split_shape = (same_doc.shape[0], same_doc.shape[1], model_width // HEAD, HEAD)
    input_low = layer_input.astype(jnp.bfloat16)
    query_low = grouped(input_low, query_weight).astype(jnp.bfloat16)
    keys_low = grouped(input_low, key_weight).astype(jnp.bfloat16)
    values_low = grouped(input_low, value_weight).astype(jnp.bfloat16)
    scores = attention_scores(
        query_low.reshape(split_shape), keys_low.reshape(split_shape), same_doc, factor
    )
    log_total = jax.nn.logsumexp(scores, axis=-1, keepdims=True)
    probability_low = jnp.exp(scores - log_total).astype(jnp.bfloat16)
    mixture = jnp.einsum(
        "bhqk,bkhd->bqhd",
        probability_low,
        values_low.reshape(split_shape),
        preferred_element_type=jnp.float32,
    )
    mixture_low = mixture.reshape(count_rows, model_width).astype(jnp.bfloat16)
    attended = jnp.dot(mixture_low, output_weight, preferred_element_type=jnp.float32)
    residual_a = layer_input + attended
    hidden = layer_norm(residual_a, attention_gain, attention_bias)
    hidden_low = hidden.astype(jnp.bfloat16)
    expanded = grouped(hidden_low, expand_weight)
    active_low = gelu_exact(expanded).astype(jnp.bfloat16)
    residual_f = hidden + grouped(active_low, shrink_weight)
    output = layer_norm(residual_f, feed_gain, feed_bias)
    stored = (
        input_low,
        query_low,
        keys_low,
        values_low,
        log_total,
        mixture_low,
        residual_a,
        hidden_low,
        expanded,
        active_low,
        residual_f,
    )
    return (output, stored)


def layer_backward(gradient, same_doc, weights, stored, factor):
    (
        query_weight,
        key_weight,
        value_weight,
        output_weight,
        attention_gain,
        attention_bias,
        expand_weight,
        shrink_weight,
        feed_gain,
        feed_bias,
    ) = weights
    (
        input_low,
        query_low,
        keys_low,
        values_low,
        log_total,
        mixture_low,
        residual_a,
        hidden_low,
        expanded,
        active_low,
        residual_f,
    ) = stored
    count_rows, model_width = input_low.shape
    split_shape = (same_doc.shape[0], same_doc.shape[1], model_width // HEAD, HEAD)
    _, norm_pull = jax.vjp(layer_norm, residual_f, feed_gain, feed_bias)
    feed_back, feed_gain_grad, feed_bias_grad = norm_pull(gradient)
    shrink_in = feed_back.astype(jnp.bfloat16)
    shrink_grad = grouped_weight(active_low, shrink_in, shrink_weight)
    active_back = grouped_back(shrink_in, shrink_weight)
    _, gelu_pull = jax.vjp(gelu_exact, expanded)
    expand_in = gelu_pull(active_back)[0].astype(jnp.bfloat16)
    expand_grad = grouped_weight(hidden_low, expand_in, expand_weight)
    hidden_back = feed_back + grouped_back(expand_in, expand_weight)
    _, norm_pull = jax.vjp(layer_norm, residual_a, attention_gain, attention_bias)
    attn_back, attn_gain_grad, attn_bias_grad = norm_pull(hidden_back)
    attended_in = attn_back.astype(jnp.bfloat16)
    output_grad = lax.dot_general(
        mixture_low, attended_in, (((0,), (0,)), ((), ())), preferred_element_type=jnp.float32
    )
    mixture_back = (
        lax.dot_general(
            attended_in, output_weight, (((1,), (1,)), ((), ())), preferred_element_type=jnp.float32
        )
        .astype(jnp.bfloat16)
        .reshape(split_shape)
    )
    query_split = query_low.reshape(split_shape)
    keys_split = keys_low.reshape(split_shape)
    values_split = values_low.reshape(split_shape)
    scores = attention_scores(query_split, keys_split, same_doc, factor)
    probability = jnp.exp(scores - log_total)
    prob_back = jnp.einsum(
        "bqhd,bkhd->bhqk", mixture_back, values_split, preferred_element_type=jnp.float32
    )
    values_back = jnp.einsum(
        "bhqk,bqhd->bkhd",
        probability.astype(jnp.bfloat16),
        mixture_back,
        preferred_element_type=jnp.float32,
    )
    scores_back = (
        probability * (prob_back - jnp.sum(prob_back * probability, axis=-1, keepdims=True))
    ).astype(jnp.bfloat16)
    query_back = (
        (
            jnp.einsum(
                "bhqk,bkhd->bqhd", scores_back, keys_split, preferred_element_type=jnp.float32
            )
            * factor
        )
        .astype(jnp.bfloat16)
        .reshape(count_rows, model_width)
    )
    keys_back = (
        (
            jnp.einsum(
                "bhqk,bqhd->bkhd", scores_back, query_split, preferred_element_type=jnp.float32
            )
            * factor
        )
        .astype(jnp.bfloat16)
        .reshape(count_rows, model_width)
    )
    values_back = values_back.astype(jnp.bfloat16).reshape(count_rows, model_width)
    query_grad = grouped_weight(input_low, query_back, query_weight)
    key_grad = grouped_weight(input_low, keys_back, key_weight)
    value_grad = grouped_weight(input_low, values_back, value_weight)
    input_back = (
        attn_back
        + grouped_back(query_back, query_weight)
        + grouped_back(keys_back, key_weight)
        + grouped_back(values_back, value_weight)
    )
    return (
        input_back,
        (
            query_grad,
            key_grad,
            value_grad,
            output_grad,
            attn_gain_grad,
            attn_bias_grad,
            expand_grad,
            shrink_grad,
            feed_gain_grad,
            feed_bias_grad,
        ),
    )


def per_device(
    token_ids,
    segment_ids,
    masked_pos,
    word_table,
    position_table,
    embed_gain,
    embed_bias,
    query_weight,
    key_weight,
    value_weight,
    output_weight,
    attention_gain,
    attention_bias,
    expand_weight,
    shrink_weight,
    feed_gain,
    feed_bias,
    logit_grad,
):
    factor = HEAD ** (-0.5)
    leading = lax.axis_index("section") == 0
    weights = tuple(
        (
            array[0]
            for array in (
                query_weight,
                key_weight,
                value_weight,
                output_weight,
                attention_gain,
                attention_bias,
                expand_weight,
                shrink_weight,
                feed_gain,
                feed_bias,
            )
        )
    )
    rows_local, length = token_ids.shape
    batch_rows = rows_local // MICRO
    model_width = word_table.shape[1]
    vocab_table = lax.all_gather(word_table, "dp", axis=0, tiled=True)
    vocab_size = vocab_table.shape[0]
    positions = restart(segment_ids)
    same_all = segment_ids[:, :, None] == segment_ids[:, None, :]

    def rows_of(array, number):
        return array[number * batch_rows : (number + 1) * batch_rows]

    summed_all = []
    for number in range(MICRO):
        looked = vocab_table[rows_of(token_ids, number)].astype(jnp.float32) + position_table[
            rows_of(positions, number)
        ].astype(jnp.float32)
        summed_all.append(looked.reshape(batch_rows * length, model_width))
    arrived = jnp.zeros((batch_rows * length, model_width), jnp.bfloat16)
    stored_all = []
    outputs_all = []
    masks_all = []
    for moment in range(MICRO + 1):
        lead_index = min(moment, MICRO - 1)
        trail_index = max(moment - 1, 0)
        started = layer_norm(summed_all[lead_index], embed_gain, embed_bias)
        layer_input = jnp.where(leading, started, arrived.astype(jnp.float32))
        same_doc = jnp.where(leading, rows_of(same_all, lead_index), rows_of(same_all, trail_index))
        output, stored = layer_forward(layer_input, same_doc, weights, factor)
        stored_all.append(stored)
        outputs_all.append(output)
        masks_all.append(same_doc)
        if moment < MICRO:
            arrived = shifted_2(output.astype(jnp.bfloat16), "section", 1)
    final = jnp.stack(outputs_all[1:])
    halfway = masked_pos.shape[1] // 2
    picked = jnp.take_along_axis(final, masked_pos[:, :, None], axis=1).astype(jnp.bfloat16)
    lent = shifted_2(picked[:, :halfway], "section", -1)
    head_rows = jnp.where(leading, lent, picked[:, halfway:]).reshape(
        rows_local * halfway, model_width
    )
    logits = lax.dot_general(
        head_rows, vocab_table, (((1,), (1,)), ((), ())), preferred_element_type=jnp.float32
    )
    flat_grad = logit_grad.reshape(rows_local * halfway, vocab_size)
    rows_back = jnp.dot(flat_grad, vocab_table, preferred_element_type=jnp.float32).reshape(
        rows_local, halfway, model_width
    )
    table_back = lax.dot_general(
        flat_grad, head_rows, (((0,), (0,)), ((), ())), preferred_element_type=jnp.float32
    )
    returned = shifted_2(rows_back, "section", 1)
    picked_back = jnp.concatenate([returned, rows_back], axis=1)
    row_numbers = lax.broadcasted_iota(jnp.int32, masked_pos.shape, 0)
    final_back = (
        jnp.zeros((rows_local, length, model_width), jnp.float32)
        .at[row_numbers, masked_pos]
        .add(picked_back)
    )
    arrived_back = jnp.zeros((batch_rows * length, model_width), jnp.bfloat16)
    totals = None
    embed_backs = []
    embed_ids = []
    embed_places = []
    gain_back = jnp.zeros(embed_gain.shape, jnp.float32)
    bias_back = jnp.zeros(embed_bias.shape, jnp.float32)
    for moment in range(MICRO + 1):
        lead_index = max(moment - 1, 0)
        trail_index = min(moment, MICRO - 1)
        trail_grad = final_back[trail_index] if moment < MICRO else jnp.zeros_like(final_back[0])
        gradient = jnp.where(leading, arrived_back.astype(jnp.float32), trail_grad)
        stored = jax.tree.map(
            lambda upper_val, lower_val: jnp.where(leading, upper_val, lower_val),
            stored_all[lead_index],
            stored_all[trail_index + 1],
        )
        same_doc = jnp.where(leading, masks_all[lead_index], masks_all[trail_index + 1])
        input_back, layer_grads = layer_backward(gradient, same_doc, weights, stored, factor)
        totals = layer_grads if totals is None else jax.tree.map(jnp.add, totals, layer_grads)
        if moment < MICRO:
            arrived_back = shifted_2(input_back.astype(jnp.bfloat16), "section", -1)
        if moment >= 1:
            start_back = jnp.where(leading, input_back, 0.0)
            _, norm_pull = jax.vjp(layer_norm, summed_all[lead_index], embed_gain, embed_bias)
            summed_back, gain_step, bias_step = norm_pull(start_back)
            embed_backs.append(summed_back)
            embed_ids.append(rows_of(token_ids, lead_index).reshape(-1))
            embed_places.append(rows_of(positions, lead_index).reshape(-1))
            gain_back = gain_back + gain_step
            bias_back = bias_back + bias_step
    every_back = jnp.concatenate(embed_backs, axis=0)
    table_back = table_back.at[jnp.concatenate(embed_ids)].add(every_back)
    position_back = (
        jnp.zeros(position_table.shape, jnp.float32)
        .at[jnp.concatenate(embed_places)]
        .add(every_back)
    )
    (
        query_total,
        key_total,
        value_total,
        output_total,
        attn_gain_total,
        attn_bias_total,
        expand_total,
        shrink_total,
        feed_gain_total,
        feed_bias_total,
    ) = totals
    (
        query_total,
        key_total,
        value_total,
        output_total,
        attn_gain_total,
        attn_bias_total,
        expand_total,
        shrink_total,
        feed_gain_total,
        feed_bias_total,
    ) = lax.psum(
        (
            query_total,
            key_total,
            value_total,
            output_total,
            attn_gain_total,
            attn_bias_total,
            expand_total,
            shrink_total,
            feed_gain_total,
            feed_bias_total,
        ),
        "dp",
    )
    position_rows, gain_rows, bias_rows = lax.psum((position_back, gain_back, bias_back), "dp")
    position_total, gain_part, bias_part = (
        lax.psum_scatter(
            position_rows.astype(jnp.bfloat16), "section", scatter_dimension=1, tiled=True
        ).astype(jnp.float32),
        lax.psum_scatter(
            gain_rows[None].astype(jnp.bfloat16), "section", scatter_dimension=1, tiled=True
        ).astype(jnp.float32),
        lax.psum_scatter(
            bias_rows[None].astype(jnp.bfloat16), "section", scatter_dimension=1, tiled=True
        ).astype(jnp.float32),
    )
    gain_total = gain_part[0]
    bias_total = bias_part[0]
    shard_sum = lax.psum_scatter(table_back, "dp", scatter_dimension=0, tiled=True)
    table_total = lax.psum(shard_sum.astype(jnp.bfloat16), "section").astype(jnp.float32)
    return (
        logits.astype(jnp.bfloat16).reshape(rows_local, halfway, vocab_size),
        table_total,
        position_total,
        gain_total,
        bias_total,
        query_total[None],
        key_total[None],
        value_total[None],
        output_total[None],
        attn_gain_total[None],
        attn_bias_total[None],
        expand_total[None],
        shrink_total[None],
        feed_gain_total[None],
        feed_bias_total[None],
    )


def solution(mesh):
    placed = (
        P("dp", None),
        P("dp", None),
        P("dp", None),
        P("dp", None),
        P(),
        P(),
        P(),
        P("section", None, None, None),
        P("section", None, None, None),
        P("section", None, None, None),
        P("section", None, None),
        P("section", None),
        P("section", None),
        P("section", None, None, None),
        P("section", None, None, None),
        P("section", None),
        P("section", None),
        P("dp", "section", None),
    )
    return jax.shard_map(
        per_device,
        mesh=mesh,
        in_specs=placed,
        out_specs=(
            P("dp", "section", None),
            P("dp", None),
            P(None, "section"),
            P("section"),
            P("section"),
            P("section", None, None, None),
            P("section", None, None, None),
            P("section", None, None, None),
            P("section", None, None),
            P("section", None),
            P("section", None),
            P("section", None, None, None),
            P("section", None, None, None),
            P("section", None),
            P("section", None),
        ),
        check_vma=False,
    )
```

profile of v0, /device:TPU:0, one launch (start us, length us, event | category | flops | bytes accessed | tf_op | source)
XLA Modules:
  0.0 1596.1 jit_solution(12243984626060729128)
XLA Ops:
  26.1 107.5 %all-gather.2.cloned.1.call-done = bf16[15360,768]{1,0:T(8,128)(2,1)} async-done(((bf16[960,768]{1,0:T(8,128)(2,1)}), bf16[15360,768]{1,0:T(8,128)(2,1)}) %all-gather.2.cloned.1.call-update) | async-done | bytes 23592976 | tf_op jit(solution)/shard_map/all_gather | solution.py:278
  133.6 14.3 gather_fusion.2
  176.1 17.4 %fusion.10 = (bf16[512,4,768]{2,0,1:T(8,128)(2,1)S(1)}, f32[4,512,768]{2,1,0:T(8,128)}) fusion(bf16[512,4,192]{0,2,1:T(8,128)(2,1)} %bitcast.974, bf16[1,4,192,768]{3,2,1,0:T(8,128)(2,1)} %param.31), kind=kOutput, calls=%fused_computation.44 | convolution fusion | flops 706215936 | bytes 11403264 | tf_op jit(solution)/shard_map/ngi,gio->ngo/dot_general | solution.py:41
  209.6 10.5 fusion
  222.2 14.2 gather_fusion
  244.8 22.5 %scatter_fusion = f32[2,512,768]{2,1,0:T(8,128)} fusion(f32[2,512,768]{2,1,0:T(8,128)} %broadcast_in_dim.242, s32[160]{0:T(256)S(1)} %reshape.1281, f32[160,768]{1,0:T(8,128)} %bitcast.970), kind=kCustom, calls=%fused_computation.5 | custom fusion | flops 122880 | bytes 1475840 | tf_op jit(solution)/shard_map/scatter-add | solution.py:331
  296.5 17.3 %fusion.13 = (bf16[512,4,768]{2,0,1:T(8,128)(2,1)S(1)}, f32[4,512,768]{2,1,0:T(8,128)}) fusion(bf16[512,4,192]{0,2,1:T(8,128)(2,1)} %bitcast.975, bf16[1,4,192,768]{3,2,1,0:T(8,128)(2,1)} %param.31), kind=kOutput, calls=%fused_computation.47 | convolution fusion | flops 706215936 | bytes 11403264 | tf_op jit(solution)/shard_map/ngi,gio->ngo/dot_general | solution.py:41
  339.7 17.8 %fusion.21 = bf16[512,4,768]{2,0,1:T(8,128)(2,1)S(1)} fusion(f32[4,512,768]{2,1,0:T(8,128)} %get-tuple-element.140, f32[4,512,768]{2,1,0:T(8,128)} %get-tuple-element.146, pred[]{:T(512)S(6)} %eq.16, bf16[512,4,192]{0,2,1:T(8,128)(2,1)} %bitcast.955, bf16[1,4,768,192]{2,3,1,0:T(8,128)(2,1)} %param.32), kind=kOutput, calls=%fused_computation.55 | convolution fusion | flops 718798848 | bytes 17694720 | tf_op jit(solution)/shard_map/ngo,gio->ngi/dot_general | solution.py:48
  411.6 17.2 %fusion.16 = (bf16[512,4,768]{2,0,1:T(8,128)(2,1)S(1)}, f32[4,512,768]{2,1,0:T(8,128)}) fusion(bf16[512,4,192]{0,2,1:T(8,128)(2,1)} %bitcast.976, bf16[1,4,192,768]{3,2,1,0:T(8,128)(2,1)} %param.31), kind=kOutput, calls=%fused_computation.50 | convolution fusion | flops 706215936 | bytes 11403264 | tf_op jit(solution)/shard_map/ngi,gio->ngo/dot_general | solution.py:41
  448.8 13.7 multiply_reduce_fusion.2
  548.0 17.9 %fusion.26 = bf16[512,4,768]{2,0,1:T(8,128)(2,1)S(1)} fusion(f32[4,512,768]{2,1,0:T(8,128)} %get-tuple-element.140, f32[4,512,768]{2,1,0:T(8,128)} %get-tuple-element.152, pred[]{:T(512)S(6)} %eq.16, bf16[512,4,192]{0,2,1:T(8,128)(2,1)} %bitcast.959, bf16[1,4,768,192]{2,3,1,0:T(8,128)(2,1)} %param.32), kind=kOutput, calls=%fused_computation.60 | convolution fusion | flops 718798848 | bytes 17694720 | tf_op jit(solution)/shard_map/ngo,gio->ngi/dot_general | solution.py:48
  582.7 13.7 multiply_reduce_fusion.1
  636.5 18.4 %convolution_bitcast_fusion = f32[15360,768]{0,1:T(8,128)} fusion(bf16[2,40,768]{2,1,0:T(8,128)(2,1)S(1)} %copy-done.129, bf16[2,40,15360]{2,1,0:T(8,128)(2,1)S(1)} %copy-done), kind=kOutput, calls=%fused_computation.8 | convolution fusion | flops 1887436800 | bytes 49766400 | tf_op jit(solution)/shard_map/dot_general | solution.py:322
  654.9 45.8 %copy.207 = f32[15360,768]{1,0:T(8,128)} copy(f32[15360,768]{0,1:T(8,128)} %convolution_bitcast_fusion) | data formatting | bytes 94371840 | tf_op jit(solution)/shard_map/dot_general | solution.py:322
  709.2 17.6 %fusion.31 = bf16[512,4,768]{2,0,1:T(8,128)(2,1)S(1)} fusion(f32[4,512,768]{2,1,0:T(8,128)} %get-tuple-element.146, f32[4,512,768]{2,1,0:T(8,128)} %get-tuple-element.152, pred[]{:T(512)S(6)} %eq.16, bf16[512,4,192]{0,2,1:T(8,128)(2,1)S(1)} %bitcast.957, bf16[1,4,768,192]{2,3,1,0:T(8,128)(2,1)} %param.32), kind=kOutput, calls=%fused_computation.65 | convolution fusion | flops 718798848 | bytes 17694720 | tf_op jit(solution)/shard_map/ngo,gio->ngi/dot_general | solution.py:48
  750.0 9.8 multiply_reduce_fusion
  794.4 38.4 %scatter_custom_fusion.1 = f32[15360,768]{1,0:T(8,128)} fusion(f32[15360,768]{1,0:T(8,128)} %copy.207, s32[1024]{0:T(1024)} %bitcast.987, f32[512,768]{1,0:T(8,128)} %broadcast_add_fusion, f32[512,768]{1,0:T(8,128)} %broadcast_add_fusion.1), kind=kCustom, calls=%fused_computation.545 | custom fusion | flops 1572864 | bytes 50331648 | tf_op jit(solution)/shard_map/scatter-add | solution.py:365
  875.4 10.0 scatter_custom_fusion.2
  885.3 91.1 %all-reduce.10 = (bf16[512,768]{1,0:T(8,128)(2,1)}, bf16[768]{0:T(1024)(128)(2,1)S(1)}, bf16[768]{0:T(1024)(128)(2,1)S(1)}, f32[1,768]{1,0:T(1,128)}, f32[1,768]...) all-reduce(f32[512,768]{1,0:T(8,128)} %scatter_custom_fusion.2, ...), channel_id=1, replica_groups=mesh['section'=2,'dp'=16] {'dp'}, use_global_device_ids=true, to_apply=%region_60.61 | all-reduce | flops 397824 | bytes 2393088 | tf_op jit(solution)/shard_map/psum | solution.py:409
  996.9 290.8 %reduce-scatter.11.cloned.1.call-done = f32[960,768]{1,0:T(8,128)} async-done(((f32[15360,768]{1,0:T(8,128)}), f32[960,768]{1,0:T(8,128)}) %reduce-scatter.11.cloned.1.call-update) | async-done | bytes 2949136 | tf_op jit(solution)/shard_map/reduce_scatter | solution.py:423
  1302.9 12.7 convolution_convert_fusion
  1318.8 14.5 reduce-scatter.13.cloned.1.call-done
  1335.4 50.1 %all-reduce.7.cloned.1.call-done = bf16[960,768]{1,0:T(8,128)(2,1)} async-done(((bf16[960,768]{1,0:T(8,128)(2,1)}), bf16[960,768]{1,0:T(8,128)(2,1)}) %all-reduce.7.cloned.1.call-update) | async-done | bytes 1474576 | tf_op jit(solution)/shard_map/psum | solution.py:424
  1388.7 189.9 %all-reduce.9.cloned.1.call-done = (f32[1,4,192,192]{3,2,1,0:T(8,128)}, f32[1,4,192,192]{3,2,1,0:T(8,128)}, f32[1,4,192,192]{3,2,1,0:T(8,128)}, f32[1,768,768]{2...) async-done(((f32[1,4,192,192]{3,2,1,0:T(8,128)}, f32[1,4,192,192]{3,2,1,0:T(8,128)}, f32[1,4,192,192]{3,2,1,0:T(8,128)}, f32[1,768,768]{2,1,0:T(8,128)}, ...) | async-done | bytes 8847376 | tf_op jit(solution)/shard_map/psum | solution.py:394
  (803 shorter events, 506.0 us)
Async XLA Ops:
  7.2 202.4 %copy-start = (bf16[2,40,15360]{2,1,0:T(8,128)(2,1)S(1)}, bf16[2,40,15360]{2,1,0:T(8,128)(2,1)}, u32[]{:S(2)}) copy-start(bf16[2,40,15360]{2,1,0:T(8,128)(2,1)} %param.35) | copy-start | bytes 7372804
  7.2 126.3 %all-gather.2.cloned.1.call-start = ((), (), s32[]{:S(2)}) async-start(), calls=%async_computation.4 | async-start | bytes 25067520 | tf_op jit(solution)/shard_map/all_gather | solution.py:278
  7.9 1279.8 %reduce-scatter.11.cloned.1.call-start = ((), (), s32[]{:S(2)}) async-start(), calls=%async_computation.5 | async-start | bytes 50135040 | tf_op jit(solution)/shard_map/reduce_scatter | solution.py:423
  14.2 319.1 %copy-start.137 = (f32[768]{0:T(1024)}, f32[768]{0:T(1024)S(1)}, u32[]{:S(2)}) copy-start(f32[768]{0:T(1024)S(1)} %reduce.26) | copy-start | bytes 9220
  26.1 121.7 %copy-start.16 = (bf16[512,768]{1,0:T(8,128)(2,1)S(1)}, bf16[512,768]{1,0:T(8,128)(2,1)}, u32[]{:S(2)}) copy-start(bf16[512,768]{1,0:T(8,128)(2,1)} %gather_fusion.3) | copy-start | bytes 2359300
  165.4 118.4 %copy-start.141 = (f32[12,512]{1,0:T(8,128)}, f32[12,512]{1,0:T(8,128)S(1)}, u32[]{:S(2)}) copy-start(f32[12,512]{1,0:T(8,128)S(1)} %log_add_fusion.2) | copy-start | bytes 73732
  176.1 19.1 %copy-start.91 = (bf16[1,4,768,192]{2,3,1,0:T(8,128)(2,1)S(1)}, bf16[1,4,768,192]{2,3,1,0:T(8,128)(2,1)}, u32[]{:S(2)}) copy-start(bf16[1,4,768,192]{2,3,1,0:T(8,128)(2,1)} %param.32) | copy-start | bytes 3538948
  205.3 62.0 %collective-permute-start = (bf16[512,768]{1,0:T(8,128)(2,1)}, bf16[512,768]{1,0:T(8,128)(2,1)}, u32[]{:S(2)}, u32[]{:S(2)}) collective-permute-start(bf16[512,768]{1,0:T(8,128)(2,1)} %add_convert_fusion.1), channel_id=1, source_target_pairs={{0,16},{1,17},{2,18},{3,19},{4,20},{5,21},{6,22},{7,23},{8,24},{9,... | collective-permute-start | bytes 2359304 | tf_op jit(solution)/shard_map/ppermute | solution.py:16
  220.1 21.0 %collective-permute-start.3 = (f32[2,40,768]{2,1,0:T(8,128)}, f32[2,40,768]{2,1,0:T(8,128)}, u32[]{:S(2)}, u32[]{:S(2)}) collective-permute-start(f32[2,40,768]{2,1,0:T(8,128)} %fusion), channel_id=1, source_target_pairs={{0,16},{1,17},{2,18},{3,19},{4,20},{5,21},{6,22},{7,23},{8,24},{9,... | collective-permute-start | bytes 737288 | tf_op jit(solution)/shard_map/ppermute | solution.py:16
  296.5 18.9 %copy-start.92 = (bf16[1,4,768,192]{2,3,1,0:T(8,128)(2,1)S(1)}, bf16[1,4,768,192]{2,3,1,0:T(8,128)(2,1)}, u32[]{:S(2)}) copy-start(bf16[1,4,768,192]{2,3,1,0:T(8,128)(2,1)} %param.32) | copy-start | bytes 3538948
  339.7 19.5 %copy-start.94 = (bf16[1,4,192,768]{3,2,1,0:T(8,128)(2,1)S(1)}, bf16[1,4,192,768]{3,2,1,0:T(8,128)(2,1)}, u32[]{:S(2)}) copy-start(bf16[1,4,192,768]{3,2,1,0:T(8,128)(2,1)} %param.31) | copy-start | bytes 3538948
  366.4 19.1 %collective-permute-start.1 = (bf16[512,768]{1,0:T(8,128)(2,1)}, bf16[512,768]{1,0:T(8,128)(2,1)S(1)}, u32[]{:S(2)}, u32[]{:S(2)}) collective-permute-start(bf16[512,768]{1,0:T(8,128)(2,1)} %get-tuple-element.128), channel_id=1, source_target_pairs={{0,16},{1,17},{2,18},{3,19},{4,20},{5,21},{6,22},{7,23},{8,24},{9,... | collective-permute-start | bytes 2359304 | tf_op jit(solution)/shard_map/ppermute | solution.py:16
  443.5 65.7 %copy-start.212 = (f32[512]{0:T(512)}, f32[512]{0:T(512)S(1)}, u32[]{:S(2)}) copy-start(f32[512]{0:T(512)S(1)} %negate_multiply_fusion.12) | copy-start | bytes 6148
  513.2 25.4 %collective-permute-start.4 = (bf16[512,768]{1,0:T(8,128)(2,1)}, bf16[512,768]{1,0:T(8,128)(2,1)}, u32[]{:S(2)}, u32[]{:S(2)}) collective-permute-start(bf16[512,768]{1,0:T(8,128)(2,1)} %add_convert_fusion), channel_id=1, source_target_pairs={{16,0},{17,1},{18,2},{19,3},{20,4},{21,5},{22,6},{23,7},{24,8},{25... | collective-permute-start | bytes 2359304 | tf_op jit(solution)/shard_map/ppermute | solution.py:16
  530.5 7.5 collective-permute-start.2
  548.0 19.6 %copy-start.95 = (bf16[1,4,192,768]{3,2,1,0:T(8,128)(2,1)S(1)}, bf16[1,4,192,768]{3,2,1,0:T(8,128)(2,1)}, u32[]{:S(2)}) copy-start(bf16[1,4,192,768]{3,2,1,0:T(8,128)(2,1)} %param.31) | copy-start | bytes 3538948
  577.5 50.6 %copy-start.192 = (f32[512]{0:T(512)}, f32[512]{0:T(512)S(1)}, u32[]{:S(2)}) copy-start(f32[512]{0:T(512)S(1)} %negate_multiply_fusion.10) | copy-start | bytes 6148
  635.2 68.4 %collective-permute-start.5 = (bf16[512,768]{1,0:T(8,128)(2,1)}, bf16[512,768]{1,0:T(8,128)(2,1)S(1)}, u32[]{:S(2)}, u32[]{:S(2)}) collective-permute-start(bf16[512,768]{1,0:T(8,128)(2,1)} %get-tuple-element.99), channel_id=1, source_target_pairs={{16,0},{17,1},{18,2},{19,3},{20,4},{21,5},{22,6},{23,7},{24,8},{25... | collective-permute-start | bytes 2359304 | tf_op jit(solution)/shard_map/ppermute | solution.py:16
  709.2 19.2 %copy-start.96 = (bf16[1,4,192,768]{3,2,1,0:T(8,128)(2,1)S(1)}, bf16[1,4,192,768]{3,2,1,0:T(8,128)(2,1)}, u32[]{:S(2)}) copy-start(bf16[1,4,192,768]{3,2,1,0:T(8,128)(2,1)} %param.31) | copy-start | bytes 3538948
  832.9 482.7 %reduce-scatter.17.cloned.1.call-start = ((), (), s32[]{:S(2)}) async-start(), calls=%async_computation.9 | async-start | bytes 294912
  977.3 339.3 %reduce-scatter.15.cloned.1.call-start = ((), (), s32[]{:S(2)}) async-start(), calls=%async_computation.8 | async-start | bytes 294912
  978.2 355.1 %reduce-scatter.13.cloned.1.call-start = ((), (), s32[]{:S(2)}) async-start(), calls=%async_computation.7 | async-start | bytes 1179648
  983.5 402.0 %all-reduce.7.cloned.1.call-start = ((), (), s32[]{:S(2)}) async-start(), calls=%async_computation.6 | async-start | bytes 2949120 | tf_op jit(solution)/shard_map/psum | solution.py:424
  1290.8 287.7 %all-reduce.9.cloned.1.call-start = ((), (), s32[]{:S(2)}) async-start(), calls=%async_computation.10 | async-start | bytes 18874368 | tf_op jit(solution)/shard_map/psum | solution.py:394
  (239 other events, 1168.1 us)
Sparse Core Ops, SparseCore 0:
  9.6 123.8 all-gather.1
  833.0 454.7 reduce-scatter.10
  1290.0 10.0 reduce-scatter.16
  1302.2 10.9 reduce-scatter.14
  1315.8 17.4 reduce-scatter.12
  1336.1 49.3 all-reduce.6
  1391.7 186.7 all-reduce.8
where the time goes:
time: 1610 us; the launch traced here: 1600 us
  waiting for transfers between devices  662 us (41%)
  matrix products  360 us (22%)
  other arithmetic  234 us (15%)
  local copies, waits for them, and re-layouts  220 us (14%)
  blocking collectives  91.1 us (6%)
  between operations  17.1 us (1%)
    reduce_scatter x1, waiting for transfers between devices, per_device(): lax.psum_scatter(table_back, 'dp', scatter_dimension=0, tiled=True)  291 us
    psum x1, waiting for transfers between devices, per_device(): lax.psum((query_total, key_total, value_total, output_total, attn_gain_to...  190 us
    all_gather x1, waiting for transfers between devices, per_device(): vocab_table = lax.all_gather(word_table, 'dp', axis=0, tiled=True)  107 us
    psum x1, blocking collectives, per_device(): lax.psum((position_back, gain_back, bias_back), 'dp')  91.1 us
    dot_general x15, matrix products, grouped_back(): jnp.einsum('ngo,gio->ngi', pieces, weight, preferred_element_type=jnp.flo...  81.1 us
    dot_general x15, matrix products, grouped(): jnp.einsum('ngi,gio->ngo', pieces, weight, preferred_element_type=jnp.flo...  73.6 us
    psum x1, waiting for transfers between devices, per_device(): lax.psum(shard_sum.astype(jnp.bfloat16), 'section').astype(jnp.float32)  50.1 us
    unnamed x512, local copies, waits for them, and re-layouts  46.8 us
  transfers between devices with their start and end apart: 13, of which 7 were waited for; matrix products, arithmetic and copies ran while one was open for 17% of the time, Pallas kernels for 0%

commit v1 on v0

v1 whole, which is shorter than its diff:
```python
import functools
import jax
import jax.numpy as jnp
from jax import lax
from jax.sharding import PartitionSpec as P
from jax.experimental import pallas as pl
from jax.experimental.pallas import tpu as pltpu

HEAD = 64
norm_eps = 1e-06
BF = jnp.bfloat16
F32 = jnp.float32
LANE = 128
N = 512
D = 768
FF = 3072
GROUPS = 4
WIDE = 192
HEADS = 12
PAIRS = 6
VMEM_LIMIT = 60 * 1024 * 1024
QKV_ROWS = 768
CHUNKS = 16
ROWS_A = 144
ROWS_B = 48
SLAB = 16
GFLOP = 10 ** 9


def mm(a, b):
    return lax.dot_general(a, b, (((1,), (0,)), ((), ())), preferred_element_type=F32)


def mm_nt(a, b):
    return lax.dot_general(a, b, (((1,), (1,)), ((), ())), preferred_element_type=F32)


def mm_tn(a, b):
    return lax.dot_general(a, b, (((0,), (0,)), ((), ())), preferred_element_type=F32)


def window(group):
    return 384 * (group // 2) + 128 * (group % 2)


def lanes(group):
    return slice(window(group), window(group) + 256)


def own_lanes(group):
    counter = lax.broadcasted_iota(jnp.int32, (1, 256), 1)
    return counter < WIDE if group % 2 == 0 else counter >= 64


def fetch_weights(refs, own, other, use_own, core, sems):
    shrink, expand, output, qkv, vecs = refs
    mine, rest = other[0:4], other[4:8]

    def copies(sources, halves):
        made = []
        for number in range(2):
            half = halves[number]
            shrink_src, expand_src, output_src, qkv_src = sources[number]
            for j in range(2 if shrink is not None else 0):
                made.append(pltpu.make_async_copy(shrink_src.at[pl.ds(j * WIDE, WIDE)], shrink.at[2 * half + j, pl.ds(64 * j, WIDE)], sems.at[6 * number + j]))
                made.append(pltpu.make_async_copy(expand_src.at[pl.ds(j * WIDE, WIDE)], expand.at[2 * half + j, pl.ds(64 * j, WIDE)], sems.at[6 * number + 2 + j]))
            if output is not None:
                made.append(pltpu.make_async_copy(output_src, output.at[pl.ds(pl.multiple_of(half * 384, 384), 384)], sems.at[6 * number + 4]))
            if qkv is not None:
                made.append(pltpu.make_async_copy(qkv_src, qkv.at[pl.ds(pl.multiple_of(half * 288, 288), 288)], sems.at[6 * number + 5]))
        return made

    halves_of = [[ref.at[pl.ds(h * (ref.shape[0] // 2), ref.shape[0] // 2)] for ref in own[0:4]] for h in range(2)]
    whole = copies(halves_of, (0, 1))
    parts = copies((mine, rest), (core, 1 - core))
    if vecs is not None:
        whole.append(pltpu.make_async_copy(own[4], vecs, sems.at[12]))
        parts.append(pltpu.make_async_copy(other[8], vecs, sems.at[12]))

    @pl.when(use_own)
    def _():
        for c in whole:
            c.start()

    @pl.when(jnp.logical_not(use_own))
    def _():
        for c in parts:
            c.start()

    for g in range(GROUPS if shrink is not None else 0):
        at = WIDE * (1 - g % 2)
        shrink[g, at : at + 64, :] = jnp.zeros((64, D), BF)
        expand[g, at : at + 64, :] = jnp.zeros((64, D), BF)
    return whole


def pad_qkv(qkv, padded):
    for which in range(3):
        for g in range(GROUPS):
            at = 64 * (g % 2)
            block = qkv[which * WIDE : (which + 1) * WIDE, lanes(g)]
            padded[which, g, at : at + WIDE, :] = jnp.where(own_lanes(g), block, jnp.zeros_like(block))
            gap = WIDE * (1 - g % 2)
            padded[which, g, gap : gap + 64, :] = jnp.zeros((64, 256), BF)


def norm_parts(values):
    centre = jnp.mean(values, axis=-1, keepdims=True)
    shifted = values - centre
    spread = jnp.mean(shifted * shifted, axis=-1, keepdims=True)
    rstd = lax.rsqrt(spread + norm_eps)
    return shifted * rstd, rstd


def norm_back(gradient, hat, rstd, gain):
    scaled = gradient * gain
    first = jnp.mean(scaled, axis=-1, keepdims=True)
    second = jnp.mean(scaled * hat, axis=-1, keepdims=True)
    return rstd * (scaled - first - hat * second)


def join_pair(low, high):
    return jnp.concatenate([low[:, :128], low[:, 128:] + high[:, :128], high[:, 128:]], axis=1)


def layer_fwd(x_ref, bias_ref, w, saves, stats_ref, grow_ref, save_done):
    shrink, expand, output, qkv_pad, vecs = w
    x_low, q_ref, k_ref, v_ref, e_ref, mix_ref, hat_a, hidden_low, active, slope, hat_f, inv_ref, full_ref = saves
    x_low[...] = x_ref[...].astype(BF)
    for which, target in enumerate((q_ref, k_ref, v_ref)):
        for p in range(2):
            low = mm(x_low[:, lanes(2 * p)], qkv_pad[which, 2 * p])
            high = mm(x_low[:, lanes(2 * p + 1)], qkv_pad[which, 2 * p + 1])
            joined = join_pair(low, high).astype(BF)
            if which == 0:
                joined = joined * jnp.asarray(HEAD ** (-0.5), BF)
            target[:, 384 * p : 384 * (p + 1)] = joined
    save_done(0)
    stats_ref[...] = jnp.zeros_like(stats_ref)
    lane = lax.broadcasted_iota(jnp.int32, (1, LANE), 1)

    def pair_body(p, carry):
        at = pl.ds(pl.multiple_of(p * LANE, LANE), LANE)
        qs, ks, vs = q_ref[:, at], k_ref[:, at], v_ref[:, at]
        outs = []
        for side in range(2):
            mine = (lane < HEAD) if side == 0 else (lane >= HEAD)
            scores = mm_nt(jnp.where(mine, qs, jnp.zeros_like(qs)), ks) + bias_ref[...]
            top = jnp.max(scores, axis=-1, keepdims=True)
            e = jnp.exp(scores - top).astype(BF)
            e_ref[2 * p + side] = e
            outs.append(mm(e, jnp.where(mine, vs, jnp.ones_like(vs))))
        inv = 1.0 / pltpu.roll(jnp.where(lane < HEAD, outs[1], outs[0]), HEAD, 1)
        full = jnp.where(lane < HEAD, outs[0], outs[1]) * inv
        inv_ref[:, at] = inv
        full_ref[:, at] = full
        mix_ref[:, at] = full.astype(BF)
        return carry

    lax.fori_loop(0, PAIRS, pair_body, 0)
    save_done(1)
    residual = x_ref[...] + mm(mix_ref[...], output[...])
    hat, rstd = norm_parts(residual)
    hat_a[...] = hat.astype(BF)
    stats_ref[...] = jnp.where(lane == 12, rstd, stats_ref[...])
    hidden = hat * vecs[0:1, :] + vecs[1:2, :]
    hidden_low[...] = hidden.astype(BF)
    grow_ref[...] = hidden
    for g in range(GROUPS):
        wide = slice(g * D, (g + 1) * D)
        expanded = mm(hidden_low[:, lanes(g)], expand[g])
        phi = 0.5 * (1.0 + lax.erf(expanded * (2.0 ** -0.5)))
        density = jnp.exp(expanded * expanded * -0.5) * (2.0 * jnp.pi) ** -0.5
        act = (expanded * phi).astype(BF)
        active[:, wide] = act
        slope[:, wide] = (phi + expanded * density).astype(BF)
        grow_ref[:, lanes(g)] += mm_nt(act, shrink[g])
    save_done(2)
    hat, rstd = norm_parts(grow_ref[...])
    hat_f[...] = hat.astype(BF)
    stats_ref[...] = jnp.where(lane == 13, rstd, stats_ref[...])
    x_ref[...] = hat * vecs[2:3, :] + vecs[3:4, :]
    save_done(3)


SAVE_SHAPES = (
    (N, D), (N, D), (N, D), (N, D), (HEADS, N, N), (N, D), (N, D), (N, D), (N, FF), (N, FF), (N, D),
    (N, D), (N, D), (N, LANE),
)
SAVE_TYPES = (BF,) * 11 + (F32,) * 3
SAVE_STAGES = ((0, 1, 2, 3), (4, 5, 11, 12), (6, 7, 8, 9), (10, 13))
SAVES = 14


def weight_scratch():
    return [
        pltpu.VMEM((GROUPS, 256, D), BF),
        pltpu.VMEM((GROUPS, 256, D), BF),
        pltpu.VMEM((D, D), BF),
        pltpu.VMEM((3 * WIDE, D), BF),
        pltpu.VMEM((8, D), F32),
    ]


def fwd_kernel(flag, slot_rows, dense_rows, slot_col, place_col, seg_col, seg_row, mask_col, place_table, embed_vec, *rest):
    rest = list(rest)

    def take(n):
        got = rest[:n]
        del rest[:n]
        return got

    own, other = take(5), take(9)
    (picked_ref,) = take(1)
    outs = [take(SAVES), take(SAVES)]
    hat_e_ref, stat_e_ref = take(2)
    weights = [take(5), take(5)]
    qkv_pad, bias_ref, x_ref, grow_ref = take(4)
    saves = take(SAVES)
    sem_w, sem_s, sem_d = take(3)
    leading = flag[0] == 0
    waits = [
        fetch_weights(weights[0], own, other, leading, flag[2], sem_w.at[0]),
        fetch_weights(weights[1], own, other, jnp.logical_not(leading), flag[2], sem_w.at[1]),
    ]
    counter = lax.broadcasted_iota(jnp.int32, (N, N), 1)
    one_hot = (place_col[...] == counter).astype(BF)
    slots = slot_rows.shape[0]
    wanted = (slot_col[...] == lax.broadcasted_iota(jnp.int32, (N, slots), 1)).astype(BF)
    x_ref[...] = mm(wanted, slot_rows[...])

    @pl.when(flag[1] != 0)
    def _():
        c = pltpu.make_async_copy(dense_rows, saves[0], sem_d)
        c.start()
        c.wait()
        x_ref[...] = saves[0][...].astype(F32)

    summed = x_ref[...] + mm(one_hot, place_table[...])
    hat, rstd = norm_parts(summed)
    hat_e_ref[...] = hat.astype(BF)
    stat_e_ref[...] = jnp.broadcast_to(rstd, (N, LANE))
    x_ref[...] = hat * embed_vec[0:1, :] + embed_vec[1:2, :]
    bias_ref[...] = jnp.where(seg_col[...] == seg_row[...], 0.0, -1000000000.0)
    drains = []
    for number in range(2):
        for c in waits[number] + drains:
            c.wait()
        drains = []
        shrink, expand, output, qkv, vecs = weights[number]
        pad_qkv(qkv, qkv_pad)

        def save_done(stage, number=number, drains=drains):
            for i in SAVE_STAGES[stage]:
                c = pltpu.make_async_copy(saves[i], outs[number][i], sem_s.at[number, i])
                c.start()
                drains.append(c)

        layer_fwd(
            x_ref, bias_ref, (shrink, expand, output, qkv_pad, vecs),
            saves[:13], saves[13], grow_ref, save_done,
        )
        if number == 0:
            x_ref[...] = x_ref[...].astype(BF).astype(F32)
    picks = (mask_col[...] == lax.broadcasted_iota(jnp.int32, (mask_col.shape[0], N), 1)).astype(BF)
    picked_ref[...] = mm(picks, x_ref[...].astype(BF)).astype(BF)
    for c in drains:
        c.wait()


def save_structs():
    return [jax.ShapeDtypeStruct(s, t) for s, t in zip(SAVE_SHAPES, SAVE_TYPES)]


def save_scratch():
    return [pltpu.VMEM(s, t) for s, t in zip(SAVE_SHAPES, SAVE_TYPES)]


VM = pl.BlockSpec(memory_space=pltpu.VMEM)
HB = pl.BlockSpec(memory_space=pl.ANY)
SM = pl.BlockSpec(memory_space=pltpu.SMEM)


def forward_call(flag, slot_rows, dense_rows, slot_col, place_col, seg_col, seg_row, mask_col, place_table, embed_vec, own, other):
    masks = mask_col.shape[0]
    out = pl.pallas_call(
        fwd_kernel,
        out_shape=[jax.ShapeDtypeStruct((masks, D), BF)] + save_structs() * 2
        + [jax.ShapeDtypeStruct((N, D), BF), jax.ShapeDtypeStruct((N, LANE), F32)],
        in_specs=[SM, VM, HB] + [VM] * 7 + [HB] * 14,
        out_specs=[VM] + [HB] * (2 * SAVES) + [VM] * 2,
        scratch_shapes=weight_scratch() * 2
        + [pltpu.VMEM((3, GROUPS, 256, 256), BF), pltpu.VMEM((N, N), F32), pltpu.VMEM((N, D), F32), pltpu.VMEM((N, D), F32)]
        + save_scratch()
        + [pltpu.SemaphoreType.DMA((2, 13)), pltpu.SemaphoreType.DMA((2, SAVES)), pltpu.SemaphoreType.DMA],
        compiler_params=pltpu.CompilerParams(vmem_limit_bytes=VMEM_LIMIT),
        cost_estimate=pl.CostEstimate(flops=36 * GFLOP, bytes_accessed=60 << 20, transcendentals=0),
        name="forward_layers",
    )(flag, slot_rows, dense_rows, slot_col, place_col, seg_col, seg_row, mask_col, place_table, embed_vec, *own, *other)
    return out[0], out[1 : 1 + SAVES], out[1 + SAVES : 1 + 2 * SAVES], out[-2], out[-1]


def put_chunks(packed_ref, core, source, rows, at):
    for chunk in range(CHUNKS):
        side = core if chunk % 2 == 0 else 1 - core
        packed_ref[side, chunk // 2, at : at + rows, :] = source[chunk * rows : (chunk + 1) * rows, :].astype(BF)


def bwd_a_kernel(last, flag, *rest):
    rest = list(rest)

    def take(n):
        got = rest[:n]
        del rest[:n]
        return got

    if last:
        (go_in,) = take(1)
    else:
        picked_back, mask_row = take(2)
    own, other = take(5), take(9)
    sources = take(7)
    keep_out, away_out, attn_ref, back_low, vec_ref = take(5)
    weights = take(4)
    mid_ref, low_ref, packed_ref = take(3)
    saves = take(7)
    sem_w, sem_s, sem_o, sem_g = take(4)
    mix_ref, hat_a, hidden_low, active, slope, hat_f, stats_ref = saves
    shrink, expand, output, vecs = weights
    leading, core = flag[0] == 0, flag[2]
    use_own = leading if last else jnp.logical_not(leading)
    copies = [pltpu.make_async_copy(sources[i], saves[i], sem_s.at[i]) for i in range(7)]
    wide_copies = []
    for g in range(GROUPS):
        at = pl.ds(g * D, D)
        wide_copies.append([pltpu.make_async_copy(sources[i].at[:, at], saves[i].at[:, at], sem_g.at[i - 3, g]) for i in (3, 4)])
    for i in (5, 6):
        copies[i].start()
    waits = fetch_weights((shrink, expand, output, None, vecs), own, other, use_own, core, sem_w)
    copies[2].start()
    for pair in wide_copies:
        for c in pair:
            c.start()
    for i in (1, 0):
        copies[i].start()
    vec_ref[...] = jnp.zeros_like(vec_ref)
    if last:
        go = go_in[...].astype(F32)
    else:
        masks = mask_row.shape[1]
        spread = (lax.broadcasted_iota(jnp.int32, (N, masks), 0) == mask_row[...]).astype(BF)
        go = mm(spread, picked_back[...])
    lane = lax.broadcasted_iota(jnp.int32, (1, LANE), 1)

    def stat(index):
        return jnp.sum(jnp.where(lane == index, stats_ref[...], 0.0), axis=-1, keepdims=True)

    copies[5].wait()
    copies[6].wait()
    for c in waits:
        c.wait()
    hat = hat_f[...].astype(F32)
    vec_ref[2:3, :] = jnp.sum(go * hat, axis=0, keepdims=True)
    vec_ref[3:4, :] = jnp.sum(go, axis=0, keepdims=True)
    feed_back = norm_back(go, hat, stat(13), vecs[2:3, :])
    mid_ref[...] = feed_back
    low_ref[...] = feed_back.astype(BF)
    copies[2].wait()
    each = WIDE // (CHUNKS // GROUPS)
    for g in range(GROUPS):
        wide = slice(g * D, (g + 1) * D)
        rows = slice(64 * (g % 2), 64 * (g % 2) + WIDE)
        for c in wide_copies[g]:
            c.wait()
        shrink_in = low_ref[:, lanes(g)]
        shrink_grad = mm_tn(shrink_in, active[:, wide])[rows].astype(BF)
        expand_in = (mm(shrink_in, shrink[g]) * slope[:, wide].astype(F32)).astype(BF)
        expand_grad = mm_tn(hidden_low[:, lanes(g)], expand_in)[rows].astype(BF)
        mid_ref[:, lanes(g)] += mm_nt(expand_in, expand[g])
        for part in range(CHUNKS // GROUPS):
            chunk = g * (CHUNKS // GROUPS) + part
            side = core if chunk % 2 == 0 else 1 - core
            packed_ref[side, chunk // 2, 0:each, :] = shrink_grad[part * each : (part + 1) * each, :]
            packed_ref[side, chunk // 2, each : 2 * each, :] = expand_grad[part * each : (part + 1) * each, :]
    copies[1].wait()
    hidden_back = mid_ref[...]
    hat = hat_a[...].astype(F32)
    vec_ref[0:1, :] = jnp.sum(hidden_back * hat, axis=0, keepdims=True)
    vec_ref[1:2, :] = jnp.sum(hidden_back, axis=0, keepdims=True)
    attn_back = norm_back(hidden_back, hat, stat(12), vecs[0:1, :])
    attn_ref[...] = attn_back
    attended_in = attn_back.astype(BF)
    copies[0].wait()
    put_chunks(packed_ref, core, mm_tn(mix_ref[...], attended_in), each, 2 * each)
    ship = [pltpu.make_async_copy(packed_ref.at[1], away_out, sem_o.at[0]), pltpu.make_async_copy(packed_ref.at[0], keep_out, sem_o.at[1])]
    for c in ship:
        c.start()
    back_low[...] = mm_nt(attended_in, output[...]).astype(BF)
    for c in ship:
        c.wait()


def backward_a_call(last, flag, extra, own, other, saved):
    chosen = (5, 6, 7, 8, 9, 10, 13)
    return pl.pallas_call(
        functools.partial(bwd_a_kernel, last),
        out_shape=[
            jax.ShapeDtypeStruct((CHUNKS // 2, ROWS_A, D), BF), jax.ShapeDtypeStruct((CHUNKS // 2, ROWS_A, D), BF),
            jax.ShapeDtypeStruct((N, D), F32), jax.ShapeDtypeStruct((N, D), BF), jax.ShapeDtypeStruct((16, D), F32),
        ],
        in_specs=[SM] + [VM] * len(extra) + [HB] * (14 + len(chosen)),
        out_specs=[HB, HB, VM, VM, VM],
        scratch_shapes=[
            pltpu.VMEM((GROUPS, 256, D), BF), pltpu.VMEM((GROUPS, 256, D), BF), pltpu.VMEM((D, D), BF), pltpu.VMEM((8, D), F32),
            pltpu.VMEM((N, D), F32), pltpu.VMEM((N, D), BF), pltpu.VMEM((2, CHUNKS // 2, ROWS_A, D), BF),
        ]
        + [pltpu.VMEM(SAVE_SHAPES[i], SAVE_TYPES[i]) for i in chosen]
        + [pltpu.SemaphoreType.DMA((13,)), pltpu.SemaphoreType.DMA((len(chosen),)), pltpu.SemaphoreType.DMA((2,)), pltpu.SemaphoreType.DMA((2, GROUPS))],
        compiler_params=pltpu.CompilerParams(vmem_limit_bytes=VMEM_LIMIT),
        cost_estimate=pl.CostEstimate(flops=12 * GFLOP, bytes_accessed=20 << 20, transcendentals=0),
        name="backward_first_a" if last else "backward_second_a",
    )(flag, *extra, *own, *other, *[saved[i] for i in chosen])


def bwd_b_kernel(last, flag, attn_in, back_low, vec_in, *rest):
    rest = list(rest)

    def take(n):
        got = rest[:n]
        del rest[:n]
        return got

    if last:
        slot_row, place_row, hat_e_ref, stat_e_ref, embed_vec = take(5)
    own, other = take(5), take(9)
    sources = take(7)
    keep_out, away_out, back_ref = take(3)
    if last:
        (slot_grad,) = take(1)
    qkv, qkv_pad, go_ref, vec_ref, packed_ref = take(5)
    dq_ref, dk_ref, dv_ref, grad_ref = take(4)
    saves = take(7)
    sem_w, sem_s, sem_o = take(3)
    x_low, q_ref, k_ref, v_ref, e_ref, inv_ref, full_ref = saves
    leading, core = flag[0] == 0, flag[2]
    use_own = leading if last else jnp.logical_not(leading)
    whole = pltpu.make_async_copy(sources[0], saves[0], sem_s.at[0, 0])

    def pair_copies(p):
        at = pl.ds(p * LANE if isinstance(p, int) else pl.multiple_of(p * LANE, LANE), LANE)
        made = [pltpu.make_async_copy(sources[4].at[pl.ds(2 * p, 2)], saves[4].at[pl.ds(2 * p, 2)], sem_s.at[4, p])]
        for i in (1, 2, 3, 5, 6):
            made.append(pltpu.make_async_copy(sources[i].at[:, at], saves[i].at[:, at], sem_s.at[i, p]))
        return made

    for p in range(PAIRS):
        for c in pair_copies(p):
            c.start()
    waits = fetch_weights((None, None, None, qkv, None), own, other, use_own, core, sem_w)
    whole.start()
    lane = lax.broadcasted_iota(jnp.int32, (1, LANE), 1)

    def pair_body(p, carry):
        for c in pair_copies(p):
            c.wait()
        at = pl.ds(pl.multiple_of(p * LANE, LANE), LANE)
        first = lane < HEAD
        d_low = (back_low[:, at].astype(F32) * inv_ref[:, at]).astype(BF)
        weighted = d_low.astype(F32) * full_ref[:, at]
        qs, ks, vs = q_ref[:, at], k_ref[:, at], v_ref[:, at]
        d_v = d_q = d_k = None
        for side in range(2):
            mine = first if side == 0 else jnp.logical_not(first)
            delta = jnp.sum(jnp.where(mine, weighted, 0.0), axis=-1, keepdims=True)
            e = e_ref[2 * p + side]
            d_side = jnp.where(mine, d_low, jnp.zeros_like(d_low))
            prob_back = mm_nt(d_side, vs)
            d_s = (e.astype(F32) * (prob_back - delta)).astype(BF)
            part_v = mm_tn(e, d_side)
            part_q = mm(d_s, jnp.where(mine, ks, jnp.zeros_like(ks)))
            part_k = mm_tn(d_s, jnp.where(mine, qs, jnp.zeros_like(qs)))
            d_v = part_v if d_v is None else d_v + part_v
            d_q = part_q if d_q is None else d_q + part_q
            d_k = part_k if d_k is None else d_k + part_k
        dv_ref[:, at] = d_v.astype(BF)
        dq_ref[:, at] = (d_q * HEAD ** (-0.5)).astype(BF)
        dk_ref[:, at] = d_k.astype(BF)
        return carry

    lax.fori_loop(0, PAIRS, pair_body, 0)
    whole.wait()
    for c in waits:
        c.wait()
    pad_qkv(qkv, qkv_pad)
    go_ref[...] = attn_in[...]
    vec_ref[...] = jnp.zeros_like(vec_ref)
    vec_ref[0:8, :] = vec_in[0:8, :]
    for which, d_ref in enumerate((dq_ref, dk_ref, dv_ref)):
        for p in range(2):
            made = []
            for g in (2 * p, 2 * p + 1):
                rows = slice(64 * (g % 2), 64 * (g % 2) + WIDE)
                d_part = d_ref[:, lanes(g)]
                made.append(jnp.where(own_lanes(g), mm_tn(x_low[:, lanes(g)], d_part)[rows], 0.0))
                go_ref[:, lanes(g)] += mm_nt(d_part, qkv_pad[which, g])
            grad_ref[which * WIDE : (which + 1) * WIDE, 384 * p : 384 * (p + 1)] = join_pair(*made).astype(BF)
    go = go_ref[...]
    if last:
        hat = hat_e_ref[...].astype(F32)
        gain_row = jnp.sum(go * hat, axis=0, keepdims=True)
        bias_row = jnp.sum(go, axis=0, keepdims=True)
        for s in range(2):
            at = slice(s * (D // 2), (s + 1) * (D // 2))
            vec_ref[8 + s : 9 + s, :] = jnp.concatenate([gain_row[:, at], bias_row[:, at]], axis=1)
        back = norm_back(go, hat, stat_e_ref[:, 0:1], embed_vec[0:1, :]).astype(BF)
        back_ref[...] = back
        places = (lax.broadcasted_iota(jnp.int32, (N, N), 0) == place_row[...]).astype(BF)
        grad = mm(places, back).astype(BF)
        for s in range(2):
            block = jnp.concatenate([grad[part * (N // 2) : (part + 1) * (N // 2), s * 384 : (s + 1) * 384] for part in range(2)], axis=1)
            put_chunks(packed_ref, core, block, SLAB, ROWS_B + s * SLAB)
        slots = slot_grad.shape[0]
        slot_grad[...] = mm((lax.broadcasted_iota(jnp.int32, (slots, N), 0) == slot_row[...]).astype(BF), back).astype(BF)
    else:
        back_ref[...] = go.astype(BF)
    grad_ref[3 * WIDE :, :] = vec_ref[...].astype(BF)
    put_chunks(packed_ref, core, grad_ref, ROWS_B, 0)
    ship = [pltpu.make_async_copy(packed_ref.at[1], away_out, sem_o.at[0]), pltpu.make_async_copy(packed_ref.at[0], keep_out, sem_o.at[1])]
    for c in ship:
        c.start()
    for c in ship:
        c.wait()


def backward_b_call(last, flag, extra, own, other, saved, slots=0):
    chosen = (0, 1, 2, 3, 4, 11, 12)
    rows = ROWS_B + 2 * SLAB if last else ROWS_B
    out_shape = [
        jax.ShapeDtypeStruct((CHUNKS // 2, rows, D), BF), jax.ShapeDtypeStruct((CHUNKS // 2, rows, D), BF),
        jax.ShapeDtypeStruct((N, D), BF),
    ]
    if last:
        out_shape.append(jax.ShapeDtypeStruct((slots, D), BF))
    return pl.pallas_call(
        functools.partial(bwd_b_kernel, last),
        out_shape=out_shape,
        in_specs=[SM] + [VM] * len(extra) + [HB] * (14 + len(chosen)),
        out_specs=[HB, HB] + [VM] * (len(out_shape) - 2),
        scratch_shapes=[
            pltpu.VMEM((3 * WIDE, D), BF), pltpu.VMEM((3, GROUPS, 256, 256), BF), pltpu.VMEM((N, D), F32),
            pltpu.VMEM((QKV_ROWS - 3 * WIDE, D), F32), pltpu.VMEM((2, CHUNKS // 2, rows, D), BF),
        ]
        + [pltpu.VMEM((N, D), BF)] * 3 + [pltpu.VMEM((QKV_ROWS, D), BF)]
        + [pltpu.VMEM(SAVE_SHAPES[i], SAVE_TYPES[i]) for i in chosen]
        + [pltpu.SemaphoreType.DMA((13,)), pltpu.SemaphoreType.DMA((len(chosen), PAIRS)), pltpu.SemaphoreType.DMA((2,))],
        compiler_params=pltpu.CompilerParams(vmem_limit_bytes=VMEM_LIMIT),
        cost_estimate=pl.CostEstimate(flops=15 * GFLOP, bytes_accessed=20 << 20, transcendentals=0),
        name="backward_first_b" if last else "backward_second_b",
    )(flag, *extra, *own, *other, *[saved[i] for i in chosen])


def step_y_kernel(side_ref, keep_ref, came_ref, next_keep, next_away):
    side = side_ref[0]
    for j in range(next_keep.shape[0]):
        for target, which in ((next_keep, side), (next_away, 1 - side)):
            at = 2 * j + which
            target[j] = (keep_ref[at].astype(F32) + came_ref[at].astype(F32)).astype(BF)


def step_y(side, keep, came):
    half = jax.ShapeDtypeStruct((keep.shape[0] // 2,) + keep.shape[1:], BF)
    return pl.pallas_call(
        step_y_kernel, out_shape=[half, half], in_specs=[SM, VM, VM], out_specs=[VM, VM],
        compiler_params=pltpu.CompilerParams(vmem_limit_bytes=VMEM_LIMIT),
        cost_estimate=pl.CostEstimate(flops=GFLOP, bytes_accessed=6 << 20, transcendentals=0), name="halve_chunks",
    )(side, keep, came)


def step_z_kernel(me_ref, keep_ref, came_ref, *outs):
    for step in range(4):
        at = me_ref[0] ^ step
        outs[step][...] = (keep_ref[at].astype(F32) + came_ref[at].astype(F32)).astype(BF)


def step_z(me, keep, came):
    one = jax.ShapeDtypeStruct(keep.shape[1:], BF)
    return pl.pallas_call(
        step_z_kernel, out_shape=[one] * 4, in_specs=[SM, VM, VM], out_specs=[VM] * 4,
        compiler_params=pltpu.CompilerParams(vmem_limit_bytes=VMEM_LIMIT),
        cost_estimate=pl.CostEstimate(flops=GFLOP, bytes_accessed=4 << 20, transcendentals=0), name="four_chunks",
    )(me, keep, came)


def finish_kernel(part, flag, place_ref, *refs):
    parts1, parts0 = refs[0:4], refs[4:8]
    mine, theirs = refs[8:10]
    sums = []
    for parts in (parts0, parts1):
        total = parts[0][...].astype(F32)
        for ref in parts[1:]:
            total = total + ref[...].astype(F32)
        sums.append(total)
    first, second = sums
    if part == 1:
        row = lax.broadcasted_iota(jnp.int32, (ROWS_B, 1), 0) + place_ref[0] * ROWS_B
        extra = jnp.where(row >= 3 * WIDE + 8, first[:ROWS_B], 0.0)
        second = jnp.concatenate([second + extra, first[ROWS_B + SLAB :]], axis=0)
        first = first[: ROWS_B + SLAB]
    leading = flag[0] == 0
    mine[...] = jnp.where(leading, first, second).astype(BF)
    theirs[...] = jnp.where(leading, second, first).astype(BF)


def finish_call(part, flag, place, parts1, parts0):
    rows = ROWS_A if part == 0 else ROWS_B + SLAB
    one = jax.ShapeDtypeStruct((rows, D), BF)
    return pl.pallas_call(
        functools.partial(finish_kernel, part), out_shape=[one, one], in_specs=[SM, SM] + [VM] * 8, out_specs=[VM] * 2,
        compiler_params=pltpu.CompilerParams(vmem_limit_bytes=VMEM_LIMIT),
        cost_estimate=pl.CostEstimate(flops=GFLOP, bytes_accessed=2 << 20, transcendentals=0), name="finish_chunks",
    )(flag, place, *parts1, *parts0)


def unpack_kernel(flag, place_ref, a_own, a_came, b_own, b_came, shrink, expand, output, query, key, value, vecs, embed, position, grid, slab):
    each = ROWS_A // 3
    half = CHUNKS // 2
    for core in range(2):
        a_ref, b_ref = (a_own, b_own) if core == 0 else (a_came, b_came)
        for i in range(half):
            device = place_ref[0] ^ (4 * (i % 4) + 2 * (i // 4) + core)
            rows = pl.ds(pl.multiple_of(device * each, each), each)
            block = a_ref[i].astype(F32)
            shrink[rows, :] = block[0:each]
            expand[rows, :] = block[each : 2 * each]
            output[rows, :] = block[2 * each :]
            block = b_ref[i].astype(F32)
            grid[pl.ds(pl.multiple_of(device * ROWS_B, ROWS_B), ROWS_B), :] = block[:ROWS_B]
            slab[pl.ds(pl.multiple_of(device * SLAB, SLAB), SLAB), :] = block[ROWS_B:]
    for which, target in enumerate((query, key, value)):
        for g in range(GROUPS):
            target[g] = grid[which * WIDE : (which + 1) * WIDE, g * WIDE : (g + 1) * WIDE]
    vecs[...] = grid[3 * WIDE : 3 * WIDE + 8, :]
    rows = grid[3 * WIDE + 8 : 3 * WIDE + 16, :]
    embed[...] = jnp.where(flag[0] == 0, rows[0:1], rows[1:2])
    for part in range(2):
        position[part * (N // 2) : (part + 1) * (N // 2), :] = slab[:, part * (D // 2) : (part + 1) * (D // 2)]


def unpack_call(flag, place, a_own, a_came, b_own, b_came):
    square = jax.ShapeDtypeStruct((D, D), F32)
    group = jax.ShapeDtypeStruct((GROUPS, WIDE, WIDE), F32)
    return pl.pallas_call(
        unpack_kernel,
        out_shape=[square] * 3 + [group] * 3
        + [jax.ShapeDtypeStruct((8, D), F32), jax.ShapeDtypeStruct((1, D), F32), jax.ShapeDtypeStruct((N, D // 2), F32)],
        in_specs=[SM, SM] + [VM] * 4,
        out_specs=[VM] * 9,
        scratch_shapes=[pltpu.VMEM((QKV_ROWS, D), F32), pltpu.VMEM((CHUNKS * SLAB, D), F32)],
        compiler_params=pltpu.CompilerParams(vmem_limit_bytes=VMEM_LIMIT),
        cost_estimate=pl.CostEstimate(flops=GFLOP, bytes_accessed=16 << 20, transcendentals=0), name="unpack_sums",
    )(flag, place, a_own, a_came, b_own, b_came)


def plan_kernel(room, id_row, id_col, owner_row, owner_col, slot_col, slot_row, want_ref, most_ref):
    slots = want_ref.shape[1]
    across = lax.broadcasted_iota(jnp.int32, (N, N), 1)
    down = lax.broadcasted_iota(jnp.int32, (N, N), 0)
    same = id_col[...] == id_row[...]
    first_col = jnp.min(jnp.where(same, across, N).astype(F32), axis=1, keepdims=True).astype(jnp.int32)
    first_row = jnp.min(jnp.where(same, down, N).astype(F32), axis=0, keepdims=True).astype(jnp.int32)
    fresh_row = first_row == lax.broadcasted_iota(jnp.int32, (1, N), 1)
    fresh_col = first_col == lax.broadcasted_iota(jnp.int32, (N, 1), 0)
    mates = owner_col[...] == owner_row[...]
    rank_col = jnp.sum(jnp.where(mates & fresh_row & (across < first_col), 1.0, 0.0), axis=1, keepdims=True).astype(jnp.int32)
    rank_row = jnp.sum(jnp.where(mates & fresh_col & (down < first_row), 1.0, 0.0), axis=0, keepdims=True).astype(jnp.int32)
    col = jnp.where(rank_col < room, owner_col[...] * room + rank_col, -1)
    slot_col[...] = col
    slot_row[...] = jnp.where(rank_row < room, owner_row[...] * room + rank_row, -1)
    chosen = (col == lax.broadcasted_iota(jnp.int32, (N, slots), 1)) & fresh_col
    want = jnp.sum(jnp.where(chosen, (id_col[...] + 1).astype(F32), 0.0), axis=0, keepdims=True)
    want_ref[...] = want.astype(jnp.int32) - 1
    most = jnp.max(rank_row.astype(F32), axis=1, keepdims=True).astype(jnp.int32) + 1
    most_ref[...] = jnp.broadcast_to(most, most_ref.shape)


def plan_call(ids, owners, room, slots):
    return pl.pallas_call(
        functools.partial(plan_kernel, room),
        out_shape=[
            jax.ShapeDtypeStruct((N, 1), jnp.int32), jax.ShapeDtypeStruct((1, N), jnp.int32),
            jax.ShapeDtypeStruct((1, slots), jnp.int32), jax.ShapeDtypeStruct((8, LANE), jnp.int32),
        ],
        in_specs=[VM] * 4,
        out_specs=[VM] * 4,
        compiler_params=pltpu.CompilerParams(vmem_limit_bytes=VMEM_LIMIT),
        name="plan_slots",
    )(ids[None], ids[:, None], owners[None], owners[:, None])


def serve_kernel(base_ref, ids_ref, table_ref, out_ref):
    counter = lax.broadcasted_iota(jnp.int32, (ids_ref.shape[0], table_ref.shape[0]), 1) + base_ref[0]
    out_ref[...] = mm((ids_ref[...] == counter).astype(BF), table_ref[...]).astype(BF)


def serve_call(base, ids_col, table):
    return pl.pallas_call(
        serve_kernel,
        out_shape=jax.ShapeDtypeStruct((ids_col.shape[0], D), BF),
        in_specs=[SM, VM, VM],
        out_specs=VM,
        compiler_params=pltpu.CompilerParams(vmem_limit_bytes=VMEM_LIMIT),
        cost_estimate=pl.CostEstimate(flops=3 * GFLOP, bytes_accessed=3 << 20, transcendentals=0),
        name="serve_rows",
    )(base, ids_col, table)


def stream_kernel(grad_ref, head_ref, table_ref, back_ref, logit_ref):
    @pl.when(pl.program_id(0) == 0)
    def _():
        back_ref[...] = jnp.zeros_like(back_ref)

    back_ref[...] += mm(grad_ref[...], table_ref[...])
    logit_ref[...] = mm_nt(head_ref[...], table_ref[...]).astype(BF)


def stream_call(flat_grad, head_rows, table):
    vocab, masks = table.shape[0], flat_grad.shape[0]
    tile = 1024
    return pl.pallas_call(
        stream_kernel,
        grid=(vocab // tile,),
        out_shape=[jax.ShapeDtypeStruct((masks, D), F32), jax.ShapeDtypeStruct((masks, vocab), BF)],
        in_specs=[
            pl.BlockSpec((masks, tile), lambda i: (0, i)),
            pl.BlockSpec((masks, D), lambda i: (0, 0)),
            pl.BlockSpec((tile, D), lambda i: (i, 0)),
        ],
        out_specs=[pl.BlockSpec((masks, D), lambda i: (0, 0)), pl.BlockSpec((masks, tile), lambda i: (0, i))],
        compiler_params=pltpu.CompilerParams(vmem_limit_bytes=VMEM_LIMIT),
        cost_estimate=pl.CostEstimate(flops=10 * GFLOP, bytes_accessed=28 << 20, transcendentals=0),
        name="table_pass",
    )(flat_grad, head_rows, table)


def owner_kernel(base_ref, ids_ref, rows_ref, acc_ref, out_ref):
    counter = lax.broadcasted_iota(jnp.int32, (out_ref.shape[0], ids_ref.shape[1]), 0) + base_ref[0]
    out_ref[...] = (acc_ref[...] + mm((counter == ids_ref[...]).astype(BF), rows_ref[...])).astype(BF)


def owner_call(base, ids_row, rows, total):
    return pl.pallas_call(
        owner_kernel,
        out_shape=jax.ShapeDtypeStruct(total.shape, BF),
        in_specs=[SM, VM, VM, VM],
        out_specs=VM,
        compiler_params=pltpu.CompilerParams(vmem_limit_bytes=VMEM_LIMIT),
        cost_estimate=pl.CostEstimate(flops=3 * GFLOP, bytes_accessed=6 << 20, transcendentals=0),
        name="owner_sum",
    )(base, ids_row, rows, total)


def dense_kernel(base_ref, ids_ref, rows_ref, out_ref):
    @pl.when(pl.program_id(0) == 0)
    def _():
        out_ref[...] = jnp.zeros_like(out_ref)

    counter = lax.broadcasted_iota(jnp.int32, (out_ref.shape[0], N), 0) + base_ref[0]
    out_ref[...] += mm((counter == ids_ref[0]).astype(BF), rows_ref[0])


def dense_call(base, ids, rows, entries):
    return pl.pallas_call(
        dense_kernel,
        grid=(ids.shape[0],),
        out_shape=jax.ShapeDtypeStruct((entries, D), F32),
        in_specs=[SM, pl.BlockSpec((1, 1, N), lambda i: (i, 0, 0)), pl.BlockSpec((1, N, D), lambda i: (i, 0, 0))],
        out_specs=pl.BlockSpec((entries, D), lambda i: (0, 0)),
        compiler_params=pltpu.CompilerParams(vmem_limit_bytes=VMEM_LIMIT),
        name="dense_sum",
    )(base, ids, rows)


def partner(values, axis, bit):
    size = lax.axis_size(axis)
    return lax.ppermute(values, axis, [(i, i ^ bit) for i in range(size)])


def bits_of(axis):
    return [1 << b for b in range(lax.axis_size(axis).bit_length() - 1)]


def exclusive(place, stacked):
    count = stacked.shape[0]
    bit = 1
    while bit < count:
        paired = stacked.reshape((count // (2 * bit), 2, bit) + stacked.shape[1:])
        flipped = jnp.stack([paired[:, 1], paired[:, 0]], axis=1)
        stacked = jnp.where((place & bit) != 0, flipped, paired).reshape(stacked.shape)
        bit *= 2
    return stacked


def packed(weight):
    return jnp.swapaxes(weight, 0, 1).reshape(WIDE, D)


def per_device(
    token_ids,
    segment_ids,
    masked_pos,
    word_table,
    position_table,
    embed_gain,
    embed_bias,
    query_weight,
    key_weight,
    value_weight,
    output_weight,
    attention_gain,
    attention_bias,
    expand_weight,
    shrink_weight,
    feed_gain,
    feed_bias,
    logit_grad,
):
    section = lax.axis_index("section")
    place = lax.axis_index("dp")
    devices = lax.axis_size("dp")
    leading = section == 0
    shard_rows = word_table.shape[0]
    vocab = shard_rows * devices
    masks = masked_pos.shape[1]
    half = masks // 2
    room = max(16, 768 // devices)
    slots = room * devices
    base = (place * shard_rows).astype(jnp.int32).reshape(1)

    def swap(values):
        return lax.ppermute(values, "section", [(0, 1), (1, 0)])

    core = place % 2

    def after(values, *others):
        return lax.optimization_barrier((values, *others))[0]

    def exchange(values):
        return lax.all_to_all(values, "dp", 0, 0, tiled=True)

    ids = jnp.where(leading, token_ids[0], token_ids[1])
    table = lax.all_gather(word_table, "dp", axis=0, tiled=True)
    flat_grad = logit_grad.reshape(masks, vocab)

    def gather_by_exchange(array):
        if devices > 16:
            return lax.all_gather(array, "dp")
        return exchange(jnp.broadcast_to(array[None], (devices,) + array.shape))

    slot_col, slot_row, want, most = plan_call(ids, ids // shard_rows, room, slots)
    told = jnp.concatenate([want.reshape(devices, room), jnp.broadcast_to(most[:1, :16], (devices, 16))], axis=1)
    heard = exchange(told)
    asked = heard[:, :room].reshape(1, slots)
    served = serve_call(base, asked.reshape(slots, 1), word_table)
    slot_rows = exchange(served.reshape(devices, room, D)).reshape(slots, D)
    grad_parts = jnp.swapaxes(flat_grad.reshape(masks, devices, shard_rows), 0, 1)
    slot_rows, grad_parts = lax.optimization_barrier((slot_rows, grad_parts))

    most = after(jnp.max(heard[:, room:]).reshape(1, 1), served)
    most = jnp.maximum(most, swap(most))[0, 0]
    crowded = most > room
    flag = jnp.stack([section.astype(jnp.int32), crowded.astype(jnp.int32), core.astype(jnp.int32)])
    dense_rows = lax.cond(
        crowded,
        lambda: gather_by_exchange(word_table).reshape(vocab, D)[ids],
        lambda: jnp.zeros((N, D), BF),
    )

    vectors = jnp.concatenate([attention_gain, attention_bias, feed_gain, feed_bias, jnp.zeros((4, D), F32)], axis=0)
    own = (
        jnp.swapaxes(shrink_weight[0], 1, 2).reshape(D, D),
        expand_weight[0].reshape(D, D),
        output_weight[0],
        jnp.concatenate([packed(query_weight[0]), packed(key_weight[0]), packed(value_weight[0])], axis=0),
        vectors,
    )
    halves = []
    for array in own[:4]:
        rows = array.shape[0] // 2
        halves.append(swap(lax.dynamic_slice_in_dim(array, core * rows, rows, 0)))
    rest = [partner(array, "dp", 1) for array in halves]
    other = tuple(halves) + tuple(rest) + (swap(own[4]),)

    seg_row = jnp.where(leading, segment_ids[0], segment_ids[1])[None]
    mask_row = jnp.where(leading, masked_pos[0], masked_pos[1])[None]
    earlier = jnp.sum((seg_row < seg_row.T).astype(jnp.int32), axis=1)
    places = lax.iota(jnp.int32, N) - earlier
    embed_vec = jnp.stack([embed_gain, embed_bias])

    def chunked(arrays):
        return jnp.concatenate([array.reshape(devices, -1, D) for array in arrays], axis=1)

    def split_halves(values):
        mine = jnp.where(leading, values[:half], values[half:])
        theirs = jnp.where(leading, values[half:], values[:half])
        return mine, theirs

    def join_halves(mine, theirs):
        return jnp.where(leading, jnp.concatenate([mine, theirs]), jnp.concatenate([theirs, mine]))

    picked, saved0, saved1, hat_e, stat_e = forward_call(
        flag, slot_rows, dense_rows, slot_col, places[:, None], seg_row.T, seg_row, mask_row.T, position_table, embed_vec, own, other
    )
    mine, theirs = split_halves(picked)
    head_rows = join_halves(mine, swap(theirs))
    small = devices <= 16
    heads = [partner(head_rows, "dp", 4 * step) for step in (1, 2, 3)] if small else [lax.all_gather(head_rows, "dp", axis=0)]
    rows_back, logits = stream_call(flat_grad, head_rows, table)
    logits = logits.reshape(2, half, vocab)
    rows_back, heads = lax.optimization_barrier((rows_back, heads))
    if small:
        heads = jnp.stack([head_rows] + heads)
        heads = [heads, partner(heads, "dp", 2)]
    grad_parts = after(grad_parts, rows_back)
    grad_rows = exchange(grad_parts).reshape(devices * masks, shard_rows)
    mine, theirs = split_halves(rows_back)
    picked_back = join_halves(mine, swap(theirs)).astype(BF)

    def spread_on(array):
        if devices <= 16:
            return array
        groups = [list(range(low, devices, 16)) for low in range(16)]
        return lax.psum(array.astype(F32), "dp", axis_index_groups=groups).astype(BF)

    low_place = (place % 16).astype(jnp.int32).reshape(1)
    side_y = ((place // 2) % 2).astype(jnp.int32).reshape(1)
    me_z = ((place // 4) % 4).astype(jnp.int32).reshape(1)

    def across_z(parts):
        return [spread_on(parts[0])] + [partner(spread_on(parts[step]), "dp", 4 * step) for step in (1, 2, 3)]

    keep_a1, away_a1, attn1, low1, vec1 = backward_a_call(False, flag, [picked_back, mask_row], own, other, saved1)
    came = partner(away_a1, "dp", 1)
    keep_b1, away_b1, middle = backward_b_call(False, flag, [attn1, low1, vec1], own, other, saved1)
    middle, came, heads = lax.optimization_barrier((middle, came, heads))
    if small:
        heads = jnp.concatenate(heads)
        heads = [heads, partner(heads, "dp", 1)]
    keep_a1, away_a1 = step_y(side_y, keep_a1, came)
    middle, away_a1 = lax.optimization_barrier((middle, away_a1))
    came_a = partner(away_a1, "dp", 2)
    came_b = partner(away_b1, "dp", 1)
    keep_a0, away_a0, attn0, low0, vec0 = backward_a_call(True, flag, [middle], own, other, saved0)
    attn0, came_a, came_b, grad_rows = lax.optimization_barrier((attn0, came_a, came_b, grad_rows))
    parts_a1 = across_z(step_z(me_z, keep_a1, came_a))
    keep_b1, away_b1 = step_y(side_y, keep_b1, came_b)
    came_b = partner(away_b1, "dp", 2)
    came_a = partner(away_a0, "dp", 1)
    keep_b0, away_b0, back, slot_grad = backward_b_call(
        True, flag, [attn0, low0, vec0, slot_row, places[None], hat_e, stat_e, embed_vec], own, other, saved0, slots
    )
    slot_grad, away_b0, parts_a1, came_a, came_b = lax.optimization_barrier((slot_grad, away_b0, parts_a1, came_a, came_b))
    keep_a0, away_a0 = step_y(side_y, keep_a0, came_a)
    away_a0, slot_grad, away_b0, keep_b1, parts_a1, heads = lax.optimization_barrier(
        (away_a0, slot_grad, away_b0, keep_b1, parts_a1, heads)
    )
    came_a = partner(away_a0, "dp", 2)
    if small:
        heads = jnp.concatenate(heads)
        every_head = exclusive(place, jnp.stack([heads[c * 8 + b * 4 + z] for z in range(4) for b in range(2) for c in range(2)]))
    else:
        every_head = heads[0]
    every_head = every_head.reshape(devices * masks, D)
    table_back = lax.dot_general(grad_rows, every_head, (((0,), (0,)), ((), ())), preferred_element_type=F32)

    sent = exchange(slot_grad.reshape(devices, room, D)).reshape(slots, D)
    crowd_sum = lax.cond(
        crowded,
        lambda: dense_call(base, gather_by_exchange(ids[None]), gather_by_exchange(back), shard_rows),
        lambda: jnp.zeros((shard_rows, D), F32),
    )
    names = jnp.where(crowded, -1, asked)
    partial = owner_call(base, names, sent, table_back + crowd_sum)
    parts_b1 = across_z(step_z(me_z, keep_b1, came_b))
    came_b = partner(away_b0, "dp", 1)
    parts_a0 = across_z(step_z(me_z, keep_a0, came_a))
    partial, parts_a0 = lax.optimization_barrier((partial, parts_a0))
    keep_b0, away_b0 = step_y(side_y, keep_b0, came_b)
    came_b = partner(away_b0, "dp", 2)
    parts_b0 = across_z(step_z(me_z, keep_b0, came_b))

    def to_all(mine, theirs):
        chunk = (mine.astype(F32) + theirs.astype(F32)).astype(BF)
        held = jnp.stack([chunk] + [partner(chunk, "dp", 4 * step) for step in (1, 2, 3)])
        held = jnp.concatenate([held, partner(held, "dp", 2)])
        return held, partner(held, "dp", 1)

    mine_a, theirs_a = finish_call(0, flag, low_place, parts_a1, parts_a0)
    theirs_a = swap(theirs_a)
    mine_b, theirs_b = finish_call(1, flag, low_place, parts_b1, parts_b0)
    theirs_b = swap(theirs_b)
    partial, theirs_b = lax.optimization_barrier((partial, theirs_b))
    table_total = partial.astype(F32) + swap(partial).astype(F32)
    shrink_total, expand_total, output_total, query_total, key_total, value_total, vec_total, embed_total, position_total = unpack_call(
        flag, low_place, *to_all(mine_a, theirs_a), *to_all(mine_b, theirs_b)
    )
    embed_total = embed_total.reshape(2, D // 2)
    return (
        logits,
        table_total,
        position_total,
        embed_total[0],
        embed_total[1],
        query_total[None],
        key_total[None],
        value_total[None],
        output_total[None],
        vec_total[0:1],
        vec_total[1:2],
        expand_total.reshape(1, GROUPS, WIDE, D),
        jnp.swapaxes(shrink_total.reshape(1, GROUPS, WIDE, D), 2, 3),
        vec_total[2:3],
        vec_total[3:4],
    )


def solution(mesh):
    placed = (
        P("dp", None),
        P("dp", None),
        P("dp", None),
        P("dp", None),
        P(),
        P(),
        P(),
        P("section", None, None, None),
        P("section", None, None, None),
        P("section", None, None, None),
        P("section", None, None),
        P("section", None),
        P("section", None),
        P("section", None, None, None),
        P("section", None, None, None),
        P("section", None),
        P("section", None),
        P("dp", "section", None),
    )
    return jax.shard_map(
        per_device,
        mesh=mesh,
        in_specs=placed,
        out_specs=(
            P("dp", "section", None),
            P("dp", None),
            P(None, "section"),
            P("section"),
            P("section"),
            P("section", None, None, None),
            P("section", None, None, None),
            P("section", None, None, None),
            P("section", None, None),
            P("section", None),
            P("section", None),
            P("section", None, None, None),
            P("section", None, None, None),
            P("section", None),
            P("section", None),
        ),
        check_vma=False,
    )
```

time: 1610 us -> 494 us (0.31)
  waiting for transfers between devices: 662 us -> 143 us
  matrix products: 360 us -> 2.2 us
  other arithmetic: 234 us -> 18.8 us
  local copies, waits for them, and re-layouts: 220 us -> 44.7 us
  Pallas kernels: 0 us -> 171 us
  blocking collectives: 91.1 us -> 0 us
  starting transfers between devices: 12.7 us -> 89.9 us
    dot_general x78 -> x1, matrix products: 360 us -> 2.2 us  [per_device(): lax.dot_general(grad_rows, every_head, (((0,), (0,)), ((), ())), preferre...]
    reduce_scatter x1 -> x0, waiting for transfers between devices: 291 us -> none  [per_device(): lax.psum_scatter(table_back, 'dp', scatter_dimension=0, tiled=True)]
    psum x2 -> x0, waiting for transfers between devices: 240 us -> none  [the longest x1 190 us: per_device(): lax.psum((query_total, key_total, value_total, output_total, attn_gain_to...]
    pallas_call x0 -> x20, Pallas kernels: none -> 171 us  [the longest x2 37.7 us: backward_b_call(): pl.pallas_call(functools.partial(bwd_b_kernel, last), out_shape=out_shape...]
    ppermute x6 -> x50, waiting for transfers between devices: 8.59 us -> 128 us  [the longest x39 80 us: partner(): return lax.ppermute(values, axis, [(i, i ^ bit) for i in range(size)])]
    all_gather x1, waiting for transfers between devices: 107 us -> 7.11 us  [per_device(): table = lax.all_gather(word_table, 'dp', axis=0, tiled=True)]
    psum x1 -> x0, blocking collectives: 91.1 us -> none  [per_device(): lax.psum((position_back, gain_back, bias_back), 'dp')]
    reduce_sum x39 -> x1, other arithmetic: 83.3 us -> 0.25 us  [per_device(): earlier = jnp.sum((seg_row < seg_row.T).astype(jnp.int32), axis=1)]
  transfers between devices with their start and end apart: 13 -> 55, of which waited for: 7 -> 18; matrix products, arithmetic and copies ran while one was open for 17% -> 12% of each run, Pallas kernels for 0% -> 34%
where the time goes in v1:
time: 494 us; the launch traced here: 486 us
  Pallas kernels  171 us (35%)
  waiting for transfers between devices  143 us (29%)
  starting transfers between devices  89.9 us (18%)
  local copies, waits for them, and re-layouts  44.7 us (9%)
  other arithmetic  18.8 us (4%)
  between operations  16.5 us (3%)
    ppermute x39, waiting for transfers between devices, partner(): return lax.ppermute(values, axis, [(i, i ^ bit) for i in range(size)])  80 us
    ppermute x11, waiting for transfers between devices, swap(): return lax.ppermute(values, 'section', [(0, 1), (1, 0)])  48.3 us
    ppermute x39, starting transfers between devices, partner(): return lax.ppermute(values, axis, [(i, i ^ bit) for i in range(size)])  43.4 us
    pallas_call x2, Pallas kernels, backward_b_call(): pl.pallas_call(functools.partial(bwd_b_kernel, last), out_shape=out_shape...  37.7 us
    pallas_call x1, Pallas kernels, forward_call(): pl.pallas_call(fwd_kernel, out_shape=[jax.ShapeDtypeStruct((masks, D), BF...  37.6 us
    all_to_all x4, starting transfers between devices, exchange(): return lax.all_to_all(values, 'dp', 0, 0, tiled=True)  32.8 us
    pallas_call x2, Pallas kernels, backward_a_call(): pl.pallas_call(functools.partial(bwd_a_kernel, last), out_shape=[jax.Shap...  31.1 us
    unnamed x108, local copies, waits for them, and re-layouts  20.4 us
  transfers between devices with their start and end apart: 55, of which 18 were waited for; matrix products, arithmetic and copies ran while one was open for 12% of the time, Pallas kernels for 34%

profile of v1, /device:TPU:0, one launch (start us, length us, event | category | flops | bytes accessed | tf_op | source)
XLA Modules:
  0.0 485.9 jit_solution(4811683829926618946)
XLA Ops:
  15.6 7.4 %all-to-all-start.3 = ((s32[16,1,64]{2,1,0:T(1,128)}), s32[16,1,64]{2,1,0:T(1,128)S(1)}, u32[]{:S(2)}, u32[]{:S(2)}) async-start(s32[16,1,64]{2,1,0:T(1,128)} %bitcast.5), calls=%async_computation.3 | async-start | bytes 16384 | tf_op jit(solution)/shard_map/all_to_all | solution.py:848
  23.0 6.4 %all-to-all-done.3 = s32[16,1,64]{2,1,0:T(1,128)S(1)} async-done(((s32[16,1,64]{2,1,0:T(1,128)}), s32[16,1,64]{2,1,0:T(1,128)S(1)}, u32[]{:S(2)}, u32[]{:S(2)}) %all-to-all-start.3) | async-done | bytes 4128 | tf_op jit(solution)/shard_map/all_to_all | solution.py:848
  39.7 4.7 all-to-all-start.4
  56.6 7.0 %collective-permute-done.3.rest_7_.rest_9_.rest_8_.rest_12_ = bf16[384,768]{1,0:T(8,128)(2,1)} collective-permute-done((bf16[384,768]{1,0:T(8,128)(2,1)}, bf16[384,768]{1,0:T(8,128)(2,1)}, u32[]{:S(2)}, u32[]{:S(2)}) %collective-permute-start.3) | collective-permute-done | bytes 589856 | tf_op jit(solution)/shard_map/ppermute | solution.py:840
  63.5 12.6 %collective-permute-done.1.rest_5_.rest_7_.rest_6_.rest_10_ = bf16[384,768]{1,0:T(8,128)(2,1)} collective-permute-done((bf16[384,768]{1,0:T(8,128)(2,1)S(1)}, bf16[384,768]{1,0:T(8,128)(2,1)}, u32[]{:S(2)}, u32[]{:S(2)}) %collective-permute-start.1) | collective-permute-done | bytes 589856 | tf_op jit(solution)/shard_map/ppermute | solution.py:840
  76.2 12.6 %collective-permute-done.2.rest_6_.rest_8_.rest_7_.rest_11_ = bf16[384,768]{1,0:T(8,128)(2,1)} collective-permute-done((bf16[384,768]{1,0:T(8,128)(2,1)S(1)}, bf16[384,768]{1,0:T(8,128)(2,1)}, u32[]{:S(2)}, u32[]{:S(2)}) %collective-permute-start.2) | collective-permute-done | bytes 589856 | tf_op jit(solution)/shard_map/ppermute | solution.py:840
  101.6 37.6 %forward_layers.1 = (bf16[80,768]{1,0:T(8,128)(2,1)}, bf16[512,768]{1,0:T(8,128)(2,1)}, bf16[512,768]{1,0:T(8,128)(2,1)}, bf16[512,768]{1,0:T(8,128)(2,1)}, bf16...) custom-call(s32[3]{0:T(128)} %pad_add_fusion.1.flag, ...), custom_call_target="tpu_custom_call" | custom-call | flops 35999997952 | bytes 62914560 | tf_op jit(solution)/shard_map/forward_layers/pallas_call | solution.py:286
  148.9 7.1 %all-gather.2.cloned.1.call-done.table_ref = bf16[15360,768]{1,0:T(8,128)(2,1)} async-done(((bf16[960,768]{1,0:T(8,128)(2,1)}), bf16[15360,768]{1,0:T(8,128)(2,1)}) %all-gather.2.cloned.1.call-update) | async-done | bytes 23592976 | tf_op jit(solution)/shard_map/all_gather | solution.py:851
  156.0 20.2 %table_pass.1 = (f32[80,768]{1,0:T(8,128)}, bf16[80,15360]{1,0:T(8,128)(2,1)}) custom-call(bf16[80,15360]{1,0:T(8,128)(2,1)} %bitcast.123, bf16[80,768]{1,0:T(8,128)(2,1)} %copy-done.18, bf16[15360,768]{1,0:T(8,128)(2,1)} %all-gather.2.cloned.1.call-done.table_ref), custom_call_target="tpu_custom_call" | custom-call | flops 10000000000 | bytes 29360128 | tf_op jit(solution)/shard_map/table_pass/pallas_call | solution.py:729
  180.6 16.1 %all-to-all-start.5 = ((bf16[16,80,960]{2,1,0:T(8,128)(2,1)}), bf16[16,80,960]{2,1,0:T(8,128)(2,1)S(1)}, u32[]{:S(2)}, u32[]{:S(2)}) async-start(bf16[16,80,960]{2,1,0:T(8,128)(2,1)} %bitcast.109), calls=%async_computation.5 | async-start | bytes 5242880 | tf_op jit(solution)/shard_map/all_to_all | solution.py:848
  197.4 15.5 %backward_second_a.1 = (bf16[8,144,768]{2,1,0:T(8,128)(2,1)}, bf16[8,144,768]{2,1,0:T(8,128)(2,1)}, f32[512,768]{1,0:T(8,128)}, bf16[512,768]{1,0:T(8,128)(2,1)}, f32[16,768]{1,0:T(8,128)}) custom-call(s32[3]{0:T(128)} %pad_add_fusion.1.flag, bf16[80,768]{1,0:T(8,128)(2,1)} %fusion.4.rest_0_, s32[1,80]{1,0:T(1,128)} %broadcast_select_fusion.6.rest_1_, ...), custom_call_target="tpu_custom_call" | custom-call | flops 12000000000 | bytes 20971520 | tf_op jit(solution)/shard_map/backward_second_a/pallas_call | solution.py:405
  216.2 17.6 %backward_second_b.1 = (bf16[8,48,768]{2,1,0:T(8,128)(2,1)}, bf16[8,48,768]{2,1,0:T(8,128)(2,1)}, bf16[512,768]{1,0:T(8,128)(2,1)}) custom-call(s32[3]{0:T(128)} %pad_add_fusion.1.flag, f32[512,768]{1,0:T(8,128)} %get-tuple-element.186.attn_in, bf16[512,768]{1,0:T(8,128)(2,1)} %get-tuple-element.187.back_low, f32[16,768]{1,0:T(8,128)} %get-tuple-element.188.vec_in, ...), custom_call_target="tpu_custom_call" | custom-call | flops 15000000512 | bytes 20971520 | tf_op jit(solution)/shard_map/backward_second_b/pallas_call | solution.py:544
  241.5 15.7 %backward_first_a.1 = (bf16[8,144,768]{2,1,0:T(8,128)(2,1)}, bf16[8,144,768]{2,1,0:T(8,128)(2,1)}, f32[512,768]{1,0:T(8,128)}, bf16[512,768]{1,0:T(8,128)(2,1)}, f32[16,768]{1,0:T(8,128)}) custom-call(s32[3]{0:T(128)} %pad_add_fusion.1.flag, bf16[512,768]{1,0:T(8,128)(2,1)} %get-tuple-element.205.rest_0_, bf16[768,768]{1,0:T(8,128)(2,1)} %bitcast.141, ...), custom_call_target="tpu_custom_call" | custom-call | flops 12000000000 | bytes 20971520 | tf_op jit(solution)/shard_map/backward_first_a/pallas_call | solution.py:405
  264.3 16.1 %collective-permute-done.17.came_ref = bf16[4,144,768]{2,1,0:T(8,128)(2,1)} collective-permute-done((bf16[4,144,768]{2,1,0:T(8,128)(2,1)}, bf16[4,144,768]{2,1,0:T(8,128)(2,1)}, u32[]{:S(2)}, u32[]{:S(2)}) %collective-permute-start.17) | collective-permute-done | bytes 884768 | tf_op jit(solution)/shard_map/ppermute | solution.py:785
  292.2 20.1 %backward_first_b.1 = (bf16[8,80,768]{2,1,0:T(8,128)(2,1)}, bf16[8,80,768]{2,1,0:T(8,128)(2,1)}, bf16[512,768]{1,0:T(8,128)(2,1)}, bf16[768,768]{1,0:T(8,128)(2,1)}) custom-call(s32[3]{0:T(128)} %pad_add_fusion.1.flag, f32[512,768]{1,0:T(8,128)} %get-tuple-element.219.attn_in, bf16[512,768]{1,0:T(8,128)(2,1)} %get-tuple-element.220.back_low, ...), custom_call_target="tpu_custom_call" | custom-call | flops 15000000512 | bytes 20971520 | tf_op jit(solution)/shard_map/backward_first_b/pallas_call | solution.py:544
  345.3 10.1 %collective-permute-done.25.came_ref = bf16[4,144,768]{2,1,0:T(8,128)(2,1)} collective-permute-done((bf16[4,144,768]{2,1,0:T(8,128)(2,1)}, bf16[4,144,768]{2,1,0:T(8,128)(2,1)}, u32[]{:S(2)}, u32[]{:S(2)}) %collective-permute-start.25) | collective-permute-done | bytes 884768 | tf_op jit(solution)/shard_map/ppermute | solution.py:785
  365.2 4.6 owner_sum.1
  369.9 8.4 %collective-permute-done.27.refs_6_ = bf16[144,768]{1,0:T(8,128)(2,1)S(1)} collective-permute-done((bf16[144,768]{1,0:T(8,128)(2,1)}, bf16[144,768]{1,0:T(8,128)(2,1)S(1)}, u32[]{:S(2)}, u32[]{:S(2)}) %collective-permute-start.27) | collective-permute-done | bytes 221216 | tf_op jit(solution)/shard_map/ppermute | solution.py:785
  403.5 10.9 %collective-permute-done.35.refs_6_ = bf16[80,768]{1,0:T(8,128)(2,1)S(1)} collective-permute-done((bf16[80,768]{1,0:T(8,128)(2,1)}, bf16[80,768]{1,0:T(8,128)(2,1)S(1)}, u32[]{:S(2)}, u32[]{:S(2)}) %collective-permute-start.35) | collective-permute-done | bytes 122912 | tf_op jit(solution)/shard_map/ppermute | solution.py:785
  421.9 4.9 %collective-permute-done.41 = bf16[144,768]{1,0:T(8,128)(2,1)S(1)} collective-permute-done((bf16[144,768]{1,0:T(8,128)(2,1)S(1)}, bf16[144,768]{1,0:T(8,128)(2,1)S(1)}, u32[]{:S(2)}, u32[]{:S(2)}) %collective-permute-start.41) | collective-permute-done | bytes 221216 | tf_op jit(solution)/shard_map/ppermute | solution.py:785
  433.3 14.3 %collective-permute-done.43 = bf16[4,144,768]{2,1,0:T(8,128)(2,1)S(1)} collective-permute-done((bf16[4,144,768]{2,1,0:T(8,128)(2,1)S(1)}, bf16[4,144,768]{2,1,0:T(8,128)(2,1)S(1)}, u32[]{:S(2)}, u32[]{:S(2)}) %collective-permute-start.43) | collective-permute-done | bytes 884768 | tf_op jit(solution)/shard_map/ppermute | solution.py:785
  448.5 10.9 %collective-permute-done.48 = bf16[4,64,768]{2,1,0:T(8,128)(2,1)S(1)} collective-permute-done((bf16[4,64,768]{2,1,0:T(8,128)(2,1)S(1)}, bf16[4,64,768]{2,1,0:T(8,128)(2,1)S(1)}, u32[]{:S(2)}, u32[]{:S(2)}) %collective-permute-start.48) | collective-permute-done | bytes 393248 | tf_op jit(solution)/shard_map/ppermute | solution.py:785
  459.6 5.5 %collective-permute-done.38 = bf16[960,768]{1,0:T(8,128)(2,1)S(1)} collective-permute-done((bf16[960,768]{1,0:T(8,128)(2,1)S(1)}, bf16[960,768]{1,0:T(8,128)(2,1)S(1)}, u32[]{:S(2)}, u32[]{:S(2)}) %collective-permute-start.38) | collective-permute-done | bytes 1474592 | tf_op jit(solution)/shard_map/ppermute | solution.py:840
  469.1 7.0 %unpack_sums.1 = (f32[768,768]{1,0:T(8,128)}, f32[768,768]{1,0:T(8,128)}, f32[768,768]{1,0:T(8,128)}, f32[4,192,192]{2,1,0:T(8,128)}, f32[4,192,192]{2,1,0:T(8,1...) custom-call(s32[3]{0:T(128)} %pad_add_fusion.1.flag, ...), custom_call_target="tpu_custom_call" | custom-call | flops 1000000000 | bytes 16777216 | tf_op jit(solution)/shard_map/unpack_sums/pallas_call | solution.py:652
  (292 shorter events, 176.2 us)
Async XLA Ops:
  7.2 148.8 %all-gather.2.cloned.1.call-start = ((), (), s32[]{:S(2)}) async-start(), calls=%async_computation.7 | async-start | bytes 25067520 | tf_op jit(solution)/shard_map/all_gather | solution.py:851
  39.7 61.1 %all-to-all-start.4 = ((bf16[16,48,768]{2,1,0:T(8,128)(2,1)}), bf16[16,48,768]{2,1,0:T(8,128)(2,1)}, u32[]{:S(2)}, u32[]{:S(2)}) async-start(bf16[16,48,768]{2,1,0:T(8,128)(2,1)} %bitcast.12), calls=%async_computation.4 | async-start | bytes 2359296 | tf_op jit(solution)/shard_map/all_to_all | solution.py:848
  44.6 56.2 %collective-permute-start.9 = (f32[8,768]{1,0:T(8,128)S(1)}, f32[8,768]{1,0:T(8,128)S(1)}, u32[]{:S(2)}, u32[]{:S(2)}) collective-permute-start(f32[8,768]{1,0:T(8,128)S(1)} %concatenate.61.rest_4_.rest_6_.rest_5_.rest_9_), channel_id=1, source_target_pairs={{0,16},{16,0},{1,17},{17,1},{2,18},{18,2},{3,19},{19,3},{4,20},{20... | collective-permute-start | bytes 73736 | tf_op jit(solution)/shard_map/ppermute | solution.py:840
  48.7 27.5 %collective-permute-start.1 = (bf16[384,768]{1,0:T(8,128)(2,1)S(1)}, bf16[384,768]{1,0:T(8,128)(2,1)}, u32[]{:S(2)}, u32[]{:S(2)}) collective-permute-start(bf16[384,768]{1,0:T(8,128)(2,1)S(1)} %constant_dynamic-slice_fusion.2), channel_id=1, source_target_pairs={{0,16},{16,0},{1,17},{17,1},{2,18},{18,2},{3,19},{19,3},{4,20},{20... | collective-permute-start | bytes 1769480 | tf_op jit(solution)/shard_map/ppermute | solution.py:840
  51.4 37.4 %collective-permute-start.2 = (bf16[384,768]{1,0:T(8,128)(2,1)S(1)}, bf16[384,768]{1,0:T(8,128)(2,1)}, u32[]{:S(2)}, u32[]{:S(2)}) collective-permute-start(bf16[384,768]{1,0:T(8,128)(2,1)S(1)} %constant_dynamic-slice_fusion.1), channel_id=1, source_target_pairs={{0,16},{16,0},{1,17},{17,1},{2,18},{18,2},{3,19},{19,3},{4,20},{20... | collective-permute-start | bytes 1769480 | tf_op jit(solution)/shard_map/ppermute | solution.py:840
  55.0 43.3 %collective-permute-start.4 = (bf16[288,768]{1,0:T(8,128)(2,1)}, bf16[288,768]{1,0:T(8,128)(2,1)}, u32[]{:S(2)}, u32[]{:S(2)}) collective-permute-start(bf16[288,768]{1,0:T(8,128)(2,1)} %constant_dynamic-slice_fusion), channel_id=1, source_target_pairs={{0,16},{16,0},{1,17},{17,1},{2,18},{18,2},{3,19},{19,3},{4,20},{20... | collective-permute-start | bytes 1327112 | tf_op jit(solution)/shard_map/ppermute | solution.py:840
  63.5 37.3 %collective-permute-start.7 = (bf16[384,768]{1,0:T(8,128)(2,1)}, bf16[384,768]{1,0:T(8,128)(2,1)}, u32[]{:S(2)}, u32[]{:S(2)}) collective-permute-start(bf16[384,768]{1,0:T(8,128)(2,1)} %collective-permute-done.3.rest_7_.rest_9_.rest_8_.rest_12_), channel_id=1, source_target_pairs={{0,1},{1,0},{2,3},{3,2},{4,5},{5,4},{6,7},{7,6},{8,9},{9,8},{10,11... | collective-permute-start | bytes 1769480 | tf_op jit(solution)/shard_map/ppermute | solution.py:785
  76.2 24.7 %collective-permute-start.5 = (bf16[384,768]{1,0:T(8,128)(2,1)}, bf16[384,768]{1,0:T(8,128)(2,1)}, u32[]{:S(2)}, u32[]{:S(2)}) collective-permute-start(bf16[384,768]{1,0:T(8,128)(2,1)} %collective-permute-done.1.rest_5_.rest_7_.rest_6_.rest_10_), channel_id=1, source_target_pairs={{0,1},{1,0},{2,3},{3,2},{4,5},{5,4},{6,7},{7,6},{8,9},{9,8},{10,11... | collective-permute-start | bytes 1769480 | tf_op jit(solution)/shard_map/ppermute | solution.py:785
  144.4 31.8 %collective-permute-start.13 = (bf16[80,768]{1,0:T(8,128)(2,1)S(1)}, bf16[80,768]{1,0:T(8,128)(2,1)S(1)}, u32[]{:S(2)}, u32[]{:S(2)}) collective-permute-start(bf16[80,768]{1,0:T(8,128)(2,1)S(1)} %maximum_select_fusion.1.head_ref), channel_id=1, source_target_pairs={{0,12},{1,13},{2,14},{3,15},{4,8},{5,9},{6,10},{7,11},{8,4},{9,5},... | collective-permute-start | bytes 368648 | tf_op jit(solution)/shard_map/ppermute | solution.py:785
  148.2 27.9 %collective-permute-start.12 = (bf16[80,768]{1,0:T(8,128)(2,1)S(1)}, bf16[80,768]{1,0:T(8,128)(2,1)S(1)}, u32[]{:S(2)}, u32[]{:S(2)}) collective-permute-start(bf16[80,768]{1,0:T(8,128)(2,1)S(1)} %maximum_select_fusion.1.head_ref), channel_id=1, source_target_pairs={{0,8},{1,9},{2,10},{3,11},{4,12},{5,13},{6,14},{7,15},{8,0},{9,1},... | collective-permute-start | bytes 368648 | tf_op jit(solution)/shard_map/ppermute | solution.py:785
  148.2 28.0 %collective-permute-start.11 = (bf16[80,768]{1,0:T(8,128)(2,1)S(1)}, bf16[80,768]{1,0:T(8,128)(2,1)S(1)}, u32[]{:S(2)}, u32[]{:S(2)}) collective-permute-start(bf16[80,768]{1,0:T(8,128)(2,1)S(1)} %maximum_select_fusion.1.head_ref), channel_id=1, source_target_pairs={{0,4},{1,5},{2,6},{3,7},{4,0},{5,1},{6,2},{7,3},{8,12},{9,13},{10,... | collective-permute-start | bytes 368648 | tf_op jit(solution)/shard_map/ppermute | solution.py:785
  180.6 99.8 %all-to-all-start.5 = ((bf16[16,80,960]{2,1,0:T(8,128)(2,1)}), bf16[16,80,960]{2,1,0:T(8,128)(2,1)S(1)}, u32[]{:S(2)}, u32[]{:S(2)}) async-start(bf16[16,80,960]{2,1,0:T(8,128)(2,1)} %bitcast.109), calls=%async_computation.5 | async-start | bytes 5242880 | tf_op jit(solution)/shard_map/all_to_all | solution.py:848
  212.9 24.8 %collective-permute-start.15 = (bf16[8,144,768]{2,1,0:T(8,128)(2,1)}, bf16[8,144,768]{2,1,0:T(8,128)(2,1)}, u32[]{:S(2)}, u32[]{:S(2)}) collective-permute-start(bf16[8,144,768]{2,1,0:T(8,128)(2,1)} %get-tuple-element.197), channel_id=1, source_target_pairs={{0,1},{1,0},{2,3},{3,2},{4,5},{5,4},{6,7},{7,6},{8,9},{9,8},{10,11... | collective-permute-start | bytes 5308424 | tf_op jit(solution)/shard_map/ppermute | solution.py:785
  257.2 33.2 %collective-permute-start.22 = (bf16[8,144,768]{2,1,0:T(8,128)(2,1)}, bf16[8,144,768]{2,1,0:T(8,128)(2,1)}, u32[]{:S(2)}, u32[]{:S(2)}) collective-permute-start(bf16[8,144,768]{2,1,0:T(8,128)(2,1)} %get-tuple-element.240), channel_id=1, source_target_pairs={{0,1},{1,0},{2,3},{3,2},{4,5},{5,4},{6,7},{7,6},{8,9},{9,8},{10,11... | collective-permute-start | bytes 5308424 | tf_op jit(solution)/shard_map/ppermute | solution.py:785
  263.9 52.4 %collective-permute-start.24 = (bf16[8,80,768]{2,1,0:T(8,128)(2,1)}, bf16[8,80,768]{2,1,0:T(8,128)(2,1)}, u32[]{:S(2)}, u32[]{:S(2)}) collective-permute-start(bf16[8,80,768]{2,1,0:T(8,128)(2,1)} %constant_dynamic-update-slice_fusion.3), channel_id=1, source_target_pairs={{0,1},{1,0},{2,3},{3,2},{4,5},{5,4},{6,7},{7,6},{8,9},{9,8},{10,11... | collective-permute-start | bytes 2949128 | tf_op jit(solution)/shard_map/ppermute | solution.py:785
  283.9 28.7 %collective-permute-start.19 = (bf16[144,768]{1,0:T(8,128)(2,1)}, bf16[144,768]{1,0:T(8,128)(2,1)}, u32[]{:S(2)}, u32[]{:S(2)}) collective-permute-start(bf16[144,768]{1,0:T(8,128)(2,1)} %get-tuple-element.237), channel_id=1, source_target_pairs={{0,4},{1,5},{2,6},{3,7},{4,0},{5,1},{6,2},{7,3},{8,12},{9,13},{10,... | collective-permute-start | bytes 663560 | tf_op jit(solution)/shard_map/ppermute | solution.py:785
  285.3 27.3 %collective-permute-start.20 = (bf16[144,768]{1,0:T(8,128)(2,1)}, bf16[144,768]{1,0:T(8,128)(2,1)}, u32[]{:S(2)}, u32[]{:S(2)}) collective-permute-start(bf16[144,768]{1,0:T(8,128)(2,1)} %get-tuple-element.238), channel_id=1, source_target_pairs={{0,8},{1,9},{2,10},{3,11},{4,12},{5,13},{6,14},{7,15},{8,0},{9,1},... | collective-permute-start | bytes 663560 | tf_op jit(solution)/shard_map/ppermute | solution.py:785
  287.3 25.3 %collective-permute-start.21 = (bf16[144,768]{1,0:T(8,128)(2,1)}, bf16[144,768]{1,0:T(8,128)(2,1)}, u32[]{:S(2)}, u32[]{:S(2)}) collective-permute-start(bf16[144,768]{1,0:T(8,128)(2,1)} %get-tuple-element.239), channel_id=1, source_target_pairs={{0,12},{1,13},{2,14},{3,15},{4,8},{5,9},{6,10},{7,11},{8,4},{9,5},... | collective-permute-start | bytes 663560 | tf_op jit(solution)/shard_map/ppermute | solution.py:785
  316.3 48.9 %all-to-all-start.6 = ((bf16[16,48,768]{2,1,0:T(8,128)(2,1)}), bf16[16,48,768]{2,1,0:T(8,128)(2,1)}, u32[]{:S(2)}, u32[]{:S(2)}) async-start(bf16[16,48,768]{2,1,0:T(8,128)(2,1)} %bitcast.124), calls=%async_computation.6 | async-start | bytes 2359296 | tf_op jit(solution)/shard_map/all_to_all | solution.py:848
  320.9 34.5 %collective-permute-start.25 = (bf16[4,144,768]{2,1,0:T(8,128)(2,1)}, bf16[4,144,768]{2,1,0:T(8,128)(2,1)}, u32[]{:S(2)}, u32[]{:S(2)}) collective-permute-start(bf16[4,144,768]{2,1,0:T(8,128)(2,1)} %get-tuple-element.261), channel_id=1, source_target_pairs={{0,2},{1,3},{2,0},{3,1},{4,6},{5,7},{6,4},{7,5},{8,10},{9,11},{10,... | collective-permute-start | bytes 2654216 | tf_op jit(solution)/shard_map/ppermute | solution.py:785
  322.7 39.5 %collective-permute-start.32 = (bf16[8,80,768]{2,1,0:T(8,128)(2,1)}, bf16[8,80,768]{2,1,0:T(8,128)(2,1)}, u32[]{:S(2)}, u32[]{:S(2)}) collective-permute-start(bf16[8,80,768]{2,1,0:T(8,128)(2,1)} %get-tuple-element.274), channel_id=1, source_target_pairs={{0,1},{1,0},{2,3},{3,2},{4,5},{5,4},{6,7},{7,6},{8,9},{9,8},{10,11... | collective-permute-start | bytes 2949128 | tf_op jit(solution)/shard_map/ppermute | solution.py:785
  364.8 26.9 %collective-permute-start.33 = (bf16[4,80,768]{2,1,0:T(8,128)(2,1)}, bf16[4,80,768]{2,1,0:T(8,128)(2,1)S(1)}, u32[]{:S(2)}, u32[]{:S(2)}) collective-permute-start(bf16[4,80,768]{2,1,0:T(8,128)(2,1)} %get-tuple-element.276), channel_id=1, source_target_pairs={{0,2},{1,3},{2,0},{3,1},{4,6},{5,7},{6,4},{7,5},{8,10},{9,11},{10,... | collective-permute-start | bytes 1474568 | tf_op jit(solution)/shard_map/ppermute | solution.py:785
  401.5 25.3 %collective-permute-start.41 = (bf16[144,768]{1,0:T(8,128)(2,1)S(1)}, bf16[144,768]{1,0:T(8,128)(2,1)S(1)}, u32[]{:S(2)}, u32[]{:S(2)}) collective-permute-start(bf16[144,768]{1,0:T(8,128)(2,1)S(1)} %get-tuple-element.309), channel_id=1, source_target_pairs={{0,8},{1,9},{2,10},{3,11},{4,12},{5,13},{6,14},{7,15},{8,0},{9,1},... | collective-permute-start | bytes 663560 | tf_op jit(solution)/shard_map/ppermute | solution.py:785
  433.0 32.1 %collective-permute-start.38 = (bf16[960,768]{1,0:T(8,128)(2,1)S(1)}, bf16[960,768]{1,0:T(8,128)(2,1)S(1)}, u32[]{:S(2)}, u32[]{:S(2)}) collective-permute-start(bf16[960,768]{1,0:T(8,128)(2,1)S(1)} %copy-done.6), channel_id=1, source_target_pairs={{0,16},{16,0},{1,17},{17,1},{2,18},{18,2},{3,19},{19,3},{4,20},{20... | collective-permute-start | bytes 4423688 | tf_op jit(solution)/shard_map/ppermute | solution.py:840
  (73 other events, 899.1 us)
Sparse Core Ops, SparseCore 0:
  9.6 146.3 all-gather.1

commit v2 on v1

--- a/solution.py
+++ b/solution.py
@@ -300,10 +300,26 @@
     return out[0], out[1 : 1 + SAVES], out[1 + SAVES : 1 + 2 * SAVES], out[-2], out[-1]
 
 
-def put_chunks(packed_ref, core, source, rows, at):
+def chunk_place(chunk, core, in_order):
+    if in_order:
+        return chunk
+    return chunk // 2 + (CHUNKS // 2) * (core if chunk % 2 == 0 else 1 - core)
+
+
+def put_chunks(packed_ref, core, in_order, source, rows, at):
     for chunk in range(CHUNKS):
-        side = core if chunk % 2 == 0 else 1 - core
-        packed_ref[side, chunk // 2, at : at + rows, :] = source[chunk * rows : (chunk + 1) * rows, :].astype(BF)
+        packed_ref[chunk_place(chunk, core, in_order), at : at + rows, :] = source[chunk * rows : (chunk + 1) * rows, :].astype(BF)
+
+
+def ship_chunks(packed_ref, outs, sems):
+    if len(outs) == 1:
+        made = [pltpu.make_async_copy(packed_ref, outs[0], sems.at[0])]
+    else:
+        half = CHUNKS // 2
+        made = [pltpu.make_async_copy(packed_ref.at[pl.ds(i * half, half)], outs[i], sems.at[i]) for i in range(2)]
+    for c in made:
+        c.start()
+    return made
 
 
 def bwd_a_kernel(last, flag, *rest):
@@ -320,7 +336,8 @@
         picked_back, mask_row = take(2)
     own, other = take(5), take(9)
     sources = take(7)
-    keep_out, away_out, attn_ref, back_low, vec_ref = take(5)
+    packed_out = take(1 if last else 2)
+    attn_ref, back_low, vec_ref = take(3)
     weights = take(4)
     mid_ref, low_ref, packed_ref = take(3)
     saves = take(7)
@@ -379,9 +396,9 @@
         mid_ref[:, lanes(g)] += mm_nt(expand_in, expand[g])
         for part in range(CHUNKS // GROUPS):
             chunk = g * (CHUNKS // GROUPS) + part
-            side = core if chunk % 2 == 0 else 1 - core
-            packed_ref[side, chunk // 2, 0:each, :] = shrink_grad[part * each : (part + 1) * each, :]
-            packed_ref[side, chunk // 2, each : 2 * each, :] = expand_grad[part * each : (part + 1) * each, :]
+            at = chunk_place(chunk, core, last)
+            packed_ref[at, 0:each, :] = shrink_grad[part * each : (part + 1) * each, :]
+            packed_ref[at, each : 2 * each, :] = expand_grad[part * each : (part + 1) * each, :]
     copies[1].wait()
     hidden_back = mid_ref[...]
     hat = hat_a[...].astype(F32)
@@ -391,10 +408,8 @@
     attn_ref[...] = attn_back
     attended_in = attn_back.astype(BF)
     copies[0].wait()
-    put_chunks(packed_ref, core, mm_tn(mix_ref[...], attended_in), each, 2 * each)
-    ship = [pltpu.make_async_copy(packed_ref.at[1], away_out, sem_o.at[0]), pltpu.make_async_copy(packed_ref.at[0], keep_out, sem_o.at[1])]
-    for c in ship:
-        c.start()
+    put_chunks(packed_ref, core, last, mm_tn(mix_ref[...], attended_in), each, 2 * each)
+    ship = ship_chunks(packed_ref, packed_out, sem_o)
     back_low[...] = mm_nt(attended_in, output[...]).astype(BF)
     for c in ship:
         c.wait()
@@ -404,15 +419,15 @@
     chosen = (5, 6, 7, 8, 9, 10, 13)
     return pl.pallas_call(
         functools.partial(bwd_a_kernel, last),
-        out_shape=[
-            jax.ShapeDtypeStruct((CHUNKS // 2, ROWS_A, D), BF), jax.ShapeDtypeStruct((CHUNKS // 2, ROWS_A, D), BF),
+        out_shape=([jax.ShapeDtypeStruct((CHUNKS, ROWS_A, D), BF)] if last else [jax.ShapeDtypeStruct((CHUNKS // 2, ROWS_A, D), BF)] * 2)
+        + [
             jax.ShapeDtypeStruct((N, D), F32), jax.ShapeDtypeStruct((N, D), BF), jax.ShapeDtypeStruct((16, D), F32),
         ],
         in_specs=[SM] + [VM] * len(extra) + [HB] * (14 + len(chosen)),
-        out_specs=[HB, HB, VM, VM, VM],
+        out_specs=[HB] * (1 if last else 2) + [VM, VM, VM],
         scratch_shapes=[
             pltpu.VMEM((GROUPS, 256, D), BF), pltpu.VMEM((GROUPS, 256, D), BF), pltpu.VMEM((D, D), BF), pltpu.VMEM((8, D), F32),
-            pltpu.VMEM((N, D), F32), pltpu.VMEM((N, D), BF), pltpu.VMEM((2, CHUNKS // 2, ROWS_A, D), BF),
+            pltpu.VMEM((N, D), F32), pltpu.VMEM((N, D), BF), pltpu.VMEM((CHUNKS, ROWS_A, D), BF),
         ]
         + [pltpu.VMEM(SAVE_SHAPES[i], SAVE_TYPES[i]) for i in chosen]
         + [pltpu.SemaphoreType.DMA((13,)), pltpu.SemaphoreType.DMA((len(chosen),)), pltpu.SemaphoreType.DMA((2,)), pltpu.SemaphoreType.DMA((2, GROUPS))],
@@ -518,17 +533,14 @@
         grad = mm(places, back).astype(BF)
         for s in range(2):
             block = jnp.concatenate([grad[part * (N // 2) : (part + 1) * (N // 2), s * 384 : (s + 1) * 384] for part in range(2)], axis=1)
-            put_chunks(packed_ref, core, block, SLAB, ROWS_B + s * SLAB)
+            put_chunks(packed_ref, core, False, block, SLAB, ROWS_B + s * SLAB)
         slots = slot_grad.shape[0]
         slot_grad[...] = mm((lax.broadcasted_iota(jnp.int32, (slots, N), 0) == slot_row[...]).astype(BF), back).astype(BF)
     else:
         back_ref[...] = go.astype(BF)
     grad_ref[3 * WIDE :, :] = vec_ref[...].astype(BF)
-    put_chunks(packed_ref, core, grad_ref, ROWS_B, 0)
-    ship = [pltpu.make_async_copy(packed_ref.at[1], away_out, sem_o.at[0]), pltpu.make_async_copy(packed_ref.at[0], keep_out, sem_o.at[1])]
-    for c in ship:
-        c.start()
-    for c in ship:
+    put_chunks(packed_ref, core, False, grad_ref, ROWS_B, 0)
+    for c in ship_chunks(packed_ref, (keep_out, away_out), sem_o):
         c.wait()
 
 
@@ -548,7 +560,7 @@
         out_specs=[HB, HB] + [VM] * (len(out_shape) - 2),
         scratch_shapes=[
             pltpu.VMEM((3 * WIDE, D), BF), pltpu.VMEM((3, GROUPS, 256, 256), BF), pltpu.VMEM((N, D), F32),
-            pltpu.VMEM((QKV_ROWS - 3 * WIDE, D), F32), pltpu.VMEM((2, CHUNKS // 2, rows, D), BF),
+            pltpu.VMEM((QKV_ROWS - 3 * WIDE, D), F32), pltpu.VMEM((CHUNKS, rows, D), BF),
         ]
         + [pltpu.VMEM((N, D), BF)] * 3 + [pltpu.VMEM((QKV_ROWS, D), BF)]
         + [pltpu.VMEM(SAVE_SHAPES[i], SAVE_TYPES[i]) for i in chosen]
@@ -591,9 +603,9 @@
     )(me, keep, came)
 
 
-def finish_kernel(part, flag, place_ref, *refs):
-    parts1, parts0 = refs[0:4], refs[4:8]
-    mine, theirs = refs[8:10]
+def finish_kernel(part, count1, flag, place_ref, *refs):
+    parts1, parts0 = refs[:count1], refs[count1:-2]
+    mine, theirs = refs[-2:]
     sums = []
     for parts in (parts0, parts1):
         total = parts[0][...].astype(F32)
@@ -615,24 +627,26 @@
     rows = ROWS_A if part == 0 else ROWS_B + SLAB
     one = jax.ShapeDtypeStruct((rows, D), BF)
     return pl.pallas_call(
-        functools.partial(finish_kernel, part), out_shape=[one, one], in_specs=[SM, SM] + [VM] * 8, out_specs=[VM] * 2,
+        functools.partial(finish_kernel, part, len(parts1)), out_shape=[one, one],
+        in_specs=[SM, SM] + [VM] * (len(parts1) + len(parts0)), out_specs=[VM] * 2,
         compiler_params=pltpu.CompilerParams(vmem_limit_bytes=VMEM_LIMIT),
         cost_estimate=pl.CostEstimate(flops=GFLOP, bytes_accessed=2 << 20, transcendentals=0), name="finish_chunks",
     )(flag, place, *parts1, *parts0)
 
 
-def unpack_kernel(flag, place_ref, a_own, a_came, b_own, b_came, shrink, expand, output, query, key, value, vecs, embed, position, grid, slab):
+def unpack_kernel(flag, place_ref, a_all, b_own, b_came, shrink, expand, output, query, key, value, vecs, embed, position, grid, slab):
     each = ROWS_A // 3
     half = CHUNKS // 2
+    for i in range(CHUNKS):
+        rows = slice(i * each, (i + 1) * each)
+        block = a_all[i].astype(F32)
+        shrink[rows, :] = block[0:each]
+        expand[rows, :] = block[each : 2 * each]
+        output[rows, :] = block[2 * each :]
     for core in range(2):
-        a_ref, b_ref = (a_own, b_own) if core == 0 else (a_came, b_came)
+        b_ref = b_own if core == 0 else b_came
         for i in range(half):
             device = place_ref[0] ^ (4 * (i % 4) + 2 * (i // 4) + core)
-            rows = pl.ds(pl.multiple_of(device * each, each), each)
-            block = a_ref[i].astype(F32)
-            shrink[rows, :] = block[0:each]
-            expand[rows, :] = block[each : 2 * each]
-            output[rows, :] = block[2 * each :]
             block = b_ref[i].astype(F32)
             grid[pl.ds(pl.multiple_of(device * ROWS_B, ROWS_B), ROWS_B), :] = block[:ROWS_B]
             slab[pl.ds(pl.multiple_of(device * SLAB, SLAB), SLAB), :] = block[ROWS_B:]
@@ -646,19 +660,19 @@
         position[part * (N // 2) : (part + 1) * (N // 2), :] = slab[:, part * (D // 2) : (part + 1) * (D // 2)]
 
 
-def unpack_call(flag, place, a_own, a_came, b_own, b_came):
+def unpack_call(flag, place, a_all, b_own, b_came):
     square = jax.ShapeDtypeStruct((D, D), F32)
     group = jax.ShapeDtypeStruct((GROUPS, WIDE, WIDE), F32)
     return pl.pallas_call(
         unpack_kernel,
         out_shape=[square] * 3 + [group] * 3
         + [jax.ShapeDtypeStruct((8, D), F32), jax.ShapeDtypeStruct((1, D), F32), jax.ShapeDtypeStruct((N, D // 2), F32)],
-        in_specs=[SM, SM] + [VM] * 4,
+        in_specs=[SM, SM] + [VM] * 3,
         out_specs=[VM] * 9,
         scratch_shapes=[pltpu.VMEM((QKV_ROWS, D), F32), pltpu.VMEM((CHUNKS * SLAB, D), F32)],
         compiler_params=pltpu.CompilerParams(vmem_limit_bytes=VMEM_LIMIT),
         cost_estimate=pl.CostEstimate(flops=GFLOP, bytes_accessed=16 << 20, transcendentals=0), name="unpack_sums",
-    )(flag, place, a_own, a_came, b_own, b_came)
+    )(flag, place, a_all, b_own, b_came)
 
 
 def plan_kernel(room, id_row, id_col, owner_row, owner_col, slot_col, slot_row, want_ref, most_ref):
@@ -709,54 +723,77 @@
         in_specs=[SM, VM, VM],
         out_specs=VM,
         compiler_params=pltpu.CompilerParams(vmem_limit_bytes=VMEM_LIMIT),
-        cost_estimate=pl.CostEstimate(flops=3 * GFLOP, bytes_accessed=3 << 20, transcendentals=0),
+        cost_estimate=pl.CostEstimate(flops=3 * GFLOP, bytes_accessed=20 << 20, transcendentals=0),
         name="serve_rows",
     )(base, ids_col, table)
 
 
-def stream_kernel(grad_ref, head_ref, table_ref, back_ref, logit_ref):
+def back_pass_kernel(grad_ref, table_ref, back_ref):
     @pl.when(pl.program_id(0) == 0)
     def _():
         back_ref[...] = jnp.zeros_like(back_ref)
 
     back_ref[...] += mm(grad_ref[...], table_ref[...])
+
+
+def back_pass(flat_grad, table):
+    vocab, masks = table.shape[0], flat_grad.shape[0]
+    tile = 1536
+    return pl.pallas_call(
+        back_pass_kernel,
+        grid=(vocab // tile,),
+        out_shape=jax.ShapeDtypeStruct((masks, D), F32),
+        in_specs=[pl.BlockSpec((masks, tile), lambda i: (0, i)), pl.BlockSpec((tile, D), lambda i: (i, 0))],
+        out_specs=pl.BlockSpec((masks, D), lambda i: (0, 0)),
+        compiler_params=pltpu.CompilerParams(vmem_limit_bytes=VMEM_LIMIT),
+        cost_estimate=pl.CostEstimate(flops=10 * GFLOP, bytes_accessed=20 << 20, transcendentals=0),
+        name="table_back_pass",
+    )(flat_grad, table)
+
+
+def logit_pass_kernel(head_ref, table_ref, logit_ref):
     logit_ref[...] = mm_nt(head_ref[...], table_ref[...]).astype(BF)
 
 
-def stream_call(flat_grad, head_rows, table):
-    vocab, masks = table.shape[0], flat_grad.shape[0]
-    tile = 1024
-    return pl.pallas_call(
-        stream_kernel,
+def logit_pass(head_rows, table):
+    vocab, masks = table.shape[0], head_rows.shape[0]
+    tile = 1536
+    return pl.pallas_call(
+        logit_pass_kernel,
         grid=(vocab // tile,),
-        out_shape=[jax.ShapeDtypeStruct((masks, D), F32), jax.ShapeDtypeStruct((masks, vocab), BF)],
-        in_specs=[
-            pl.BlockSpec((masks, tile), lambda i: (0, i)),
-            pl.BlockSpec((masks, D), lambda i: (0, 0)),
-            pl.BlockSpec((tile, D), lambda i: (i, 0)),
-        ],
-        out_specs=[pl.BlockSpec((masks, D), lambda i: (0, 0)), pl.BlockSpec((masks, tile), lambda i: (0, i))],
-        compiler_params=pltpu.CompilerParams(vmem_limit_bytes=VMEM_LIMIT),
-        cost_estimate=pl.CostEstimate(flops=10 * GFLOP, bytes_accessed=28 << 20, transcendentals=0),
-        name="table_pass",
-    )(flat_grad, head_rows, table)
-
-
-def owner_kernel(base_ref, ids_ref, rows_ref, acc_ref, out_ref):
+        out_shape=jax.ShapeDtypeStruct((masks, vocab), BF),
+        in_specs=[pl.BlockSpec((masks, D), lambda i: (0, 0)), pl.BlockSpec((tile, D), lambda i: (i, 0))],
+        out_specs=pl.BlockSpec((masks, tile), lambda i: (0, i)),
+        compiler_params=pltpu.CompilerParams(vmem_limit_bytes=VMEM_LIMIT),
+        cost_estimate=pl.CostEstimate(flops=10 * GFLOP, bytes_accessed=20 << 20, transcendentals=0),
+        name="table_logit_pass",
+    )(head_rows, table)
+
+
+def owner_kernel(place_ref, base_ref, ids_ref, rows_ref, grads_ref, heads_own, heads_came, crowd_ref, out_ref, ordered):
+    masks = heads_own.shape[1]
+    for core in range(2):
+        heads = heads_own if core == 0 else heads_came
+        for i in range(heads.shape[0]):
+            device = place_ref[0] ^ (4 * (i % 4) + 2 * (i // 4) + core)
+            ordered[pl.ds(pl.multiple_of(device * masks, masks), masks), :] = heads[i]
     counter = lax.broadcasted_iota(jnp.int32, (out_ref.shape[0], ids_ref.shape[1]), 0) + base_ref[0]
-    out_ref[...] = (acc_ref[...] + mm((counter == ids_ref[...]).astype(BF), rows_ref[...])).astype(BF)
-
-
-def owner_call(base, ids_row, rows, total):
+    total = crowd_ref[...] + mm((counter == ids_ref[...]).astype(BF), rows_ref[...])
+    out_ref[...] = (total + mm_tn(grads_ref[...], ordered[...])).astype(BF)
+
+
+def owner_call(place, base, ids_row, rows, grads, heads, crowd):
+    masks = heads[0].shape[1]
     return pl.pallas_call(
         owner_kernel,
-        out_shape=jax.ShapeDtypeStruct(total.shape, BF),
-        in_specs=[SM, VM, VM, VM],
+        out_shape=jax.ShapeDtypeStruct(crowd.shape, BF),
+        in_specs=[SM, SM] + [VM] * 6,
         out_specs=VM,
-        compiler_params=pltpu.CompilerParams(vmem_limit_bytes=VMEM_LIMIT),
-        cost_estimate=pl.CostEstimate(flops=3 * GFLOP, bytes_accessed=6 << 20, transcendentals=0),
+        scratch_shapes=[pltpu.VMEM((2 * heads[0].shape[0] * masks, D), BF)],
+        compiler_params=pltpu.CompilerParams(vmem_limit_bytes=VMEM_LIMIT),
+        cost_estimate=pl.CostEstimate(flops=6 * GFLOP, bytes_accessed=20 << 20, transcendentals=0),
         name="owner_sum",
-    )(base, ids_row, rows, total)
+    )(place, base, ids_row, rows, grads, heads[0], heads[1], crowd)
 
 
 def dense_kernel(base_ref, ids_ref, rows_ref, out_ref):
@@ -787,17 +824,6 @@
 
 def bits_of(axis):
     return [1 << b for b in range(lax.axis_size(axis).bit_length() - 1)]
-
-
-def exclusive(place, stacked):
-    count = stacked.shape[0]
-    bit = 1
-    while bit < count:
-        paired = stacked.reshape((count // (2 * bit), 2, bit) + stacked.shape[1:])
-        flipped = jnp.stack([paired[:, 1], paired[:, 0]], axis=1)
-        stacked = jnp.where((place & bit) != 0, flipped, paired).reshape(stacked.shape)
-        bit *= 2
-    return stacked
 
 
 def packed(weight):
@@ -914,8 +940,7 @@
     head_rows = join_halves(mine, swap(theirs))
     small = devices <= 16
     heads = [partner(head_rows, "dp", 4 * step) for step in (1, 2, 3)] if small else [lax.all_gather(head_rows, "dp", axis=0)]
-    rows_back, logits = stream_call(flat_grad, head_rows, table)
-    logits = logits.reshape(2, half, vocab)
+    rows_back = back_pass(flat_grad, table)
     rows_back, heads = lax.optimization_barrier((rows_back, heads))
     if small:
         heads = jnp.stack([head_rows] + heads)
@@ -941,36 +966,36 @@
     keep_a1, away_a1, attn1, low1, vec1 = backward_a_call(False, flag, [picked_back, mask_row], own, other, saved1)
     came = partner(away_a1, "dp", 1)
     keep_b1, away_b1, middle = backward_b_call(False, flag, [attn1, low1, vec1], own, other, saved1)
-    middle, came, heads = lax.optimization_barrier((middle, came, heads))
+    middle, came, away_b1 = lax.optimization_barrier((middle, came, away_b1))
+    keep_a1, away_a1 = step_y(side_y, keep_a1, came)
+    middle, away_a1 = lax.optimization_barrier((middle, away_a1))
+    came_a1 = partner(away_a1, "dp", 2)
+    came_b1 = partner(away_b1, "dp", 1)
+    packed_a0, attn0, low0, vec0 = backward_a_call(True, flag, [middle], own, other, saved0)
+    attn0, heads, packed_a0, grad_rows = lax.optimization_barrier((attn0, heads, packed_a0, grad_rows))
     if small:
         heads = jnp.concatenate(heads)
         heads = [heads, partner(heads, "dp", 1)]
-    keep_a1, away_a1 = step_y(side_y, keep_a1, came)
-    middle, away_a1 = lax.optimization_barrier((middle, away_a1))
-    came_a = partner(away_a1, "dp", 2)
-    came_b = partner(away_b1, "dp", 1)
-    keep_a0, away_a0, attn0, low0, vec0 = backward_a_call(True, flag, [middle], own, other, saved0)
-    attn0, came_a, came_b, grad_rows = lax.optimization_barrier((attn0, came_a, came_b, grad_rows))
-    parts_a1 = across_z(step_z(me_z, keep_a1, came_a))
-    keep_b1, away_b1 = step_y(side_y, keep_b1, came_b)
-    came_b = partner(away_b1, "dp", 2)
-    came_a = partner(away_a0, "dp", 1)
+    sixteens = [list(range(low, low + 16)) for low in range(0, devices, 16)]
+    part_a0 = spread_on(lax.psum_scatter(packed_a0, "dp", scatter_dimension=0, axis_index_groups=sixteens, tiled=True)[0])
     keep_b0, away_b0, back, slot_grad = backward_b_call(
         True, flag, [attn0, low0, vec0, slot_row, places[None], hat_e, stat_e, embed_vec], own, other, saved0, slots
     )
-    slot_grad, away_b0, parts_a1, came_a, came_b = lax.optimization_barrier((slot_grad, away_b0, parts_a1, came_a, came_b))
-    keep_a0, away_a0 = step_y(side_y, keep_a0, came_a)
-    away_a0, slot_grad, away_b0, keep_b1, parts_a1, heads = lax.optimization_barrier(
-        (away_a0, slot_grad, away_b0, keep_b1, parts_a1, heads)
+    slot_grad, away_b0, keep_a1, came_a1, head_rows, heads = lax.optimization_barrier(
+        (slot_grad, away_b0, keep_a1, came_a1, head_rows, heads)
     )
-    came_a = partner(away_a0, "dp", 2)
-    if small:
-        heads = jnp.concatenate(heads)
-        every_head = exclusive(place, jnp.stack([heads[c * 8 + b * 4 + z] for z in range(4) for b in range(2) for c in range(2)]))
-    else:
-        every_head = heads[0]
-    every_head = every_head.reshape(devices * masks, D)
-    table_back = lax.dot_general(grad_rows, every_head, (((0,), (0,)), ((), ())), preferred_element_type=F32)
+    came_b0 = partner(away_b0, "dp", 1)
+    local_a1 = step_z(me_z, keep_a1, came_a1)
+    parts_a1 = across_z(local_a1)
+    keep_b0, away_b0 = step_y(side_y, keep_b0, came_b0)
+    came_b0 = partner(away_b0, "dp", 2)
+    keep_b1, away_b1 = step_y(side_y, keep_b1, came_b1)
+    came_b1 = partner(away_b1, "dp", 2)
+    logits = logit_pass(head_rows, table)
+    came_b0, came_b1, logits = lax.optimization_barrier((came_b0, came_b1, logits))
+    logits = logits.reshape(2, half, vocab)
+    parts_b0 = across_z(step_z(me_z, keep_b0, came_b0))
+    parts_b1 = across_z(step_z(me_z, keep_b1, came_b1))
 
     sent = exchange(slot_grad.reshape(devices, room, D)).reshape(slots, D)
     crowd_sum = lax.cond(
@@ -979,29 +1004,30 @@
         lambda: jnp.zeros((shard_rows, D), F32),
     )
     names = jnp.where(crowded, -1, asked)
-    partial = owner_call(base, names, sent, table_back + crowd_sum)
-    parts_b1 = across_z(step_z(me_z, keep_b1, came_b))
-    came_b = partner(away_b0, "dp", 1)
-    parts_a0 = across_z(step_z(me_z, keep_a0, came_a))
-    partial, parts_a0 = lax.optimization_barrier((partial, parts_a0))
-    keep_b0, away_b0 = step_y(side_y, keep_b0, came_b)
-    came_b = partner(away_b0, "dp", 2)
-    parts_b0 = across_z(step_z(me_z, keep_b0, came_b))
-
-    def to_all(mine, theirs):
-        chunk = (mine.astype(F32) + theirs.astype(F32)).astype(BF)
+    if small:
+        partial = owner_call(low_place, base, names, sent, grad_rows, heads, crowd_sum)
+    else:
+        one_hot = (names.reshape(1, slots) == (lax.iota(jnp.int32, shard_rows) + base)[:, None]).astype(BF)
+        partial = jnp.dot(one_hot, sent, preferred_element_type=F32) + crowd_sum
+        every_head = heads[0].reshape(devices * masks, D)
+        partial += lax.dot_general(grad_rows, every_head, (((0,), (0,)), ((), ())), preferred_element_type=F32)
+        partial = partial.astype(BF)
+    def to_all(chunk):
         held = jnp.stack([chunk] + [partner(chunk, "dp", 4 * step) for step in (1, 2, 3)])
         held = jnp.concatenate([held, partner(held, "dp", 2)])
         return held, partner(held, "dp", 1)
 
-    mine_a, theirs_a = finish_call(0, flag, low_place, parts_a1, parts_a0)
-    theirs_a = swap(theirs_a)
     mine_b, theirs_b = finish_call(1, flag, low_place, parts_b1, parts_b0)
     theirs_b = swap(theirs_b)
-    partial, theirs_b = lax.optimization_barrier((partial, theirs_b))
+    chunk_b = (mine_b.astype(F32) + theirs_b.astype(F32)).astype(BF)
+    part_a0 = after(part_a0, chunk_b, partial)
+    mine_a, theirs_a = finish_call(0, flag, low_place, parts_a1, [part_a0])
+    theirs_a = swap(theirs_a)
+    chunk_a = (mine_a.astype(F32) + theirs_a.astype(F32)).astype(BF)
+    all_a = lax.all_gather(chunk_a, "dp", axis=0, axis_index_groups=sixteens)
     table_total = partial.astype(F32) + swap(partial).astype(F32)
     shrink_total, expand_total, output_total, query_total, key_total, value_total, vec_total, embed_total, position_total = unpack_call(
-        flag, low_place, *to_all(mine_a, theirs_a), *to_all(mine_b, theirs_b)
+        flag, low_place, all_a, *to_all(chunk_b)
     )
     embed_total = embed_total.reshape(2, D // 2)
     return (

time: 494 us -> 461 us (0.933)
  local copies, waits for them, and re-layouts: 44.7 us -> 25.9 us
  starting transfers between devices: 89.9 us -> 74.7 us
  other arithmetic: 18.8 us -> 13.7 us
    ppermute x39 -> x29, waiting for transfers between devices: 80 us -> 59.1 us  [partner(): return lax.ppermute(values, axis, [(i, i ^ bit) for i in range(size)])]
    unnamed x108 -> x88, local copies, waits for them, and re-layouts: 20.4 us -> 3.12 us
    ppermute x39 -> x29, starting transfers between devices: 43.4 us -> 27.3 us  [partner(): return lax.ppermute(values, axis, [(i, i ^ bit) for i in range(size)])]
    all_gather x0 -> x1, waiting for transfers between devices: none -> 15.8 us  [per_device(): all_a = lax.all_gather(chunk_a, 'dp', axis=0, axis_index_groups=sixteens)]
    pallas_call x6 -> x7, Pallas kernels: 60.5 us -> 71.6 us  [the longest x2 31.2 us: backward_a_call(): pl.pallas_call(functools.partial(bwd_a_kernel, last), out_shape=([jax.Sha...]
    ppermute x11, waiting for transfers between devices: 48.3 us -> 58 us  [swap(): return lax.ppermute(values, 'section', [(0, 1), (1, 0)])]
    pallas_call x4 -> x3, Pallas kernels: 12.3 us -> 8.57 us  [step_y(): pl.pallas_call(step_y_kernel, out_shape=[half, half], in_specs=[SM, VM, V...]
  transfers between devices with their start and end apart: 55 -> 47, of which waited for: 18 -> 18; matrix products, arithmetic and copies ran while one was open for 12% -> 7% of each run, Pallas kernels for 34% -> 37%
where the time goes in v2:
time: 461 us; the launch traced here: 453 us
  Pallas kernels  175 us (38%)
  waiting for transfers between devices  147 us (32%)
  starting transfers between devices  74.7 us (16%)
  local copies, waits for them, and re-layouts  25.9 us (6%)
  between operations  16.4 us (4%)
  other arithmetic  13.7 us (3%)
    ppermute x29, waiting for transfers between devices, partner(): return lax.ppermute(values, axis, [(i, i ^ bit) for i in range(size)])  59.1 us
    ppermute x11, waiting for transfers between devices, swap(): return lax.ppermute(values, 'section', [(0, 1), (1, 0)])  58 us
    pallas_call x1, Pallas kernels, forward_call(): pl.pallas_call(fwd_kernel, out_shape=[jax.ShapeDtypeStruct((masks, D), BF...  37.6 us
    pallas_call x2, Pallas kernels, backward_b_call(): pl.pallas_call(functools.partial(bwd_b_kernel, last), out_shape=out_shape...  37.6 us
    all_to_all x4, starting transfers between devices, exchange(): return lax.all_to_all(values, 'dp', 0, 0, tiled=True)  35.4 us
    pallas_call x2, Pallas kernels, backward_a_call(): pl.pallas_call(functools.partial(bwd_a_kernel, last), out_shape=([jax.Sha...  31.2 us
    ppermute x29, starting transfers between devices, partner(): return lax.ppermute(values, axis, [(i, i ^ bit) for i in range(size)])  27.3 us
    all_gather x1, waiting for transfers between devices, per_device(): all_a = lax.all_gather(chunk_a, 'dp', axis=0, axis_index_groups=sixteens)  15.8 us
  transfers between devices with their start and end apart: 47, of which 18 were waited for; matrix products, arithmetic and copies ran while one was open for 7% of the time, Pallas kernels for 37%

profile of v2, /device:TPU:0, one launch (start us, length us, event | category | flops | bytes accessed | tf_op | source)
XLA Modules:
  0.0 453.2 jit_solution(15868698334428439584)
XLA Ops:
  15.6 7.4 %all-to-all-start.3 = ((s32[16,1,64]{2,1,0:T(1,128)}), s32[16,1,64]{2,1,0:T(1,128)S(1)}, u32[]{:S(2)}, u32[]{:S(2)}) async-start(s32[16,1,64]{2,1,0:T(1,128)} %bitcast.5), calls=%async_computation.3 | async-start | bytes 16384 | tf_op jit(solution)/shard_map/all_to_all | solution.py:874
  23.0 6.4 %all-to-all-done.3 = s32[16,1,64]{2,1,0:T(1,128)S(1)} async-done(((s32[16,1,64]{2,1,0:T(1,128)}), s32[16,1,64]{2,1,0:T(1,128)S(1)}, u32[]{:S(2)}, u32[]{:S(2)}) %all-to-all-start.3) | async-done | bytes 4128 | tf_op jit(solution)/shard_map/all_to_all | solution.py:874
  56.6 7.0 %collective-permute-done.3.rest_7_.rest_9_.rest_8_.rest_12_ = bf16[384,768]{1,0:T(8,128)(2,1)} collective-permute-done((bf16[384,768]{1,0:T(8,128)(2,1)}, bf16[384,768]{1,0:T(8,128)(2,1)}, u32[]{:S(2)}, u32[]{:S(2)}) %collective-permute-start.3) | collective-permute-done | bytes 589856 | tf_op jit(solution)/shard_map/ppermute | solution.py:866
  63.6 12.6 %collective-permute-done.1.rest_5_.rest_7_.rest_6_.rest_10_ = bf16[384,768]{1,0:T(8,128)(2,1)} collective-permute-done((bf16[384,768]{1,0:T(8,128)(2,1)S(1)}, bf16[384,768]{1,0:T(8,128)(2,1)}, u32[]{:S(2)}, u32[]{:S(2)}) %collective-permute-start.1) | collective-permute-done | bytes 589856 | tf_op jit(solution)/shard_map/ppermute | solution.py:866
  76.2 12.6 %collective-permute-done.2.rest_6_.rest_8_.rest_7_.rest_11_ = bf16[384,768]{1,0:T(8,128)(2,1)} collective-permute-done((bf16[384,768]{1,0:T(8,128)(2,1)S(1)}, bf16[384,768]{1,0:T(8,128)(2,1)}, u32[]{:S(2)}, u32[]{:S(2)}) %collective-permute-start.2) | collective-permute-done | bytes 589856 | tf_op jit(solution)/shard_map/ppermute | solution.py:866
  101.5 37.6 %forward_layers.1 = (bf16[80,768]{1,0:T(8,128)(2,1)}, bf16[512,768]{1,0:T(8,128)(2,1)}, bf16[512,768]{1,0:T(8,128)(2,1)}, bf16[512,768]{1,0:T(8,128)(2,1)}, bf16...) custom-call(s32[3]{0:T(128)} %pad_add_fusion.1.flag, ...), custom_call_target="tpu_custom_call" | custom-call | flops 35999997952 | bytes 62914560 | tf_op jit(solution)/shard_map/forward_layers/pallas_call | solution.py:286
  148.8 7.2 %all-gather.4.cloned.1.call-done.table_ref = bf16[15360,768]{1,0:T(8,128)(2,1)} async-done(((bf16[960,768]{1,0:T(8,128)(2,1)}), bf16[15360,768]{1,0:T(8,128)(2,1)}) %all-gather.4.cloned.1.call-update) | async-done | bytes 23592976 | tf_op jit(solution)/shard_map/all_gather | solution.py:877
  156.0 13.7 %table_back_pass.1 = f32[80,768]{1,0:T(8,128)} custom-call(bf16[80,15360]{1,0:T(8,128)(2,1)} %bitcast.78, bf16[15360,768]{1,0:T(8,128)(2,1)} %all-gather.4.cloned.1.call-done.table_ref), custom_call_target="tpu_custom_call" | custom-call | flops 10000000000 | bytes 20971520 | tf_op jit(solution)/shard_map/table_back_pass/pallas_call | solution.py:742
  170.4 17.3 %all-to-all-start.5 = ((bf16[16,80,960]{2,1,0:T(8,128)(2,1)}), bf16[16,80,960]{2,1,0:T(8,128)(2,1)S(1)}, u32[]{:S(2)}, u32[]{:S(2)}) async-start(bf16[16,80,960]{2,1,0:T(8,128)(2,1)} %bitcast.74), calls=%async_computation.5 | async-start | bytes 5242880 | tf_op jit(solution)/shard_map/all_to_all | solution.py:874
  193.0 15.5 %backward_second_a.1 = (bf16[8,144,768]{2,1,0:T(8,128)(2,1)}, bf16[8,144,768]{2,1,0:T(8,128)(2,1)}, f32[512,768]{1,0:T(8,128)}, bf16[512,768]{1,0:T(8,128)(2,1)}, f32[16,768]{1,0:T(8,128)}) custom-call(s32[3]{0:T(128)} %pad_add_fusion.1.flag, bf16[80,768]{1,0:T(8,128)(2,1)} %fusion.1.rest_0_, s32[1,80]{1,0:T(1,128)} %broadcast_select_fusion.5.rest_1_, ...), custom_call_target="tpu_custom_call" | custom-call | flops 12000000000 | bytes 20971520 | tf_op jit(solution)/shard_map/backward_second_a/pallas_call | solution.py:420
  210.6 17.5 %backward_second_b.1 = (bf16[8,48,768]{2,1,0:T(8,128)(2,1)}, bf16[8,48,768]{2,1,0:T(8,128)(2,1)}, bf16[512,768]{1,0:T(8,128)(2,1)}) custom-call(s32[3]{0:T(128)} %pad_add_fusion.1.flag, f32[512,768]{1,0:T(8,128)} %get-tuple-element.161.attn_in, bf16[512,768]{1,0:T(8,128)(2,1)} %get-tuple-element.162.back_low, f32[16,768]{1,0:T(8,128)} %get-tuple-element.163.vec_in, ...), custom_call_target="tpu_custom_call" | custom-call | flops 15000000512 | bytes 20971520 | tf_op jit(solution)/shard_map/backward_second_b/pallas_call | solution.py:556
  231.7 15.6 %backward_first_a.1 = (bf16[16,144,768]{2,1,0:T(8,128)(2,1)}, f32[512,768]{1,0:T(8,128)}, bf16[512,768]{1,0:T(8,128)(2,1)}, f32[16,768]{1,0:T(8,128)}) custom-call(s32[3]{0:T(128)} %pad_add_fusion.1.flag, bf16[512,768]{1,0:T(8,128)(2,1)} %get-tuple-element.178.rest_0_, bf16[768,768]{1,0:T(8,128)(2,1)} %bitcast.92, bf16[768,768]{1,0:T(8,128)(2,1)} %bitcast.98, ...), custom_call_target="tpu_custom_call" | custom-call | flops 12000000000 | bytes 20971520 | tf_op jit(solution)/shard_map/backward_first_a/pallas_call | solution.py:420
  251.1 20.1 %backward_first_b.1 = (bf16[8,80,768]{2,1,0:T(8,128)(2,1)}, bf16[8,80,768]{2,1,0:T(8,128)(2,1)}, bf16[512,768]{1,0:T(8,128)(2,1)}, bf16[768,768]{1,0:T(8,128)(2,1)}) custom-call(s32[3]{0:T(128)} %pad_add_fusion.1.flag, f32[512,768]{1,0:T(8,128)} %get-tuple-element.193.attn_in, bf16[512,768]{1,0:T(8,128)(2,1)} %get-tuple-element.194.back_low, ...), custom_call_target="tpu_custom_call" | custom-call | flops 15000000512 | bytes 20971520 | tf_op jit(solution)/shard_map/backward_first_b/pallas_call | solution.py:556
  285.1 15.4 %table_logit_pass.1 = bf16[80,15360]{1,0:T(8,128)(2,1)} custom-call(bf16[80,768]{1,0:T(8,128)(2,1)} %copy-done.15, bf16[15360,768]{1,0:T(8,128)(2,1)} %all-gather.4.cloned.1.call-done.table_ref), custom_call_target="tpu_custom_call" | custom-call | flops 10000000000 | bytes 20971520 | tf_op jit(solution)/shard_map/table_logit_pass/pallas_call | solution.py:761
  300.5 6.0 %collective-permute-done.22.came_ref = bf16[4,48,768]{2,1,0:T(8,128)(2,1)S(1)} collective-permute-done((bf16[4,48,768]{2,1,0:T(8,128)(2,1)}, bf16[4,48,768]{2,1,0:T(8,128)(2,1)S(1)}, u32[]{:S(2)}, u32[]{:S(2)}) %collective-permute-start.22) | collective-permute-done | bytes 294944 | tf_op jit(solution)/shard_map/ppermute | solution.py:822
  306.5 13.5 %collective-permute-done.20.came_ref = bf16[4,80,768]{2,1,0:T(8,128)(2,1)S(1)} collective-permute-done((bf16[4,80,768]{2,1,0:T(8,128)(2,1)}, bf16[4,80,768]{2,1,0:T(8,128)(2,1)S(1)}, u32[]{:S(2)}, u32[]{:S(2)}) %collective-permute-start.20) | collective-permute-done | bytes 491552 | tf_op jit(solution)/shard_map/ppermute | solution.py:822
  332.4 18.2 %collective-permute-done.28.refs_2_ = bf16[48,768]{1,0:T(8,128)(2,1)} collective-permute-done((bf16[48,768]{1,0:T(8,128)(2,1)S(1)}, bf16[48,768]{1,0:T(8,128)(2,1)}, u32[]{:S(2)}, u32[]{:S(2)}) %collective-permute-start.28) | collective-permute-done | bytes 73760 | tf_op jit(solution)/shard_map/ppermute | solution.py:822
  363.2 7.1 %owner_sum.1 = bf16[960,768]{1,0:T(8,128)(2,1)} custom-call(s32[1]{0:T(128)} %bitcast.43.place_ref, s32[1]{0:T(128)} %bitcast.8.base_ref, s32[1,768]{1,0:T(1,128)} %select_n.201.ids_ref, bf16[768,768]{1,0:T(8,128)(2,1)} %bitcast.45.rows_ref, bf16[1280,960]{1,0:T(8,128)(2,1)} %bitcast.77, bf16[8,80,768]{2,1,0:T(8,128)(2,1)} %constant_dynamic-update-slice_fusion.3.heads_own, ...), custom_call_target="tpu_custom_call" | custom-call | flops 6000000000 | bytes 20971520 | tf_op jit(solution)/shard_map/owner_sum/pallas_call | solution.py:787
  370.3 8.3 %collective-permute-done.25.refs_2_ = bf16[144,768]{1,0:T(8,128)(2,1)} collective-permute-done((bf16[144,768]{1,0:T(8,128)(2,1)}, bf16[144,768]{1,0:T(8,128)(2,1)}, u32[]{:S(2)}, u32[]{:S(2)}) %collective-permute-start.25) | collective-permute-done | bytes 221216 | tf_op jit(solution)/shard_map/ppermute | solution.py:822
  381.3 6.8 %collective-permute-done.34 = bf16[144,768]{1,0:T(8,128)(2,1)S(1)} collective-permute-done((bf16[144,768]{1,0:T(8,128)(2,1)}, bf16[144,768]{1,0:T(8,128)(2,1)S(1)}, u32[]{:S(2)}, u32[]{:S(2)}) %collective-permute-start.34) | collective-permute-done | bytes 221216 | tf_op jit(solution)/shard_map/ppermute | solution.py:866
  400.1 7.8 %collective-permute-done.38 = bf16[4,64,768]{2,1,0:T(8,128)(2,1)S(1)} collective-permute-done((bf16[4,64,768]{2,1,0:T(8,128)(2,1)S(1)}, bf16[4,64,768]{2,1,0:T(8,128)(2,1)S(1)}, u32[]{:S(2)}, u32[]{:S(2)}) %collective-permute-start.38) | collective-permute-done | bytes 393248 | tf_op jit(solution)/shard_map/ppermute | solution.py:822
  407.9 10.7 %collective-permute-done.23 = bf16[960,768]{1,0:T(8,128)(2,1)S(1)} collective-permute-done((bf16[960,768]{1,0:T(8,128)(2,1)S(1)}, bf16[960,768]{1,0:T(8,128)(2,1)S(1)}, u32[]{:S(2)}, u32[]{:S(2)}) %collective-permute-start.23) | collective-permute-done | bytes 1474592 | tf_op jit(solution)/shard_map/ppermute | solution.py:866
  420.6 15.8 %all-gather.6.cloned.1.call-done = bf16[2304,768]{1,0:T(8,128)(2,1)} async-done(((bf16[144,768]{1,0:T(8,128)(2,1)}), bf16[2304,768]{1,0:T(8,128)(2,1)}) %all-gather.6.cloned.1.call-update) | async-done | bytes 3538960 | tf_op jit(solution)/shard_map/all_gather | solution.py:1027
  436.4 7.0 %unpack_sums.1 = (f32[768,768]{1,0:T(8,128)}, f32[768,768]{1,0:T(8,128)}, f32[768,768]{1,0:T(8,128)}, f32[4,192,192]{2,1,0:T(8,128)}, f32[4,192,192]{2,1,0:T(8,1...) custom-call(s32[3]{0:T(128)} %pad_add_fusion.1.flag, ...), custom_call_target="tpu_custom_call" | custom-call | flops 1000000000 | bytes 16777216 | tf_op jit(solution)/shard_map/unpack_sums/pallas_call | solution.py:666
  (241 shorter events, 129.9 us)
Async XLA Ops:
  7.2 148.8 %all-gather.4.cloned.1.call-start = ((), (), s32[]{:S(2)}) async-start(), calls=%async_computation.8 | async-start | bytes 25067520 | tf_op jit(solution)/shard_map/all_gather | solution.py:877
  39.8 61.0 %all-to-all-start.4 = ((bf16[16,48,768]{2,1,0:T(8,128)(2,1)}), bf16[16,48,768]{2,1,0:T(8,128)(2,1)}, u32[]{:S(2)}, u32[]{:S(2)}) async-start(bf16[16,48,768]{2,1,0:T(8,128)(2,1)} %bitcast.13), calls=%async_computation.4 | async-start | bytes 2359296 | tf_op jit(solution)/shard_map/all_to_all | solution.py:874
  44.6 56.1 %collective-permute-start.9 = (f32[8,768]{1,0:T(8,128)S(1)}, f32[8,768]{1,0:T(8,128)S(1)}, u32[]{:S(2)}, u32[]{:S(2)}) collective-permute-start(f32[8,768]{1,0:T(8,128)S(1)} %concatenate.52.rest_4_.rest_6_.rest_5_.rest_9_), channel_id=1, source_target_pairs={{0,16},{16,0},{1,17},{17,1},{2,18},{18,2},{3,19},{19,3},{4,20},{20... | collective-permute-start | bytes 73736 | tf_op jit(solution)/shard_map/ppermute | solution.py:866
  48.7 27.5 %collective-permute-start.1 = (bf16[384,768]{1,0:T(8,128)(2,1)S(1)}, bf16[384,768]{1,0:T(8,128)(2,1)}, u32[]{:S(2)}, u32[]{:S(2)}) collective-permute-start(bf16[384,768]{1,0:T(8,128)(2,1)S(1)} %constant_dynamic-slice_fusion.2), channel_id=1, source_target_pairs={{0,16},{16,0},{1,17},{17,1},{2,18},{18,2},{3,19},{19,3},{4,20},{20... | collective-permute-start | bytes 1769480 | tf_op jit(solution)/shard_map/ppermute | solution.py:866
  51.4 37.4 %collective-permute-start.2 = (bf16[384,768]{1,0:T(8,128)(2,1)S(1)}, bf16[384,768]{1,0:T(8,128)(2,1)}, u32[]{:S(2)}, u32[]{:S(2)}) collective-permute-start(bf16[384,768]{1,0:T(8,128)(2,1)S(1)} %constant_dynamic-slice_fusion.1), channel_id=1, source_target_pairs={{0,16},{16,0},{1,17},{17,1},{2,18},{18,2},{3,19},{19,3},{4,20},{20... | collective-permute-start | bytes 1769480 | tf_op jit(solution)/shard_map/ppermute | solution.py:866
  55.0 43.3 %collective-permute-start.4 = (bf16[288,768]{1,0:T(8,128)(2,1)}, bf16[288,768]{1,0:T(8,128)(2,1)}, u32[]{:S(2)}, u32[]{:S(2)}) collective-permute-start(bf16[288,768]{1,0:T(8,128)(2,1)} %constant_dynamic-slice_fusion), channel_id=1, source_target_pairs={{0,16},{16,0},{1,17},{17,1},{2,18},{18,2},{3,19},{19,3},{4,20},{20... | collective-permute-start | bytes 1327112 | tf_op jit(solution)/shard_map/ppermute | solution.py:866
  63.6 37.2 %collective-permute-start.7 = (bf16[384,768]{1,0:T(8,128)(2,1)}, bf16[384,768]{1,0:T(8,128)(2,1)}, u32[]{:S(2)}, u32[]{:S(2)}) collective-permute-start(bf16[384,768]{1,0:T(8,128)(2,1)} %collective-permute-done.3.rest_7_.rest_9_.rest_8_.rest_12_), channel_id=1, source_target_pairs={{0,1},{1,0},{2,3},{3,2},{4,5},{5,4},{6,7},{7,6},{8,9},{9,8},{10,11... | collective-permute-start | bytes 1769480 | tf_op jit(solution)/shard_map/ppermute | solution.py:822
  76.2 24.6 %collective-permute-start.5 = (bf16[384,768]{1,0:T(8,128)(2,1)}, bf16[384,768]{1,0:T(8,128)(2,1)}, u32[]{:S(2)}, u32[]{:S(2)}) collective-permute-start(bf16[384,768]{1,0:T(8,128)(2,1)} %collective-permute-done.1.rest_5_.rest_7_.rest_6_.rest_10_), channel_id=1, source_target_pairs={{0,1},{1,0},{2,3},{3,2},{4,5},{5,4},{6,7},{7,6},{8,9},{9,8},{10,11... | collective-permute-start | bytes 1769480 | tf_op jit(solution)/shard_map/ppermute | solution.py:822
  144.4 25.3 %collective-permute-start.13 = (bf16[80,768]{1,0:T(8,128)(2,1)S(1)}, bf16[80,768]{1,0:T(8,128)(2,1)S(1)}, u32[]{:S(2)}, u32[]{:S(2)}) collective-permute-start(bf16[80,768]{1,0:T(8,128)(2,1)S(1)} %maximum_select_fusion.1.head_ref), channel_id=1, source_target_pairs={{0,12},{1,13},{2,14},{3,15},{4,8},{5,9},{6,10},{7,11},{8,4},{9,5},... | collective-permute-start | bytes 368648 | tf_op jit(solution)/shard_map/ppermute | solution.py:822
  148.1 21.6 %collective-permute-start.12 = (bf16[80,768]{1,0:T(8,128)(2,1)S(1)}, bf16[80,768]{1,0:T(8,128)(2,1)S(1)}, u32[]{:S(2)}, u32[]{:S(2)}) collective-permute-start(bf16[80,768]{1,0:T(8,128)(2,1)S(1)} %maximum_select_fusion.1.head_ref), channel_id=1, source_target_pairs={{0,8},{1,9},{2,10},{3,11},{4,12},{5,13},{6,14},{7,15},{8,0},{9,1},... | collective-permute-start | bytes 368648 | tf_op jit(solution)/shard_map/ppermute | solution.py:822
  148.1 21.6 %collective-permute-start.11 = (bf16[80,768]{1,0:T(8,128)(2,1)S(1)}, bf16[80,768]{1,0:T(8,128)(2,1)S(1)}, u32[]{:S(2)}, u32[]{:S(2)}) collective-permute-start(bf16[80,768]{1,0:T(8,128)(2,1)S(1)} %maximum_select_fusion.1.head_ref), channel_id=1, source_target_pairs={{0,4},{1,5},{2,6},{3,7},{4,0},{5,1},{6,2},{7,3},{8,12},{9,13},{10,... | collective-permute-start | bytes 368648 | tf_op jit(solution)/shard_map/ppermute | solution.py:822
  170.4 77.0 %all-to-all-start.5 = ((bf16[16,80,960]{2,1,0:T(8,128)(2,1)}), bf16[16,80,960]{2,1,0:T(8,128)(2,1)S(1)}, u32[]{:S(2)}, u32[]{:S(2)}) async-start(bf16[16,80,960]{2,1,0:T(8,128)(2,1)} %bitcast.74), calls=%async_computation.5 | async-start | bytes 5242880 | tf_op jit(solution)/shard_map/all_to_all | solution.py:874
  187.7 182.6 %reduce-scatter.2.cloned.1.call-start = ((), (), s32[]{:S(2)}) async-start(), calls=%async_computation.9 | async-start | bytes 3760128 | tf_op jit(solution)/shard_map/reduce_scatter | solution.py:980
  208.8 38.6 %collective-permute-start.16 = (bf16[4,80,768]{2,1,0:T(8,128)(2,1)S(1)}, bf16[4,80,768]{2,1,0:T(8,128)(2,1)}, u32[]{:S(2)}, u32[]{:S(2)}) collective-permute-start(bf16[4,80,768]{2,1,0:T(8,128)(2,1)S(1)} %pad_maximum_fusion), channel_id=1, source_target_pairs={{0,2},{1,3},{2,0},{3,1},{4,6},{5,7},{6,4},{7,5},{8,10},{9,11},{10,... | collective-permute-start | bytes 1474568 | tf_op jit(solution)/shard_map/ppermute | solution.py:822
  248.1 23.2 %collective-permute-start.17 = (bf16[4,144,768]{2,1,0:T(8,128)(2,1)}, bf16[4,144,768]{2,1,0:T(8,128)(2,1)}, u32[]{:S(2)}, u32[]{:S(2)}) collective-permute-start(bf16[4,144,768]{2,1,0:T(8,128)(2,1)} %get-tuple-element.210), channel_id=1, source_target_pairs={{0,2},{1,3},{2,0},{3,1},{4,6},{5,7},{6,4},{7,5},{8,10},{9,11},{10,... | collective-permute-start | bytes 2654216 | tf_op jit(solution)/shard_map/ppermute | solution.py:822
  272.0 91.1 %all-to-all-start.6 = ((bf16[16,48,768]{2,1,0:T(8,128)(2,1)}), bf16[16,48,768]{2,1,0:T(8,128)(2,1)}, u32[]{:S(2)}, u32[]{:S(2)}) async-start(bf16[16,48,768]{2,1,0:T(8,128)(2,1)} %bitcast.79), calls=%async_computation.6 | async-start | bytes 2359296 | tf_op jit(solution)/shard_map/all_to_all | solution.py:874
  278.0 158.4 %all-gather.6.cloned.1.call-start = ((), (), s32[]{:S(2)}) async-start(), calls=%async_computation.10 | async-start | bytes 3760128 | tf_op jit(solution)/shard_map/all_gather | solution.py:1027
  280.4 26.1 %collective-permute-start.22 = (bf16[4,48,768]{2,1,0:T(8,128)(2,1)}, bf16[4,48,768]{2,1,0:T(8,128)(2,1)S(1)}, u32[]{:S(2)}, u32[]{:S(2)}) collective-permute-start(bf16[4,48,768]{2,1,0:T(8,128)(2,1)} %get-tuple-element.217), channel_id=1, source_target_pairs={{0,2},{1,3},{2,0},{3,1},{4,6},{5,7},{6,4},{7,5},{8,10},{9,11},{10,... | collective-permute-start | bytes 884744 | tf_op jit(solution)/shard_map/ppermute | solution.py:822
  285.0 35.1 %collective-permute-start.20 = (bf16[4,80,768]{2,1,0:T(8,128)(2,1)}, bf16[4,80,768]{2,1,0:T(8,128)(2,1)S(1)}, u32[]{:S(2)}, u32[]{:S(2)}) collective-permute-start(bf16[4,80,768]{2,1,0:T(8,128)(2,1)} %get-tuple-element.214), channel_id=1, source_target_pairs={{0,2},{1,3},{2,0},{3,1},{4,6},{5,7},{6,4},{7,5},{8,10},{9,11},{10,... | collective-permute-start | bytes 1474568 | tf_op jit(solution)/shard_map/ppermute | solution.py:822
  325.2 25.4 %collective-permute-start.30 = (bf16[80,768]{1,0:T(8,128)(2,1)}, bf16[80,768]{1,0:T(8,128)(2,1)S(1)}, u32[]{:S(2)}, u32[]{:S(2)}) collective-permute-start(bf16[80,768]{1,0:T(8,128)(2,1)} %get-tuple-element.241), channel_id=1, source_target_pairs={{0,4},{1,5},{2,6},{3,7},{4,0},{5,1},{6,2},{7,3},{8,12},{9,13},{10,... | collective-permute-start | bytes 368648 | tf_op jit(solution)/shard_map/ppermute | solution.py:822
  326.2 24.4 %collective-permute-start.31 = (bf16[80,768]{1,0:T(8,128)(2,1)}, bf16[80,768]{1,0:T(8,128)(2,1)S(1)}, u32[]{:S(2)}, u32[]{:S(2)}) collective-permute-start(bf16[80,768]{1,0:T(8,128)(2,1)} %get-tuple-element.242), channel_id=1, source_target_pairs={{0,8},{1,9},{2,10},{3,11},{4,12},{5,13},{6,14},{7,15},{8,0},{9,1},... | collective-permute-start | bytes 368648 | tf_op jit(solution)/shard_map/ppermute | solution.py:822
  327.9 22.7 %collective-permute-start.32 = (bf16[80,768]{1,0:T(8,128)(2,1)}, bf16[80,768]{1,0:T(8,128)(2,1)S(1)}, u32[]{:S(2)}, u32[]{:S(2)}) collective-permute-start(bf16[80,768]{1,0:T(8,128)(2,1)} %get-tuple-element.243), channel_id=1, source_target_pairs={{0,12},{1,13},{2,14},{3,15},{4,8},{5,9},{6,10},{7,11},{8,4},{9,5},... | collective-permute-start | bytes 368648 | tf_op jit(solution)/shard_map/ppermute | solution.py:822
  329.6 21.0 %collective-permute-start.28 = (bf16[48,768]{1,0:T(8,128)(2,1)S(1)}, bf16[48,768]{1,0:T(8,128)(2,1)}, u32[]{:S(2)}, u32[]{:S(2)}) collective-permute-start(bf16[48,768]{1,0:T(8,128)(2,1)S(1)} %copy-done.39), channel_id=1, source_target_pairs={{0,8},{1,9},{2,10},{3,11},{4,12},{5,13},{6,14},{7,15},{8,0},{9,1},... | collective-permute-start | bytes 221192 | tf_op jit(solution)/shard_map/ppermute | solution.py:822
  389.8 28.8 %collective-permute-start.23 = (bf16[960,768]{1,0:T(8,128)(2,1)S(1)}, bf16[960,768]{1,0:T(8,128)(2,1)S(1)}, u32[]{:S(2)}, u32[]{:S(2)}) collective-permute-start(bf16[960,768]{1,0:T(8,128)(2,1)S(1)} %copy-done.3), channel_id=1, source_target_pairs={{0,16},{16,0},{1,17},{17,1},{2,18},{18,2},{3,19},{19,3},{4,20},{20... | collective-permute-start | bytes 4423688 | tf_op jit(solution)/shard_map/ppermute | solution.py:866
  (64 other events, 761.5 us)
Sparse Core Ops, SparseCore 0:
  9.6 146.3 all-gather.3
  247.5 100.0 reduce-scatter.1
  389.9 46.4 all-gather.5

commit v3 on v2

--- a/solution.py
+++ b/solution.py
@@ -336,7 +336,7 @@
         picked_back, mask_row = take(2)
     own, other = take(5), take(9)
     sources = take(7)
-    packed_out = take(1 if last else 2)
+    packed_out = take(2 if last else 1)
     attn_ref, back_low, vec_ref = take(3)
     weights = take(4)
     mid_ref, low_ref, packed_ref = take(3)
@@ -396,7 +396,7 @@
         mid_ref[:, lanes(g)] += mm_nt(expand_in, expand[g])
         for part in range(CHUNKS // GROUPS):
             chunk = g * (CHUNKS // GROUPS) + part
-            at = chunk_place(chunk, core, last)
+            at = chunk_place(chunk, core, not last)
             packed_ref[at, 0:each, :] = shrink_grad[part * each : (part + 1) * each, :]
             packed_ref[at, each : 2 * each, :] = expand_grad[part * each : (part + 1) * each, :]
     copies[1].wait()
@@ -408,7 +408,7 @@
     attn_ref[...] = attn_back
     attended_in = attn_back.astype(BF)
     copies[0].wait()
-    put_chunks(packed_ref, core, last, mm_tn(mix_ref[...], attended_in), each, 2 * each)
+    put_chunks(packed_ref, core, not last, mm_tn(mix_ref[...], attended_in), each, 2 * each)
     ship = ship_chunks(packed_ref, packed_out, sem_o)
     back_low[...] = mm_nt(attended_in, output[...]).astype(BF)
     for c in ship:
@@ -419,12 +419,12 @@
     chosen = (5, 6, 7, 8, 9, 10, 13)
     return pl.pallas_call(
         functools.partial(bwd_a_kernel, last),
-        out_shape=([jax.ShapeDtypeStruct((CHUNKS, ROWS_A, D), BF)] if last else [jax.ShapeDtypeStruct((CHUNKS // 2, ROWS_A, D), BF)] * 2)
+        out_shape=([jax.ShapeDtypeStruct((CHUNKS // 2, ROWS_A, D), BF)] * 2 if last else [jax.ShapeDtypeStruct((CHUNKS, ROWS_A, D), BF)])
         + [
             jax.ShapeDtypeStruct((N, D), F32), jax.ShapeDtypeStruct((N, D), BF), jax.ShapeDtypeStruct((16, D), F32),
         ],
         in_specs=[SM] + [VM] * len(extra) + [HB] * (14 + len(chosen)),
-        out_specs=[HB] * (1 if last else 2) + [VM, VM, VM],
+        out_specs=[HB] * (2 if last else 1) + [VM, VM, VM],
         scratch_shapes=[
             pltpu.VMEM((GROUPS, 256, D), BF), pltpu.VMEM((GROUPS, 256, D), BF), pltpu.VMEM((D, D), BF), pltpu.VMEM((8, D), F32),
             pltpu.VMEM((N, D), F32), pltpu.VMEM((N, D), BF), pltpu.VMEM((CHUNKS, ROWS_A, D), BF),
@@ -963,39 +963,44 @@
     def across_z(parts):
         return [spread_on(parts[0])] + [partner(spread_on(parts[step]), "dp", 4 * step) for step in (1, 2, 3)]
 
-    keep_a1, away_a1, attn1, low1, vec1 = backward_a_call(False, flag, [picked_back, mask_row], own, other, saved1)
-    came = partner(away_a1, "dp", 1)
+    sixteens = [list(range(low, low + 16)) for low in range(0, devices, 16)]
+
+    def sum_to_owner(packed):
+        return spread_on(lax.psum_scatter(packed, "dp", scatter_dimension=0, axis_index_groups=sixteens, tiled=True)[0])
+
+    packed_a1, attn1, low1, vec1 = backward_a_call(False, flag, [picked_back, mask_row], own, other, saved1)
+    part_a1 = sum_to_owner(packed_a1)
     keep_b1, away_b1, middle = backward_b_call(False, flag, [attn1, low1, vec1], own, other, saved1)
-    middle, came, away_b1 = lax.optimization_barrier((middle, came, away_b1))
-    keep_a1, away_a1 = step_y(side_y, keep_a1, came)
-    middle, away_a1 = lax.optimization_barrier((middle, away_a1))
-    came_a1 = partner(away_a1, "dp", 2)
+    middle, away_b1 = lax.optimization_barrier((middle, away_b1))
     came_b1 = partner(away_b1, "dp", 1)
-    packed_a0, attn0, low0, vec0 = backward_a_call(True, flag, [middle], own, other, saved0)
-    attn0, heads, packed_a0, grad_rows = lax.optimization_barrier((attn0, heads, packed_a0, grad_rows))
+    keep_a0, away_a0, attn0, low0, vec0 = backward_a_call(True, flag, [middle], own, other, saved0)
+    attn0, heads, away_a0, grad_rows = lax.optimization_barrier((attn0, heads, away_a0, grad_rows))
     if small:
         heads = jnp.concatenate(heads)
         heads = [heads, partner(heads, "dp", 1)]
-    sixteens = [list(range(low, low + 16)) for low in range(0, devices, 16)]
-    part_a0 = spread_on(lax.psum_scatter(packed_a0, "dp", scatter_dimension=0, axis_index_groups=sixteens, tiled=True)[0])
+    came_a0 = partner(away_a0, "dp", 1)
     keep_b0, away_b0, back, slot_grad = backward_b_call(
         True, flag, [attn0, low0, vec0, slot_row, places[None], hat_e, stat_e, embed_vec], own, other, saved0, slots
     )
-    slot_grad, away_b0, keep_a1, came_a1, head_rows, heads = lax.optimization_barrier(
-        (slot_grad, away_b0, keep_a1, came_a1, head_rows, heads)
+    slot_grad, away_b0, came_a0, came_b1, heads = lax.optimization_barrier((slot_grad, away_b0, came_a0, came_b1, heads))
+    keep_a0, away_a0 = step_y(side_y, keep_a0, came_a0)
+    away_a0, away_b0, head_rows, slot_grad, keep_b1, came_b1 = lax.optimization_barrier(
+        (away_a0, away_b0, head_rows, slot_grad, keep_b1, came_b1)
     )
+    came_a0 = partner(away_a0, "dp", 2)
     came_b0 = partner(away_b0, "dp", 1)
-    local_a1 = step_z(me_z, keep_a1, came_a1)
-    parts_a1 = across_z(local_a1)
-    keep_b0, away_b0 = step_y(side_y, keep_b0, came_b0)
-    came_b0 = partner(away_b0, "dp", 2)
+    logits = logit_pass(head_rows, table)
     keep_b1, away_b1 = step_y(side_y, keep_b1, came_b1)
     came_b1 = partner(away_b1, "dp", 2)
-    logits = logit_pass(head_rows, table)
-    came_b0, came_b1, logits = lax.optimization_barrier((came_b0, came_b1, logits))
+    keep_b0, away_b0 = step_y(side_y, keep_b0, came_b0)
+    came_a0, logits, away_b0, came_b1 = lax.optimization_barrier((came_a0, logits, away_b0, came_b1))
     logits = logits.reshape(2, half, vocab)
-    parts_b0 = across_z(step_z(me_z, keep_b0, came_b0))
-    parts_b1 = across_z(step_z(me_z, keep_b1, came_b1))
+    local_a0 = step_z(me_z, keep_a0, came_a0)
+    local_a0, away_b0, keep_b1 = lax.optimization_barrier((local_a0, away_b0, keep_b1))
+    parts_a0 = across_z(local_a0)
+    came_b0 = partner(away_b0, "dp", 2)
+    local_b1 = step_z(me_z, keep_b1, came_b1)
+    local_b0 = step_z(me_z, keep_b0, came_b0)
 
     sent = exchange(slot_grad.reshape(devices, room, D)).reshape(slots, D)
     crowd_sum = lax.cond(
@@ -1012,22 +1017,26 @@
         every_head = heads[0].reshape(devices * masks, D)
         partial += lax.dot_general(grad_rows, every_head, (((0,), (0,)), ((), ())), preferred_element_type=F32)
         partial = partial.astype(BF)
-    def to_all(chunk):
+    def to_all(chunk, earlier):
         held = jnp.stack([chunk] + [partner(chunk, "dp", 4 * step) for step in (1, 2, 3)])
+        held = after(held, earlier)
         held = jnp.concatenate([held, partner(held, "dp", 2)])
         return held, partner(held, "dp", 1)
 
+    parts_a0, local_b0, local_b1, partial = lax.optimization_barrier((parts_a0, local_b0, local_b1, partial))
+    parts_b0 = across_z(local_b0)
+    parts_b1 = across_z(local_b1)
     mine_b, theirs_b = finish_call(1, flag, low_place, parts_b1, parts_b0)
     theirs_b = swap(theirs_b)
     chunk_b = (mine_b.astype(F32) + theirs_b.astype(F32)).astype(BF)
-    part_a0 = after(part_a0, chunk_b, partial)
-    mine_a, theirs_a = finish_call(0, flag, low_place, parts_a1, [part_a0])
+    mine_a, theirs_a = finish_call(0, flag, low_place, [part_a1], parts_a0)
     theirs_a = swap(theirs_a)
     chunk_a = (mine_a.astype(F32) + theirs_a.astype(F32)).astype(BF)
     all_a = lax.all_gather(chunk_a, "dp", axis=0, axis_index_groups=sixteens)
-    table_total = partial.astype(F32) + swap(partial).astype(F32)
+    swapped = swap(partial)
+    table_total = partial.astype(F32) + swapped.astype(F32)
     shrink_total, expand_total, output_total, query_total, key_total, value_total, vec_total, embed_total, position_total = unpack_call(
-        flag, low_place, all_a, *to_all(chunk_b)
+        flag, low_place, all_a, *to_all(chunk_b, swapped)
     )
     embed_total = embed_total.reshape(2, D // 2)
     return (

time: 461 us -> 455 us (0.987)
  waiting for transfers between devices: 147 us -> 124 us
  starting transfers between devices: 74.7 us -> 87.4 us
    all_gather x1, waiting for transfers between devices: 15.8 us -> 0.02 us  [per_device(): all_a = lax.all_gather(chunk_a, 'dp', axis=0, axis_index_groups=sixteens)]
    ppermute x11, waiting for transfers between devices: 58 us -> 49 us  [swap(): return lax.ppermute(values, 'section', [(0, 1), (1, 0)])]
    ppermute x29, starting transfers between devices: 27.3 us -> 35.4 us  [partner(): return lax.ppermute(values, axis, [(i, i ^ bit) for i in range(size)])]
  transfers between devices with their start and end apart: 47 -> 47, of which waited for: 18 -> 18; matrix products, arithmetic and copies ran while one was open for 7% -> 8% of each run, Pallas kernels for 37% -> 37%
where the time goes in v3:
time: 455 us; the launch traced here: 447 us
  Pallas kernels  175 us (38%)
  waiting for transfers between devices  124 us (27%)
  starting transfers between devices  87.4 us (19%)
  local copies, waits for them, and re-layouts  27.5 us (6%)
  other arithmetic  16.4 us (4%)
  between operations  16.4 us (4%)
    ppermute x29, waiting for transfers between devices, partner(): return lax.ppermute(values, axis, [(i, i ^ bit) for i in range(size)])  61.6 us
    ppermute x11, waiting for transfers between devices, swap(): return lax.ppermute(values, 'section', [(0, 1), (1, 0)])  49 us
    all_to_all x4, starting transfers between devices, exchange(): return lax.all_to_all(values, 'dp', 0, 0, tiled=True)  39.2 us
    pallas_call x2, Pallas kernels, backward_b_call(): pl.pallas_call(functools.partial(bwd_b_kernel, last), out_shape=out_shape...  37.8 us
    pallas_call x1, Pallas kernels, forward_call(): pl.pallas_call(fwd_kernel, out_shape=[jax.ShapeDtypeStruct((masks, D), BF...  37.7 us
    ppermute x29, starting transfers between devices, partner(): return lax.ppermute(values, axis, [(i, i ^ bit) for i in range(size)])  35.4 us
    pallas_call x2, Pallas kernels, backward_a_call(): pl.pallas_call(functools.partial(bwd_a_kernel, last), out_shape=([jax.Sha...  31.2 us
    pallas_call x1, Pallas kernels, logit_pass(): pl.pallas_call(logit_pass_kernel, grid=(vocab // tile,), out_shape=jax.Sh...  15.4 us
  transfers between devices with their start and end apart: 47, of which 18 were waited for; matrix products, arithmetic and copies ran while one was open for 8% of the time, Pallas kernels for 37%

profile of v3, /device:TPU:0, one launch (start us, length us, event | category | flops | bytes accessed | tf_op | source)
XLA Modules:
  0.0 447.2 jit_solution(8049384229280490389)
XLA Ops:
  15.6 7.4 %all-to-all-start.3 = ((s32[16,1,64]{2,1,0:T(1,128)}), s32[16,1,64]{2,1,0:T(1,128)S(1)}, u32[]{:S(2)}, u32[]{:S(2)}) async-start(s32[16,1,64]{2,1,0:T(1,128)} %bitcast.5), calls=%async_computation.3 | async-start | bytes 16384 | tf_op jit(solution)/shard_map/all_to_all | solution.py:874
  23.0 6.4 %all-to-all-done.3 = s32[16,1,64]{2,1,0:T(1,128)S(1)} async-done(((s32[16,1,64]{2,1,0:T(1,128)}), s32[16,1,64]{2,1,0:T(1,128)S(1)}, u32[]{:S(2)}, u32[]{:S(2)}) %all-to-all-start.3) | async-done | bytes 4128 | tf_op jit(solution)/shard_map/all_to_all | solution.py:874
  39.6 4.8 %all-to-all-start.4 = ((bf16[16,48,768]{2,1,0:T(8,128)(2,1)}), bf16[16,48,768]{2,1,0:T(8,128)(2,1)}, u32[]{:S(2)}, u32[]{:S(2)}) async-start(bf16[16,48,768]{2,1,0:T(8,128)(2,1)} %bitcast.13), calls=%async_computation.4 | async-start | bytes 2359296 | tf_op jit(solution)/shard_map/all_to_all | solution.py:874
  56.4 7.0 %collective-permute-done.3.rest_7_.rest_9_.rest_8_.rest_12_ = bf16[384,768]{1,0:T(8,128)(2,1)} collective-permute-done((bf16[384,768]{1,0:T(8,128)(2,1)}, bf16[384,768]{1,0:T(8,128)(2,1)}, u32[]{:S(2)}, u32[]{:S(2)}) %collective-permute-start.3) | collective-permute-done | bytes 589856 | tf_op jit(solution)/shard_map/ppermute | solution.py:866
  63.4 12.6 %collective-permute-done.1.rest_5_.rest_7_.rest_6_.rest_10_ = bf16[384,768]{1,0:T(8,128)(2,1)} collective-permute-done((bf16[384,768]{1,0:T(8,128)(2,1)S(1)}, bf16[384,768]{1,0:T(8,128)(2,1)}, u32[]{:S(2)}, u32[]{:S(2)}) %collective-permute-start.1) | collective-permute-done | bytes 589856 | tf_op jit(solution)/shard_map/ppermute | solution.py:866
  76.1 12.6 %collective-permute-done.2.rest_6_.rest_8_.rest_7_.rest_11_ = bf16[384,768]{1,0:T(8,128)(2,1)} collective-permute-done((bf16[384,768]{1,0:T(8,128)(2,1)S(1)}, bf16[384,768]{1,0:T(8,128)(2,1)}, u32[]{:S(2)}, u32[]{:S(2)}) %collective-permute-start.2) | collective-permute-done | bytes 589856 | tf_op jit(solution)/shard_map/ppermute | solution.py:866
  101.4 37.7 %forward_layers.1 = (bf16[80,768]{1,0:T(8,128)(2,1)}, bf16[512,768]{1,0:T(8,128)(2,1)}, bf16[512,768]{1,0:T(8,128)(2,1)}, bf16[512,768]{1,0:T(8,128)(2,1)}, bf16...) custom-call(s32[3]{0:T(128)} %pad_add_fusion.1.flag, ...), custom_call_target="tpu_custom_call" | custom-call | flops 35999997952 | bytes 62914560 | tf_op jit(solution)/shard_map/forward_layers/pallas_call | solution.py:286
  148.9 6.4 %all-gather.4.cloned.1.call-done.table_ref = bf16[15360,768]{1,0:T(8,128)(2,1)} async-done(((bf16[960,768]{1,0:T(8,128)(2,1)}), bf16[15360,768]{1,0:T(8,128)(2,1)}) %all-gather.4.cloned.1.call-update) | async-done | bytes 23592976 | tf_op jit(solution)/shard_map/all_gather | solution.py:877
  155.4 13.7 %table_back_pass.1 = f32[80,768]{1,0:T(8,128)} custom-call(bf16[80,15360]{1,0:T(8,128)(2,1)} %bitcast.74, bf16[15360,768]{1,0:T(8,128)(2,1)} %all-gather.4.cloned.1.call-done.table_ref), custom_call_target="tpu_custom_call" | custom-call | flops 10000000000 | bytes 20971520 | tf_op jit(solution)/shard_map/table_back_pass/pallas_call | solution.py:742
  169.7 17.9 %all-to-all-start.5 = ((bf16[16,80,960]{2,1,0:T(8,128)(2,1)}), bf16[16,80,960]{2,1,0:T(8,128)(2,1)S(1)}, u32[]{:S(2)}, u32[]{:S(2)}) async-start(bf16[16,80,960]{2,1,0:T(8,128)(2,1)} %bitcast.70), calls=%async_computation.5 | async-start | bytes 5242880 | tf_op jit(solution)/shard_map/all_to_all | solution.py:874
  193.6 15.4 %backward_second_a.1 = (bf16[16,144,768]{2,1,0:T(8,128)(2,1)}, f32[512,768]{1,0:T(8,128)}, bf16[512,768]{1,0:T(8,128)(2,1)}, f32[16,768]{1,0:T(8,128)}) custom-call(s32[3]{0:T(128)} %pad_add_fusion.1.flag, bf16[80,768]{1,0:T(8,128)(2,1)} %fusion.1.rest_0_, s32[1,80]{1,0:T(1,128)} %broadcast_select_fusion.5.rest_1_, bf16[768,768]{1,0:T(8,128)(2,1)} %bitcast.83, ...), custom_call_target="tpu_custom_call" | custom-call | flops 12000000000 | bytes 20971520 | tf_op jit(solution)/shard_map/backward_second_a/pallas_call | solution.py:420
  209.1 17.5 %backward_second_b.1 = (bf16[8,48,768]{2,1,0:T(8,128)(2,1)}, bf16[8,48,768]{2,1,0:T(8,128)(2,1)}, bf16[512,768]{1,0:T(8,128)(2,1)}) custom-call(s32[3]{0:T(128)} %pad_add_fusion.1.flag, f32[512,768]{1,0:T(8,128)} %get-tuple-element.183.attn_in, bf16[512,768]{1,0:T(8,128)(2,1)} %get-tuple-element.184.back_low, f32[16,768]{1,0:T(8,128)} %get-tuple-element.185.vec_in, ...), custom_call_target="tpu_custom_call" | custom-call | flops 15000000512 | bytes 20971520 | tf_op jit(solution)/shard_map/backward_second_b/pallas_call | solution.py:556
  226.6 15.8 %backward_first_a.1 = (bf16[8,144,768]{2,1,0:T(8,128)(2,1)}, bf16[8,144,768]{2,1,0:T(8,128)(2,1)}, f32[512,768]{1,0:T(8,128)}, bf16[512,768]{1,0:T(8,128)(2,1)}, f32[16,768]{1,0:T(8,128)}) custom-call(s32[3]{0:T(128)} %pad_add_fusion.1.flag, bf16[512,768]{1,0:T(8,128)(2,1)} %get-tuple-element.195.rest_0_, bf16[768,768]{1,0:T(8,128)(2,1)} %bitcast.85, ...), custom_call_target="tpu_custom_call" | custom-call | flops 12000000000 | bytes 20971520 | tf_op jit(solution)/shard_map/backward_first_a/pallas_call | solution.py:420
  246.4 20.3 %backward_first_b.1 = (bf16[8,80,768]{2,1,0:T(8,128)(2,1)}, bf16[8,80,768]{2,1,0:T(8,128)(2,1)}, bf16[512,768]{1,0:T(8,128)(2,1)}, bf16[768,768]{1,0:T(8,128)(2,1)}) custom-call(s32[3]{0:T(128)} %pad_add_fusion.1.flag, f32[512,768]{1,0:T(8,128)} %get-tuple-element.211.attn_in, bf16[512,768]{1,0:T(8,128)(2,1)} %get-tuple-element.212.back_low, ...), custom_call_target="tpu_custom_call" | custom-call | flops 15000000512 | bytes 20971520 | tf_op jit(solution)/shard_map/backward_first_b/pallas_call | solution.py:556
  270.5 9.2 %all-to-all-start.6 = ((bf16[16,48,768]{2,1,0:T(8,128)(2,1)}), bf16[16,48,768]{2,1,0:T(8,128)(2,1)}, u32[]{:S(2)}, u32[]{:S(2)}) async-start(bf16[16,48,768]{2,1,0:T(8,128)(2,1)} %bitcast.75), calls=%async_computation.6 | async-start | bytes 2359296 | tf_op jit(solution)/shard_map/all_to_all | solution.py:874
  284.5 15.4 %table_logit_pass.1 = bf16[80,15360]{1,0:T(8,128)(2,1)} custom-call(bf16[80,768]{1,0:T(8,128)(2,1)} %copy-done.14, bf16[15360,768]{1,0:T(8,128)(2,1)} %all-gather.4.cloned.1.call-done.table_ref), custom_call_target="tpu_custom_call" | custom-call | flops 10000000000 | bytes 20971520 | tf_op jit(solution)/shard_map/table_logit_pass/pallas_call | solution.py:761
  302.5 20.7 %collective-permute-done.19.came_ref = bf16[4,144,768]{2,1,0:T(8,128)(2,1)} collective-permute-done((bf16[4,144,768]{2,1,0:T(8,128)(2,1)}, bf16[4,144,768]{2,1,0:T(8,128)(2,1)}, u32[]{:S(2)}, u32[]{:S(2)}) %collective-permute-start.19) | collective-permute-done | bytes 884768 | tf_op jit(solution)/shard_map/ppermute | solution.py:822
  333.9 4.7 %collective-permute-done.25.came_ref = bf16[4,80,768]{2,1,0:T(8,128)(2,1)} collective-permute-done((bf16[4,80,768]{2,1,0:T(8,128)(2,1)S(1)}, bf16[4,80,768]{2,1,0:T(8,128)(2,1)}, u32[]{:S(2)}, u32[]{:S(2)}) %collective-permute-start.25) | collective-permute-done | bytes 491552 | tf_op jit(solution)/shard_map/ppermute | solution.py:822
  340.6 7.1 %owner_sum.1 = bf16[960,768]{1,0:T(8,128)(2,1)} custom-call(s32[1]{0:T(128)} %bitcast.44.place_ref, s32[1]{0:T(128)} %bitcast.8.base_ref, s32[1,768]{1,0:T(1,128)} %select_n.203.ids_ref, bf16[768,768]{1,0:T(8,128)(2,1)} %bitcast.46.rows_ref, bf16[1280,960]{1,0:T(8,128)(2,1)} %bitcast.73, bf16[8,80,768]{2,1,0:T(8,128)(2,1)} %constant_dynamic-update-slice_fusion.3.heads_own, ...), custom_call_target="tpu_custom_call" | custom-call | flops 6000000000 | bytes 20971520 | tf_op jit(solution)/shard_map/owner_sum/pallas_call | solution.py:787
  351.7 4.8 %collective-permute-done.27 = bf16[144,768]{1,0:T(8,128)(2,1)S(1)} collective-permute-done((bf16[144,768]{1,0:T(8,128)(2,1)}, bf16[144,768]{1,0:T(8,128)(2,1)S(1)}, u32[]{:S(2)}, u32[]{:S(2)}) %collective-permute-start.27) | collective-permute-done | bytes 221216 | tf_op jit(solution)/shard_map/ppermute | solution.py:866
  386.2 6.2 %collective-permute-done.34 = bf16[64,768]{1,0:T(8,128)(2,1)S(1)} collective-permute-done((bf16[64,768]{1,0:T(8,128)(2,1)}, bf16[64,768]{1,0:T(8,128)(2,1)S(1)}, u32[]{:S(2)}, u32[]{:S(2)}) %collective-permute-start.34) | collective-permute-done | bytes 98336 | tf_op jit(solution)/shard_map/ppermute | solution.py:866
  402.9 12.8 %collective-permute-done.36 = bf16[64,768]{1,0:T(8,128)(2,1)S(1)} collective-permute-done((bf16[64,768]{1,0:T(8,128)(2,1)S(1)}, bf16[64,768]{1,0:T(8,128)(2,1)S(1)}, u32[]{:S(2)}, u32[]{:S(2)}) %collective-permute-start.36) | collective-permute-done | bytes 98336 | tf_op jit(solution)/shard_map/ppermute | solution.py:822
  417.5 8.4 %collective-permute-done.38 = bf16[4,64,768]{2,1,0:T(8,128)(2,1)S(1)} collective-permute-done((bf16[4,64,768]{2,1,0:T(8,128)(2,1)S(1)}, bf16[4,64,768]{2,1,0:T(8,128)(2,1)S(1)}, u32[]{:S(2)}, u32[]{:S(2)}) %collective-permute-start.38) | collective-permute-done | bytes 393248 | tf_op jit(solution)/shard_map/ppermute | solution.py:822
  430.4 7.0 %unpack_sums.1 = (f32[768,768]{1,0:T(8,128)}, f32[768,768]{1,0:T(8,128)}, f32[768,768]{1,0:T(8,128)}, f32[4,192,192]{2,1,0:T(8,128)}, f32[4,192,192]{2,1,0:T(8,1...) custom-call(s32[3]{0:T(128)} %pad_add_fusion.1.flag, ...), custom_call_target="tpu_custom_call" | custom-call | flops 1000000000 | bytes 16777216 | tf_op jit(solution)/shard_map/unpack_sums/pallas_call | solution.py:666
  (243 shorter events, 139.2 us)
Async XLA Ops:
  7.2 148.2 %all-gather.4.cloned.1.call-start = ((), (), s32[]{:S(2)}) async-start(), calls=%async_computation.8 | async-start | bytes 25067520 | tf_op jit(solution)/shard_map/all_gather | solution.py:877
  39.6 61.0 %all-to-all-start.4 = ((bf16[16,48,768]{2,1,0:T(8,128)(2,1)}), bf16[16,48,768]{2,1,0:T(8,128)(2,1)}, u32[]{:S(2)}, u32[]{:S(2)}) async-start(bf16[16,48,768]{2,1,0:T(8,128)(2,1)} %bitcast.13), calls=%async_computation.4 | async-start | bytes 2359296 | tf_op jit(solution)/shard_map/all_to_all | solution.py:874
  44.5 56.2 %collective-permute-start.9 = (f32[8,768]{1,0:T(8,128)S(1)}, f32[8,768]{1,0:T(8,128)S(1)}, u32[]{:S(2)}, u32[]{:S(2)}) collective-permute-start(f32[8,768]{1,0:T(8,128)S(1)} %concatenate.51.rest_4_.rest_6_.rest_5_.rest_9_), channel_id=1, source_target_pairs={{0,16},{16,0},{1,17},{17,1},{2,18},{18,2},{3,19},{19,3},{4,20},{20... | collective-permute-start | bytes 73736 | tf_op jit(solution)/shard_map/ppermute | solution.py:866
  48.6 27.5 %collective-permute-start.1 = (bf16[384,768]{1,0:T(8,128)(2,1)S(1)}, bf16[384,768]{1,0:T(8,128)(2,1)}, u32[]{:S(2)}, u32[]{:S(2)}) collective-permute-start(bf16[384,768]{1,0:T(8,128)(2,1)S(1)} %constant_dynamic-slice_fusion.2), channel_id=1, source_target_pairs={{0,16},{16,0},{1,17},{17,1},{2,18},{18,2},{3,19},{19,3},{4,20},{20... | collective-permute-start | bytes 1769480 | tf_op jit(solution)/shard_map/ppermute | solution.py:866
  51.3 37.4 %collective-permute-start.2 = (bf16[384,768]{1,0:T(8,128)(2,1)S(1)}, bf16[384,768]{1,0:T(8,128)(2,1)}, u32[]{:S(2)}, u32[]{:S(2)}) collective-permute-start(bf16[384,768]{1,0:T(8,128)(2,1)S(1)} %constant_dynamic-slice_fusion.1), channel_id=1, source_target_pairs={{0,16},{16,0},{1,17},{17,1},{2,18},{18,2},{3,19},{19,3},{4,20},{20... | collective-permute-start | bytes 1769480 | tf_op jit(solution)/shard_map/ppermute | solution.py:866
  54.9 43.3 %collective-permute-start.4 = (bf16[288,768]{1,0:T(8,128)(2,1)}, bf16[288,768]{1,0:T(8,128)(2,1)}, u32[]{:S(2)}, u32[]{:S(2)}) collective-permute-start(bf16[288,768]{1,0:T(8,128)(2,1)} %constant_dynamic-slice_fusion), channel_id=1, source_target_pairs={{0,16},{16,0},{1,17},{17,1},{2,18},{18,2},{3,19},{19,3},{4,20},{20... | collective-permute-start | bytes 1327112 | tf_op jit(solution)/shard_map/ppermute | solution.py:866
  63.4 37.3 %collective-permute-start.7 = (bf16[384,768]{1,0:T(8,128)(2,1)}, bf16[384,768]{1,0:T(8,128)(2,1)}, u32[]{:S(2)}, u32[]{:S(2)}) collective-permute-start(bf16[384,768]{1,0:T(8,128)(2,1)} %collective-permute-done.3.rest_7_.rest_9_.rest_8_.rest_12_), channel_id=1, source_target_pairs={{0,1},{1,0},{2,3},{3,2},{4,5},{5,4},{6,7},{7,6},{8,9},{9,8},{10,11... | collective-permute-start | bytes 1769480 | tf_op jit(solution)/shard_map/ppermute | solution.py:822
  76.1 24.6 %collective-permute-start.5 = (bf16[384,768]{1,0:T(8,128)(2,1)}, bf16[384,768]{1,0:T(8,128)(2,1)}, u32[]{:S(2)}, u32[]{:S(2)}) collective-permute-start(bf16[384,768]{1,0:T(8,128)(2,1)} %collective-permute-done.1.rest_5_.rest_7_.rest_6_.rest_10_), channel_id=1, source_target_pairs={{0,1},{1,0},{2,3},{3,2},{4,5},{5,4},{6,7},{7,6},{8,9},{9,8},{10,11... | collective-permute-start | bytes 1769480 | tf_op jit(solution)/shard_map/ppermute | solution.py:822
  144.3 24.7 %collective-permute-start.13 = (bf16[80,768]{1,0:T(8,128)(2,1)S(1)}, bf16[80,768]{1,0:T(8,128)(2,1)S(1)}, u32[]{:S(2)}, u32[]{:S(2)}) collective-permute-start(bf16[80,768]{1,0:T(8,128)(2,1)S(1)} %maximum_select_fusion.1.head_ref), channel_id=1, source_target_pairs={{0,12},{1,13},{2,14},{3,15},{4,8},{5,9},{6,10},{7,11},{8,4},{9,5},... | collective-permute-start | bytes 368648 | tf_op jit(solution)/shard_map/ppermute | solution.py:822
  148.3 20.8 %collective-permute-start.12 = (bf16[80,768]{1,0:T(8,128)(2,1)S(1)}, bf16[80,768]{1,0:T(8,128)(2,1)S(1)}, u32[]{:S(2)}, u32[]{:S(2)}) collective-permute-start(bf16[80,768]{1,0:T(8,128)(2,1)S(1)} %maximum_select_fusion.1.head_ref), channel_id=1, source_target_pairs={{0,8},{1,9},{2,10},{3,11},{4,12},{5,13},{6,14},{7,15},{8,0},{9,1},... | collective-permute-start | bytes 368648 | tf_op jit(solution)/shard_map/ppermute | solution.py:822
  148.3 20.8 %collective-permute-start.11 = (bf16[80,768]{1,0:T(8,128)(2,1)S(1)}, bf16[80,768]{1,0:T(8,128)(2,1)S(1)}, u32[]{:S(2)}, u32[]{:S(2)}) collective-permute-start(bf16[80,768]{1,0:T(8,128)(2,1)S(1)} %maximum_select_fusion.1.head_ref), channel_id=1, source_target_pairs={{0,4},{1,5},{2,6},{3,7},{4,0},{5,1},{6,2},{7,3},{8,12},{9,13},{10,... | collective-permute-start | bytes 368648 | tf_op jit(solution)/shard_map/ppermute | solution.py:822
  169.7 72.7 %all-to-all-start.5 = ((bf16[16,80,960]{2,1,0:T(8,128)(2,1)}), bf16[16,80,960]{2,1,0:T(8,128)(2,1)S(1)}, u32[]{:S(2)}, u32[]{:S(2)}) async-start(bf16[16,80,960]{2,1,0:T(8,128)(2,1)} %bitcast.70), calls=%async_computation.5 | async-start | bytes 5242880 | tf_op jit(solution)/shard_map/all_to_all | solution.py:874
  187.6 160.2 %reduce-scatter.2.cloned.1.call-start = ((), (), s32[]{:S(2)}) async-start(), calls=%async_computation.9 | async-start | bytes 3760128 | tf_op jit(solution)/shard_map/reduce_scatter | solution.py:969
  191.0 51.4 %collective-permute-start.15 = (bf16[4,80,768]{2,1,0:T(8,128)(2,1)S(1)}, bf16[4,80,768]{2,1,0:T(8,128)(2,1)}, u32[]{:S(2)}, u32[]{:S(2)}) collective-permute-start(bf16[4,80,768]{2,1,0:T(8,128)(2,1)S(1)} %pad_maximum_fusion), channel_id=1, source_target_pairs={{0,2},{1,3},{2,0},{3,1},{4,6},{5,7},{6,4},{7,5},{8,10},{9,11},{10,... | collective-permute-start | bytes 1474568 | tf_op jit(solution)/shard_map/ppermute | solution.py:822
  242.4 24.5 %collective-permute-start.16 = (bf16[8,144,768]{2,1,0:T(8,128)(2,1)}, bf16[8,144,768]{2,1,0:T(8,128)(2,1)}, u32[]{:S(2)}, u32[]{:S(2)}) collective-permute-start(bf16[8,144,768]{2,1,0:T(8,128)(2,1)} %get-tuple-element.226), channel_id=1, source_target_pairs={{0,1},{1,0},{2,3},{3,2},{4,5},{5,4},{6,7},{7,6},{8,9},{9,8},{10,11... | collective-permute-start | bytes 5308424 | tf_op jit(solution)/shard_map/ppermute | solution.py:822
  243.2 23.7 %collective-permute-start.17 = (bf16[8,48,768]{2,1,0:T(8,128)(2,1)}, bf16[8,48,768]{2,1,0:T(8,128)(2,1)}, u32[]{:S(2)}, u32[]{:S(2)}) collective-permute-start(bf16[8,48,768]{2,1,0:T(8,128)(2,1)} %get-tuple-element.227), channel_id=1, source_target_pairs={{0,1},{1,0},{2,3},{3,2},{4,5},{5,4},{6,7},{7,6},{8,9},{9,8},{10,11... | collective-permute-start | bytes 1769480 | tf_op jit(solution)/shard_map/ppermute | solution.py:822
  246.3 20.6 %collective-permute-start.18 = (bf16[8,80,768]{2,1,0:T(8,128)(2,1)}, bf16[8,80,768]{2,1,0:T(8,128)(2,1)}, u32[]{:S(2)}, u32[]{:S(2)}) collective-permute-start(bf16[8,80,768]{2,1,0:T(8,128)(2,1)} %constant_dynamic-update-slice_fusion.3.heads_own), channel_id=1, source_target_pairs={{0,1},{1,0},{2,3},{3,2},{4,5},{5,4},{6,7},{7,6},{8,9},{9,8},{10,11... | collective-permute-start | bytes 2949128 | tf_op jit(solution)/shard_map/ppermute | solution.py:822
  270.5 70.1 %all-to-all-start.6 = ((bf16[16,48,768]{2,1,0:T(8,128)(2,1)}), bf16[16,48,768]{2,1,0:T(8,128)(2,1)}, u32[]{:S(2)}, u32[]{:S(2)}) async-start(bf16[16,48,768]{2,1,0:T(8,128)(2,1)} %bitcast.75), calls=%async_computation.6 | async-start | bytes 2359296 | tf_op jit(solution)/shard_map/all_to_all | solution.py:874
  279.7 149.8 %all-gather.6.cloned.1.call-start = ((), (), s32[]{:S(2)}) async-start(), calls=%async_computation.10 | async-start | bytes 3760128 | tf_op jit(solution)/shard_map/all_gather | solution.py:1035
  279.8 20.1 %collective-permute-start.20 = (bf16[8,80,768]{2,1,0:T(8,128)(2,1)}, bf16[8,80,768]{2,1,0:T(8,128)(2,1)}, u32[]{:S(2)}, u32[]{:S(2)}) collective-permute-start(bf16[8,80,768]{2,1,0:T(8,128)(2,1)} %get-tuple-element.239), channel_id=1, source_target_pairs={{0,1},{1,0},{2,3},{3,2},{4,5},{5,4},{6,7},{7,6},{8,9},{9,8},{10,11... | collective-permute-start | bytes 2949128 | tf_op jit(solution)/shard_map/ppermute | solution.py:822
  282.4 20.1 %collective-permute-start.21 = (bf16[4,48,768]{2,1,0:T(8,128)(2,1)}, bf16[4,48,768]{2,1,0:T(8,128)(2,1)S(1)}, u32[]{:S(2)}, u32[]{:S(2)}) collective-permute-start(bf16[4,48,768]{2,1,0:T(8,128)(2,1)} %get-tuple-element.243), channel_id=1, source_target_pairs={{0,2},{1,3},{2,0},{3,1},{4,6},{5,7},{6,4},{7,5},{8,10},{9,11},{10,... | collective-permute-start | bytes 884744 | tf_op jit(solution)/shard_map/ppermute | solution.py:822
  284.1 39.1 %collective-permute-start.19 = (bf16[4,144,768]{2,1,0:T(8,128)(2,1)}, bf16[4,144,768]{2,1,0:T(8,128)(2,1)}, u32[]{:S(2)}, u32[]{:S(2)}) collective-permute-start(bf16[4,144,768]{2,1,0:T(8,128)(2,1)} %get-tuple-element.236), channel_id=1, source_target_pairs={{0,2},{1,3},{2,0},{3,1},{4,6},{5,7},{6,4},{7,5},{8,10},{9,11},{10,... | collective-permute-start | bytes 2654216 | tf_op jit(solution)/shard_map/ppermute | solution.py:822
  327.7 20.1 %collective-permute-start.22 = (bf16[144,768]{1,0:T(8,128)(2,1)}, bf16[144,768]{1,0:T(8,128)(2,1)}, u32[]{:S(2)}, u32[]{:S(2)}) collective-permute-start(bf16[144,768]{1,0:T(8,128)(2,1)} %get-tuple-element.254), channel_id=1, source_target_pairs={{0,4},{1,5},{2,6},{3,7},{4,0},{5,1},{6,2},{7,3},{8,12},{9,13},{10,... | collective-permute-start | bytes 663560 | tf_op jit(solution)/shard_map/ppermute | solution.py:822
  358.2 57.6 %collective-permute-start.26 = (bf16[960,768]{1,0:T(8,128)(2,1)S(1)}, bf16[960,768]{1,0:T(8,128)(2,1)}, u32[]{:S(2)}, u32[]{:S(2)}) collective-permute-start(bf16[960,768]{1,0:T(8,128)(2,1)S(1)} %copy-done.4), channel_id=1, source_target_pairs={{0,16},{16,0},{1,17},{17,1},{2,18},{18,2},{3,19},{19,3},{4,20},{20... | collective-permute-start | bytes 4423688 | tf_op jit(solution)/shard_map/ppermute | solution.py:866
  (66 other events, 824.0 us)
Sparse Core Ops, SparseCore 0:
  9.6 145.7 all-gather.3
  226.7 83.3 reduce-scatter.1
  358.3 59.9 all-gather.5

commit v4 on v3

--- a/solution.py
+++ b/solution.py
@@ -984,12 +984,11 @@
     )
     slot_grad, away_b0, came_a0, came_b1, heads = lax.optimization_barrier((slot_grad, away_b0, came_a0, came_b1, heads))
     keep_a0, away_a0 = step_y(side_y, keep_a0, came_a0)
-    away_a0, away_b0, head_rows, slot_grad, keep_b1, came_b1 = lax.optimization_barrier(
-        (away_a0, away_b0, head_rows, slot_grad, keep_b1, came_b1)
-    )
+    away_a0, away_b0, head_rows = lax.optimization_barrier((away_a0, away_b0, head_rows))
     came_a0 = partner(away_a0, "dp", 2)
     came_b0 = partner(away_b0, "dp", 1)
     logits = logit_pass(head_rows, table)
+    logits, slot_grad, keep_b1, came_b1 = lax.optimization_barrier((logits, slot_grad, keep_b1, came_b1))
     keep_b1, away_b1 = step_y(side_y, keep_b1, came_b1)
     came_b1 = partner(away_b1, "dp", 2)
     keep_b0, away_b0 = step_y(side_y, keep_b0, came_b0)

time: 455 us -> 470 us (1.033)
  waiting for transfers between devices: 124 us -> 141 us
    ppermute x29, waiting for transfers between devices: 61.6 us -> 77.9 us  [partner(): return lax.ppermute(values, axis, [(i, i ^ bit) for i in range(size)])]
  transfers between devices with their start and end apart: 47 -> 47, of which waited for: 18 -> 18; matrix products, arithmetic and copies ran while one was open for 8% -> 8% of each run, Pallas kernels for 37% -> 36%
where the time goes in v4:
time: 470 us; the launch traced here: 462 us
  Pallas kernels  175 us (37%)
  waiting for transfers between devices  141 us (30%)
  starting transfers between devices  86.2 us (18%)
  local copies, waits for them, and re-layouts  27.4 us (6%)
  other arithmetic  16.4 us (3%)
  between operations  16.3 us (3%)
    ppermute x29, waiting for transfers between devices, partner(): return lax.ppermute(values, axis, [(i, i ^ bit) for i in range(size)])  77.9 us
    ppermute x11, waiting for transfers between devices, swap(): return lax.ppermute(values, 'section', [(0, 1), (1, 0)])  49.2 us
    all_to_all x4, starting transfers between devices, exchange(): return lax.all_to_all(values, 'dp', 0, 0, tiled=True)  39 us
    pallas_call x2, Pallas kernels, backward_b_call(): pl.pallas_call(functools.partial(bwd_b_kernel, last), out_shape=out_shape...  37.7 us
    pallas_call x1, Pallas kernels, forward_call(): pl.pallas_call(fwd_kernel, out_shape=[jax.ShapeDtypeStruct((masks, D), BF...  37.7 us
    ppermute x29, starting transfers between devices, partner(): return lax.ppermute(values, axis, [(i, i ^ bit) for i in range(size)])  34.1 us
    pallas_call x2, Pallas kernels, backward_a_call(): pl.pallas_call(functools.partial(bwd_a_kernel, last), out_shape=([jax.Sha...  31.1 us
    pallas_call x1, Pallas kernels, logit_pass(): pl.pallas_call(logit_pass_kernel, grid=(vocab // tile,), out_shape=jax.Sh...  15.3 us
  transfers between devices with their start and end apart: 47, of which 18 were waited for; matrix products, arithmetic and copies ran while one was open for 8% of the time, Pallas kernels for 36%

profile of v4, /device:TPU:0, one launch (start us, length us, event | category | flops | bytes accessed | tf_op | source)
XLA Modules:
  0.0 462.2 jit_solution(4538407123979613179)
XLA Ops:
  15.6 7.4 %all-to-all-start.3 = ((s32[16,1,64]{2,1,0:T(1,128)}), s32[16,1,64]{2,1,0:T(1,128)S(1)}, u32[]{:S(2)}, u32[]{:S(2)}) async-start(s32[16,1,64]{2,1,0:T(1,128)} %bitcast.5), calls=%async_computation.3 | async-start | bytes 16384 | tf_op jit(solution)/shard_map/all_to_all | solution.py:874
  23.0 6.4 %all-to-all-done.3 = s32[16,1,64]{2,1,0:T(1,128)S(1)} async-done(((s32[16,1,64]{2,1,0:T(1,128)}), s32[16,1,64]{2,1,0:T(1,128)S(1)}, u32[]{:S(2)}, u32[]{:S(2)}) %all-to-all-start.3) | async-done | bytes 4128 | tf_op jit(solution)/shard_map/all_to_all | solution.py:874
  39.7 4.8 %all-to-all-start.4 = ((bf16[16,48,768]{2,1,0:T(8,128)(2,1)}), bf16[16,48,768]{2,1,0:T(8,128)(2,1)}, u32[]{:S(2)}, u32[]{:S(2)}) async-start(bf16[16,48,768]{2,1,0:T(8,128)(2,1)} %bitcast.13), calls=%async_computation.4 | async-start | bytes 2359296 | tf_op jit(solution)/shard_map/all_to_all | solution.py:874
  56.5 7.0 %collective-permute-done.3.rest_7_.rest_9_.rest_8_.rest_12_ = bf16[384,768]{1,0:T(8,128)(2,1)} collective-permute-done((bf16[384,768]{1,0:T(8,128)(2,1)}, bf16[384,768]{1,0:T(8,128)(2,1)}, u32[]{:S(2)}, u32[]{:S(2)}) %collective-permute-start.3) | collective-permute-done | bytes 589856 | tf_op jit(solution)/shard_map/ppermute | solution.py:866
  63.5 12.6 %collective-permute-done.1.rest_5_.rest_7_.rest_6_.rest_10_ = bf16[384,768]{1,0:T(8,128)(2,1)} collective-permute-done((bf16[384,768]{1,0:T(8,128)(2,1)S(1)}, bf16[384,768]{1,0:T(8,128)(2,1)}, u32[]{:S(2)}, u32[]{:S(2)}) %collective-permute-start.1) | collective-permute-done | bytes 589856 | tf_op jit(solution)/shard_map/ppermute | solution.py:866
  76.1 12.6 %collective-permute-done.2.rest_6_.rest_8_.rest_7_.rest_11_ = bf16[384,768]{1,0:T(8,128)(2,1)} collective-permute-done((bf16[384,768]{1,0:T(8,128)(2,1)S(1)}, bf16[384,768]{1,0:T(8,128)(2,1)}, u32[]{:S(2)}, u32[]{:S(2)}) %collective-permute-start.2) | collective-permute-done | bytes 589856 | tf_op jit(solution)/shard_map/ppermute | solution.py:866
  101.6 37.7 %forward_layers.1 = (bf16[80,768]{1,0:T(8,128)(2,1)}, bf16[512,768]{1,0:T(8,128)(2,1)}, bf16[512,768]{1,0:T(8,128)(2,1)}, bf16[512,768]{1,0:T(8,128)(2,1)}, bf16...) custom-call(s32[3]{0:T(128)} %pad_add_fusion.1.flag, ...), custom_call_target="tpu_custom_call" | custom-call | flops 35999997952 | bytes 62914560 | tf_op jit(solution)/shard_map/forward_layers/pallas_call | solution.py:286
  149.0 6.5 %all-gather.4.cloned.1.call-done.table_ref = bf16[15360,768]{1,0:T(8,128)(2,1)} async-done(((bf16[960,768]{1,0:T(8,128)(2,1)}), bf16[15360,768]{1,0:T(8,128)(2,1)}) %all-gather.4.cloned.1.call-update) | async-done | bytes 23592976 | tf_op jit(solution)/shard_map/all_gather | solution.py:877
  155.5 13.7 %table_back_pass.1 = f32[80,768]{1,0:T(8,128)} custom-call(bf16[80,15360]{1,0:T(8,128)(2,1)} %bitcast.74, bf16[15360,768]{1,0:T(8,128)(2,1)} %all-gather.4.cloned.1.call-done.table_ref), custom_call_target="tpu_custom_call" | custom-call | flops 10000000000 | bytes 20971520 | tf_op jit(solution)/shard_map/table_back_pass/pallas_call | solution.py:742
  169.9 17.8 %all-to-all-start.5 = ((bf16[16,80,960]{2,1,0:T(8,128)(2,1)}), bf16[16,80,960]{2,1,0:T(8,128)(2,1)S(1)}, u32[]{:S(2)}, u32[]{:S(2)}) async-start(bf16[16,80,960]{2,1,0:T(8,128)(2,1)} %bitcast.70), calls=%async_computation.5 | async-start | bytes 5242880 | tf_op jit(solution)/shard_map/all_to_all | solution.py:874
  193.6 15.4 %backward_second_a.1 = (bf16[16,144,768]{2,1,0:T(8,128)(2,1)}, f32[512,768]{1,0:T(8,128)}, bf16[512,768]{1,0:T(8,128)(2,1)}, f32[16,768]{1,0:T(8,128)}) custom-call(s32[3]{0:T(128)} %pad_add_fusion.1.flag, bf16[80,768]{1,0:T(8,128)(2,1)} %fusion.1.rest_0_, s32[1,80]{1,0:T(1,128)} %broadcast_select_fusion.5.rest_1_, bf16[768,768]{1,0:T(8,128)(2,1)} %bitcast.83, ...), custom_call_target="tpu_custom_call" | custom-call | flops 12000000000 | bytes 20971520 | tf_op jit(solution)/shard_map/backward_second_a/pallas_call | solution.py:420
  209.1 17.5 %backward_second_b.1 = (bf16[8,48,768]{2,1,0:T(8,128)(2,1)}, bf16[8,48,768]{2,1,0:T(8,128)(2,1)}, bf16[512,768]{1,0:T(8,128)(2,1)}) custom-call(s32[3]{0:T(128)} %pad_add_fusion.1.flag, f32[512,768]{1,0:T(8,128)} %get-tuple-element.184.attn_in, bf16[512,768]{1,0:T(8,128)(2,1)} %get-tuple-element.185.back_low, f32[16,768]{1,0:T(8,128)} %get-tuple-element.186.vec_in, ...), custom_call_target="tpu_custom_call" | custom-call | flops 15000000512 | bytes 20971520 | tf_op jit(solution)/shard_map/backward_second_b/pallas_call | solution.py:556
  226.6 15.7 %backward_first_a.1 = (bf16[8,144,768]{2,1,0:T(8,128)(2,1)}, bf16[8,144,768]{2,1,0:T(8,128)(2,1)}, f32[512,768]{1,0:T(8,128)}, bf16[512,768]{1,0:T(8,128)(2,1)}, f32[16,768]{1,0:T(8,128)}) custom-call(s32[3]{0:T(128)} %pad_add_fusion.1.flag, bf16[512,768]{1,0:T(8,128)(2,1)} %get-tuple-element.196.rest_0_, bf16[768,768]{1,0:T(8,128)(2,1)} %bitcast.85, ...), custom_call_target="tpu_custom_call" | custom-call | flops 12000000000 | bytes 20971520 | tf_op jit(solution)/shard_map/backward_first_a/pallas_call | solution.py:420
  246.4 20.2 %backward_first_b.1 = (bf16[8,80,768]{2,1,0:T(8,128)(2,1)}, bf16[8,80,768]{2,1,0:T(8,128)(2,1)}, bf16[512,768]{1,0:T(8,128)(2,1)}, bf16[768,768]{1,0:T(8,128)(2,1)}) custom-call(s32[3]{0:T(128)} %pad_add_fusion.1.flag, f32[512,768]{1,0:T(8,128)} %get-tuple-element.212.attn_in, bf16[512,768]{1,0:T(8,128)(2,1)} %get-tuple-element.213.back_low, ...), custom_call_target="tpu_custom_call" | custom-call | flops 15000000512 | bytes 20971520 | tf_op jit(solution)/shard_map/backward_first_b/pallas_call | solution.py:556
  270.5 15.3 %table_logit_pass.1 = bf16[80,15360]{1,0:T(8,128)(2,1)} custom-call(bf16[80,768]{1,0:T(8,128)(2,1)} %copy-done.14, bf16[15360,768]{1,0:T(8,128)(2,1)} %all-gather.4.cloned.1.call-done.table_ref), custom_call_target="tpu_custom_call" | custom-call | flops 10000000000 | bytes 20971520 | tf_op jit(solution)/shard_map/table_logit_pass/pallas_call | solution.py:761
  285.8 9.1 %all-to-all-start.6 = ((bf16[16,48,768]{2,1,0:T(8,128)(2,1)}), bf16[16,48,768]{2,1,0:T(8,128)(2,1)}, u32[]{:S(2)}, u32[]{:S(2)}) async-start(bf16[16,48,768]{2,1,0:T(8,128)(2,1)} %bitcast.75), calls=%async_computation.6 | async-start | bytes 2359296 | tf_op jit(solution)/shard_map/all_to_all | solution.py:874
  302.5 35.9 %collective-permute-done.21.came_ref = bf16[4,48,768]{2,1,0:T(8,128)(2,1)} collective-permute-done((bf16[4,48,768]{2,1,0:T(8,128)(2,1)}, bf16[4,48,768]{2,1,0:T(8,128)(2,1)}, u32[]{:S(2)}, u32[]{:S(2)}) %collective-permute-start.21) | collective-permute-done | bytes 294944 | tf_op jit(solution)/shard_map/ppermute | solution.py:822
  348.1 5.7 %collective-permute-done.25.came_ref = bf16[4,80,768]{2,1,0:T(8,128)(2,1)} collective-permute-done((bf16[4,80,768]{2,1,0:T(8,128)(2,1)S(1)}, bf16[4,80,768]{2,1,0:T(8,128)(2,1)}, u32[]{:S(2)}, u32[]{:S(2)}) %collective-permute-start.25) | collective-permute-done | bytes 491552 | tf_op jit(solution)/shard_map/ppermute | solution.py:822
  355.7 7.1 %owner_sum.1 = bf16[960,768]{1,0:T(8,128)(2,1)} custom-call(s32[1]{0:T(128)} %bitcast.44.place_ref, s32[1]{0:T(128)} %bitcast.8.base_ref, s32[1,768]{1,0:T(1,128)} %select_n.203.ids_ref, bf16[768,768]{1,0:T(8,128)(2,1)} %bitcast.46.rows_ref, bf16[1280,960]{1,0:T(8,128)(2,1)} %bitcast.73, bf16[8,80,768]{2,1,0:T(8,128)(2,1)} %constant_dynamic-update-slice_fusion.3.heads_own, ...), custom_call_target="tpu_custom_call" | custom-call | flops 6000000000 | bytes 20971520 | tf_op jit(solution)/shard_map/owner_sum/pallas_call | solution.py:787
  366.8 4.8 %collective-permute-done.27 = bf16[144,768]{1,0:T(8,128)(2,1)S(1)} collective-permute-done((bf16[144,768]{1,0:T(8,128)(2,1)}, bf16[144,768]{1,0:T(8,128)(2,1)S(1)}, u32[]{:S(2)}, u32[]{:S(2)}) %collective-permute-start.27) | collective-permute-done | bytes 221216 | tf_op jit(solution)/shard_map/ppermute | solution.py:866
  401.3 6.2 %collective-permute-done.34 = bf16[64,768]{1,0:T(8,128)(2,1)S(1)} collective-permute-done((bf16[64,768]{1,0:T(8,128)(2,1)}, bf16[64,768]{1,0:T(8,128)(2,1)S(1)}, u32[]{:S(2)}, u32[]{:S(2)}) %collective-permute-start.34) | collective-permute-done | bytes 98336 | tf_op jit(solution)/shard_map/ppermute | solution.py:866
  418.0 12.7 %collective-permute-done.36 = bf16[64,768]{1,0:T(8,128)(2,1)S(1)} collective-permute-done((bf16[64,768]{1,0:T(8,128)(2,1)S(1)}, bf16[64,768]{1,0:T(8,128)(2,1)S(1)}, u32[]{:S(2)}, u32[]{:S(2)}) %collective-permute-start.36) | collective-permute-done | bytes 98336 | tf_op jit(solution)/shard_map/ppermute | solution.py:822
  431.7 9.1 %collective-permute-done.38 = bf16[4,64,768]{2,1,0:T(8,128)(2,1)S(1)} collective-permute-done((bf16[4,64,768]{2,1,0:T(8,128)(2,1)S(1)}, bf16[4,64,768]{2,1,0:T(8,128)(2,1)S(1)}, u32[]{:S(2)}, u32[]{:S(2)}) %collective-permute-start.38) | collective-permute-done | bytes 393248 | tf_op jit(solution)/shard_map/ppermute | solution.py:822
  445.4 7.0 %unpack_sums.1 = (f32[768,768]{1,0:T(8,128)}, f32[768,768]{1,0:T(8,128)}, f32[768,768]{1,0:T(8,128)}, f32[4,192,192]{2,1,0:T(8,128)}, f32[4,192,192]{2,1,0:T(8,1...) custom-call(s32[3]{0:T(128)} %pad_add_fusion.1.flag, ...), custom_call_target="tpu_custom_call" | custom-call | flops 1000000000 | bytes 16777216 | tf_op jit(solution)/shard_map/unpack_sums/pallas_call | solution.py:666
  (241 shorter events, 138.0 us)
Async XLA Ops:
  7.2 148.3 %all-gather.4.cloned.1.call-start = ((), (), s32[]{:S(2)}) async-start(), calls=%async_computation.8 | async-start | bytes 25067520 | tf_op jit(solution)/shard_map/all_gather | solution.py:877
  39.7 61.1 %all-to-all-start.4 = ((bf16[16,48,768]{2,1,0:T(8,128)(2,1)}), bf16[16,48,768]{2,1,0:T(8,128)(2,1)}, u32[]{:S(2)}, u32[]{:S(2)}) async-start(bf16[16,48,768]{2,1,0:T(8,128)(2,1)} %bitcast.13), calls=%async_computation.4 | async-start | bytes 2359296 | tf_op jit(solution)/shard_map/all_to_all | solution.py:874
  44.6 56.2 %collective-permute-start.9 = (f32[8,768]{1,0:T(8,128)S(1)}, f32[8,768]{1,0:T(8,128)S(1)}, u32[]{:S(2)}, u32[]{:S(2)}) collective-permute-start(f32[8,768]{1,0:T(8,128)S(1)} %concatenate.51.rest_4_.rest_6_.rest_5_.rest_9_), channel_id=1, source_target_pairs={{0,16},{16,0},{1,17},{17,1},{2,18},{18,2},{3,19},{19,3},{4,20},{20... | collective-permute-start | bytes 73736 | tf_op jit(solution)/shard_map/ppermute | solution.py:866
  48.7 27.5 %collective-permute-start.1 = (bf16[384,768]{1,0:T(8,128)(2,1)S(1)}, bf16[384,768]{1,0:T(8,128)(2,1)}, u32[]{:S(2)}, u32[]{:S(2)}) collective-permute-start(bf16[384,768]{1,0:T(8,128)(2,1)S(1)} %constant_dynamic-slice_fusion.2), channel_id=1, source_target_pairs={{0,16},{16,0},{1,17},{17,1},{2,18},{18,2},{3,19},{19,3},{4,20},{20... | collective-permute-start | bytes 1769480 | tf_op jit(solution)/shard_map/ppermute | solution.py:866
  51.4 37.4 %collective-permute-start.2 = (bf16[384,768]{1,0:T(8,128)(2,1)S(1)}, bf16[384,768]{1,0:T(8,128)(2,1)}, u32[]{:S(2)}, u32[]{:S(2)}) collective-permute-start(bf16[384,768]{1,0:T(8,128)(2,1)S(1)} %constant_dynamic-slice_fusion.1), channel_id=1, source_target_pairs={{0,16},{16,0},{1,17},{17,1},{2,18},{18,2},{3,19},{19,3},{4,20},{20... | collective-permute-start | bytes 1769480 | tf_op jit(solution)/shard_map/ppermute | solution.py:866
  55.0 43.3 %collective-permute-start.4 = (bf16[288,768]{1,0:T(8,128)(2,1)}, bf16[288,768]{1,0:T(8,128)(2,1)}, u32[]{:S(2)}, u32[]{:S(2)}) collective-permute-start(bf16[288,768]{1,0:T(8,128)(2,1)} %constant_dynamic-slice_fusion), channel_id=1, source_target_pairs={{0,16},{16,0},{1,17},{17,1},{2,18},{18,2},{3,19},{19,3},{4,20},{20... | collective-permute-start | bytes 1327112 | tf_op jit(solution)/shard_map/ppermute | solution.py:866
  63.5 37.3 %collective-permute-start.7 = (bf16[384,768]{1,0:T(8,128)(2,1)}, bf16[384,768]{1,0:T(8,128)(2,1)}, u32[]{:S(2)}, u32[]{:S(2)}) collective-permute-start(bf16[384,768]{1,0:T(8,128)(2,1)} %collective-permute-done.3.rest_7_.rest_9_.rest_8_.rest_12_), channel_id=1, source_target_pairs={{0,1},{1,0},{2,3},{3,2},{4,5},{5,4},{6,7},{7,6},{8,9},{9,8},{10,11... | collective-permute-start | bytes 1769480 | tf_op jit(solution)/shard_map/ppermute | solution.py:822
  76.1 24.7 %collective-permute-start.5 = (bf16[384,768]{1,0:T(8,128)(2,1)}, bf16[384,768]{1,0:T(8,128)(2,1)}, u32[]{:S(2)}, u32[]{:S(2)}) collective-permute-start(bf16[384,768]{1,0:T(8,128)(2,1)} %collective-permute-done.1.rest_5_.rest_7_.rest_6_.rest_10_), channel_id=1, source_target_pairs={{0,1},{1,0},{2,3},{3,2},{4,5},{5,4},{6,7},{7,6},{8,9},{9,8},{10,11... | collective-permute-start | bytes 1769480 | tf_op jit(solution)/shard_map/ppermute | solution.py:822
  144.4 24.8 %collective-permute-start.13 = (bf16[80,768]{1,0:T(8,128)(2,1)S(1)}, bf16[80,768]{1,0:T(8,128)(2,1)S(1)}, u32[]{:S(2)}, u32[]{:S(2)}) collective-permute-start(bf16[80,768]{1,0:T(8,128)(2,1)S(1)} %maximum_select_fusion.1.head_ref), channel_id=1, source_target_pairs={{0,12},{1,13},{2,14},{3,15},{4,8},{5,9},{6,10},{7,11},{8,4},{9,5},... | collective-permute-start | bytes 368648 | tf_op jit(solution)/shard_map/ppermute | solution.py:822
  148.3 20.9 %collective-permute-start.12 = (bf16[80,768]{1,0:T(8,128)(2,1)S(1)}, bf16[80,768]{1,0:T(8,128)(2,1)S(1)}, u32[]{:S(2)}, u32[]{:S(2)}) collective-permute-start(bf16[80,768]{1,0:T(8,128)(2,1)S(1)} %maximum_select_fusion.1.head_ref), channel_id=1, source_target_pairs={{0,8},{1,9},{2,10},{3,11},{4,12},{5,13},{6,14},{7,15},{8,0},{9,1},... | collective-permute-start | bytes 368648 | tf_op jit(solution)/shard_map/ppermute | solution.py:822
  148.3 20.9 %collective-permute-start.11 = (bf16[80,768]{1,0:T(8,128)(2,1)S(1)}, bf16[80,768]{1,0:T(8,128)(2,1)S(1)}, u32[]{:S(2)}, u32[]{:S(2)}) collective-permute-start(bf16[80,768]{1,0:T(8,128)(2,1)S(1)} %maximum_select_fusion.1.head_ref), channel_id=1, source_target_pairs={{0,4},{1,5},{2,6},{3,7},{4,0},{5,1},{6,2},{7,3},{8,12},{9,13},{10,... | collective-permute-start | bytes 368648 | tf_op jit(solution)/shard_map/ppermute | solution.py:822
  169.9 72.5 %all-to-all-start.5 = ((bf16[16,80,960]{2,1,0:T(8,128)(2,1)}), bf16[16,80,960]{2,1,0:T(8,128)(2,1)S(1)}, u32[]{:S(2)}, u32[]{:S(2)}) async-start(bf16[16,80,960]{2,1,0:T(8,128)(2,1)} %bitcast.70), calls=%async_computation.5 | async-start | bytes 5242880 | tf_op jit(solution)/shard_map/all_to_all | solution.py:874
  187.6 175.3 %reduce-scatter.2.cloned.1.call-start = ((), (), s32[]{:S(2)}) async-start(), calls=%async_computation.9 | async-start | bytes 3760128 | tf_op jit(solution)/shard_map/reduce_scatter | solution.py:969
  191.0 51.4 %collective-permute-start.15 = (bf16[4,80,768]{2,1,0:T(8,128)(2,1)S(1)}, bf16[4,80,768]{2,1,0:T(8,128)(2,1)}, u32[]{:S(2)}, u32[]{:S(2)}) collective-permute-start(bf16[4,80,768]{2,1,0:T(8,128)(2,1)S(1)} %pad_maximum_fusion), channel_id=1, source_target_pairs={{0,2},{1,3},{2,0},{3,1},{4,6},{5,7},{6,4},{7,5},{8,10},{9,11},{10,... | collective-permute-start | bytes 1474568 | tf_op jit(solution)/shard_map/ppermute | solution.py:822
  242.4 24.5 %collective-permute-start.16 = (bf16[8,144,768]{2,1,0:T(8,128)(2,1)}, bf16[8,144,768]{2,1,0:T(8,128)(2,1)}, u32[]{:S(2)}, u32[]{:S(2)}) collective-permute-start(bf16[8,144,768]{2,1,0:T(8,128)(2,1)} %get-tuple-element.227), channel_id=1, source_target_pairs={{0,1},{1,0},{2,3},{3,2},{4,5},{5,4},{6,7},{7,6},{8,9},{9,8},{10,11... | collective-permute-start | bytes 5308424 | tf_op jit(solution)/shard_map/ppermute | solution.py:822
  243.2 23.7 %collective-permute-start.17 = (bf16[8,48,768]{2,1,0:T(8,128)(2,1)}, bf16[8,48,768]{2,1,0:T(8,128)(2,1)}, u32[]{:S(2)}, u32[]{:S(2)}) collective-permute-start(bf16[8,48,768]{2,1,0:T(8,128)(2,1)} %get-tuple-element.228), channel_id=1, source_target_pairs={{0,1},{1,0},{2,3},{3,2},{4,5},{5,4},{6,7},{7,6},{8,9},{9,8},{10,11... | collective-permute-start | bytes 1769480 | tf_op jit(solution)/shard_map/ppermute | solution.py:822
  246.3 20.6 %collective-permute-start.18 = (bf16[8,80,768]{2,1,0:T(8,128)(2,1)}, bf16[8,80,768]{2,1,0:T(8,128)(2,1)}, u32[]{:S(2)}, u32[]{:S(2)}) collective-permute-start(bf16[8,80,768]{2,1,0:T(8,128)(2,1)} %constant_dynamic-update-slice_fusion.3.heads_own), channel_id=1, source_target_pairs={{0,1},{1,0},{2,3},{3,2},{4,5},{5,4},{6,7},{7,6},{8,9},{9,8},{10,11... | collective-permute-start | bytes 2949128 | tf_op jit(solution)/shard_map/ppermute | solution.py:822
  285.8 69.9 %all-to-all-start.6 = ((bf16[16,48,768]{2,1,0:T(8,128)(2,1)}), bf16[16,48,768]{2,1,0:T(8,128)(2,1)}, u32[]{:S(2)}, u32[]{:S(2)}) async-start(bf16[16,48,768]{2,1,0:T(8,128)(2,1)} %bitcast.75), calls=%async_computation.6 | async-start | bytes 2359296 | tf_op jit(solution)/shard_map/all_to_all | solution.py:874
  294.9 149.6 %all-gather.6.cloned.1.call-start = ((), (), s32[]{:S(2)}) async-start(), calls=%async_computation.10 | async-start | bytes 3760128 | tf_op jit(solution)/shard_map/all_gather | solution.py:1034
  295.7 42.7 %collective-permute-start.19 = (bf16[4,144,768]{2,1,0:T(8,128)(2,1)}, bf16[4,144,768]{2,1,0:T(8,128)(2,1)}, u32[]{:S(2)}, u32[]{:S(2)}) collective-permute-start(bf16[4,144,768]{2,1,0:T(8,128)(2,1)} %get-tuple-element.234), channel_id=1, source_target_pairs={{0,2},{1,3},{2,0},{3,1},{4,6},{5,7},{6,4},{7,5},{8,10},{9,11},{10,... | collective-permute-start | bytes 2654216 | tf_op jit(solution)/shard_map/ppermute | solution.py:822
  299.5 38.8 %collective-permute-start.21 = (bf16[4,48,768]{2,1,0:T(8,128)(2,1)}, bf16[4,48,768]{2,1,0:T(8,128)(2,1)}, u32[]{:S(2)}, u32[]{:S(2)}) collective-permute-start(bf16[4,48,768]{2,1,0:T(8,128)(2,1)} %get-tuple-element.245), channel_id=1, source_target_pairs={{0,2},{1,3},{2,0},{3,1},{4,6},{5,7},{6,4},{7,5},{8,10},{9,11},{10,... | collective-permute-start | bytes 884744 | tf_op jit(solution)/shard_map/ppermute | solution.py:822
  341.9 21.0 %collective-permute-start.22 = (bf16[144,768]{1,0:T(8,128)(2,1)}, bf16[144,768]{1,0:T(8,128)(2,1)}, u32[]{:S(2)}, u32[]{:S(2)}) collective-permute-start(bf16[144,768]{1,0:T(8,128)(2,1)} %get-tuple-element.256), channel_id=1, source_target_pairs={{0,4},{1,5},{2,6},{3,7},{4,0},{5,1},{6,2},{7,3},{8,12},{9,13},{10,... | collective-permute-start | bytes 663560 | tf_op jit(solution)/shard_map/ppermute | solution.py:822
  343.6 19.3 %collective-permute-start.23 = (bf16[144,768]{1,0:T(8,128)(2,1)}, bf16[144,768]{1,0:T(8,128)(2,1)}, u32[]{:S(2)}, u32[]{:S(2)}) collective-permute-start(bf16[144,768]{1,0:T(8,128)(2,1)} %get-tuple-element.257), channel_id=1, source_target_pairs={{0,8},{1,9},{2,10},{3,11},{4,12},{5,13},{6,14},{7,15},{8,0},{9,1},... | collective-permute-start | bytes 663560 | tf_op jit(solution)/shard_map/ppermute | solution.py:822
  373.3 57.4 %collective-permute-start.26 = (bf16[960,768]{1,0:T(8,128)(2,1)S(1)}, bf16[960,768]{1,0:T(8,128)(2,1)}, u32[]{:S(2)}, u32[]{:S(2)}) collective-permute-start(bf16[960,768]{1,0:T(8,128)(2,1)S(1)} %copy-done.4), channel_id=1, source_target_pairs={{0,16},{16,0},{1,17},{17,1},{2,18},{18,2},{3,19},{19,3},{4,20},{20... | collective-permute-start | bytes 4423688 | tf_op jit(solution)/shard_map/ppermute | solution.py:866
  (65 other events, 794.8 us)
Sparse Core Ops, SparseCore 0:
  9.6 145.8 all-gather.3
  243.3 82.0 reduce-scatter.1
  373.4 59.5 all-gather.5
